TPU v7x, 128 devices: a whole 4x4x4 slice. The times are simulated.
128 devices in a mesh: leaf: 4 (over y), sep: 32 (over x, z, core).
Axes of the slice: x: 4, y: 4, z: 4, core: 2. Of those that a mesh axis runs over, the one named last changes fastest.
Arguments:
- leaf_rhs: float32 [128, 16, 1024], P(('leaf', 'sep')), may hold values from -6 to 6
- leaf_inv: float32 [128, 1024, 1024], P(('leaf', 'sep'))
- update_blocks: float32 [128, 1024, 1024], P(('leaf', 'sep')), may hold values from -0.1875 to 0.1875
- row_map: int32 [128, 1024], P(('leaf', 'sep')), may hold values from 0 to 24575, as said below
- live_rows: int32 [128], P(('leaf', 'sep')), may hold values from 1 to 1024, 81920 in all
- sep_rhs: float32 [16, 6, 4, 32, 32], P(None, None, None, 'sep'), may hold values from -6 to 6
- inv_diag: float32 [6, 4, 32, 32, 4096], P(None, None, 'sep', None, 'leaf')
- panels: float32 [15, 4, 32, 32, 4096], P(None, None, 'sep', None, 'leaf'), may hold values from -0.046875 to 0.046875
Outputs:
- leaf_solution: float32 [128, 16, 1024], P(('leaf', 'sep'))
- sep_solution: float32 [16, 6, 4, 32, 32], P(None, None, None, 'sep')
Inputs may be any that keep to these rules, and one draw needn't show every extreme that they name: `row_map`: the 1024 entries of one leaf are distinct global separator rows; writing a row g as k * 4096 + o * 32 + i with 0 <= i < 32, at most 16 entries of one leaf share the same o, and some leaf has exactly 16 with one o.
All inputs are finite; a program needn't handle non-finite values. No bound on the sum of `live_rows` on one device may be relied on, other than what follows from the above.
Results may differ from a plain program's by a relative error of at most 0.0001.
Values sent between devices are 32-bit elements; how exact they have to be, the bound alone decides.
No kernel may reach another device: no remote copies, remote signals or barrier semaphores. Data moves between devices by JAX's collectives and lax.ppermute only.
A program may use at most 128 MiB of HBM per device.

v0:
```python
import jax
import jax.numpy as jnp
from jax import lax
from jax.sharding import PartitionSpec as P


def pair_start(lower_level, levels):
    return lower_level * (levels - 1) - lower_level * (lower_level - 1) // 2


def pair_index(upper_level, lower_level, levels):
    return pair_start(lower_level, levels) + upper_level - lower_level - 1


def per_device(leaf_rhs, leaf_inv, update_blocks, row_map, live_rows, sep_rhs, inv_diag, panels):
    precise = lax.Precision.HIGHEST
    levels = inv_diag.shape[0]
    leaf_count = lax.axis_size("leaf")
    sep_count = lax.axis_size("sep")
    vectors = sep_rhs.shape[0]
    segment = sep_rhs.shape[4]
    quarter = inv_diag.shape[4]
    separator = quarter * leaf_count
    leaf_place = lax.axis_index("leaf")
    local_inv = leaf_inv[0]
    local_update = update_blocks[0]
    update_rows = local_update.shape[1]
    leaf_y = lax.dot_general(leaf_rhs[0], local_inv, (((1,), (1,)), ((), ())), precision=precise)
    live_mask = (jnp.arange(update_rows, dtype=jnp.int32) < live_rows[0]).astype(jnp.float32)
    contrib = jnp.dot(leaf_y, local_update, precision=precise) * live_mask[None, :]
    global_rows = row_map[0]
    scattered = (
        jnp.zeros((vectors, levels * separator), jnp.float32).at[:, global_rows].add(contrib)
    )
    shaped = scattered.reshape(vectors, levels, leaf_count, sep_count, segment)
    partial_sum = lax.psum_scatter(shaped, "sep", scatter_dimension=3, tiled=True)
    update_sum = lax.psum(partial_sum, "leaf")
    base_rows = (sep_rhs - update_sum)[:, :, :, 0, :]
    pending = jnp.zeros_like(base_rows)
    y_terms = []
    for level_now in range(levels):
        correction = lax.psum(pending[:, level_now], "leaf")
        current = base_rows[:, level_now] - correction
        whole_vec = lax.all_gather(current[:, :, None, :], "sep", axis=2, tiled=True)
        own_cols = lax.dynamic_index_in_dim(whole_vec, leaf_place, 1, keepdims=False).reshape(
            vectors, quarter
        )
        y_terms.append(
            jnp.einsum("rc,qic->rqi", own_cols, inv_diag[level_now, :, 0], precision=precise)
        )
        if level_now + 1 < levels:
            first_pair = pair_start(level_now, levels)
            block_set = panels[first_pair : first_pair + levels - 1 - level_now, :, 0]
            later_terms = jnp.einsum("rc,mqic->rmqi", own_cols, block_set, precision=precise)
            pending = pending.at[:, level_now + 1 :].add(later_terms)
    y_rows = lax.psum(jnp.stack(y_terms, axis=1), "leaf")
    back_pending = jnp.zeros((vectors, levels, quarter), jnp.float32)
    solutions = [None] * levels
    for level_now in range(levels - 1, -1, -1):
        column_term = jnp.einsum(
            "rqi,qic->rc", y_rows[:, level_now], inv_diag[level_now, :, 0], precision=precise
        )
        column_term = column_term + back_pending[:, level_now]
        own_part = lax.psum_scatter(
            column_term.reshape(vectors, sep_count, segment), "sep", scatter_dimension=1, tiled=True
        )
        solved = lax.all_gather(own_part, "leaf", axis=1, tiled=True)
        solutions[level_now] = solved
        for lower_level in range(level_now):
            coupling = panels[pair_index(level_now, lower_level, levels), :, 0]
            lower_term = jnp.einsum("rqi,qic->rc", solved, coupling, precision=precise)
            back_pending = back_pending.at[:, lower_level].add(-lower_term)
    sep_solution = jnp.stack(solutions, axis=1)[:, :, :, None, :]
    spread = lax.all_gather(sep_solution, "sep", axis=3, tiled=True).reshape(
        vectors, levels * separator
    )
    mapped = jnp.take(spread, global_rows, axis=1) * live_mask[None, :]
    reduced = leaf_y - lax.dot_general(
        mapped, local_update, (((1,), (1,)), ((), ())), precision=precise
    )
    leaf_x = jnp.dot(reduced, local_inv, precision=precise)
    return (leaf_x[None], sep_solution)


def solution(mesh):
    in_specs = (
        P(("leaf", "sep"), None, None),
        P(("leaf", "sep"), None, None),
        P(("leaf", "sep"), None, None),
        P(("leaf", "sep"), None),
        P(("leaf", "sep")),
        P(None, None, None, "sep", None),
        P(None, None, "sep", None, "leaf"),
        P(None, None, "sep", None, "leaf"),
    )
    out_specs = (P(("leaf", "sep"), None, None), P(None, None, None, "sep", None))
    return jax.shard_map(
        per_device, mesh=mesh, in_specs=in_specs, out_specs=out_specs, check_vma=False
    )
```

profile of v0, /device:TPU:1, one launch (start us, length us, event | category | flops | bytes accessed | tf_op | source)
XLA Modules:
  0.0 1123.2 jit_solution(12611309071497061544)
XLA Ops:
  18.2 11.4 %scatter_custom_fusion = f32[16,24576]{0,1:T(8,128)} fusion(s32[1024]{0:T(1024)S(1)} %bitcast.584, f32[1024,16]{1,0:T(8,128)S(1)} %copy.82, f32[]{:T(128)} %constant.503.clone.1), kind=kCustom, calls=%fused_computation.2 | custom fusion | flops 16384 | bytes 1572868 | tf_op jit(solution)/shard_map/scatter-add | solution.py:33
  29.5 9.8 copy.84
  45.0 82.5 %reduce-scatter.8.cloned.1.call-done = f32[16,6,4,1,32]{4,0,2,1,3:T(8,128)} async-done(((f32[16,6,4,32,32]{4,0,2,1,3:T(8,128)}), f32[16,6,4,1,32]{4,0,2,1,3:T(8,128)}) %reduce-scatter.8.cloned.1.call-update) | async-done | bytes 49168 | tf_op jit(solution)/shard_map/reduce_scatter | solution.py:36
  127.5 16.7 %psum.52 = f32[16,6,4,1,32]{4,0,2,1,3:T(8,128)} all-reduce(f32[16,6,4,1,32]{4,0,2,1,3:T(8,128)} %reduce-scatter.8.cloned.1.call-done), channel_id=1, replica_groups=mesh['leaf'=4,'sep'=32] {'leaf'}, use_global_device_ids=true, to_apply=%region_2.0 | all-reduce | flops 12288 | bytes 98304 | tf_op jit(solution)/shard_map/psum | solution.py:37
  145.4 30.9 %all-gather = f32[16,1,4,1024]{0,2,1,3:T(4,128)S(1)} all-gather(f32[16,1,4,32]{0,2,1,3:T(4,128)S(1)} %copy.86), channel_id=2, replica_groups=mesh['leaf'=4,'sep'=32] {'sep'}, dimensions={3}, use_global_device_ids=true | all-gather | bytes 270336 | tf_op jit(solution)/shard_map/all_gather | solution.py:44
  177.6 10.1 fusion.10
  188.4 11.3 %psum.53 = f32[16,4,32]{2,0,1:T(8,128)S(1)} all-reduce(f32[16,4,32]{2,0,1:T(8,128)S(1)} %slice_bitcast_fusion.78), channel_id=1, replica_groups=mesh['leaf'=4,'sep'=32] {'leaf'}, use_global_device_ids=true, to_apply=%region_3.0 | all-reduce | flops 2048 | bytes 16384 | tf_op jit(solution)/shard_map/psum | solution.py:42
  203.2 27.1 %all-gather.1 = f32[16,4,1024]{0,1,2:T(4,128)S(1)} all-gather(f32[16,4,32]{0,1,2:T(4,128)S(1)} %copy.90), channel_id=3, replica_groups=mesh['leaf'=4,'sep'=32] {'sep'}, dimensions={2}, use_global_device_ids=true | all-gather | bytes 270336 | tf_op jit(solution)/shard_map/all_gather | solution.py:44
  231.7 8.3 fusion.18
  240.0 12.5 %psum.54 = f32[16,4,32]{2,0,1:T(8,128)S(1)} all-reduce(f32[16,4,32]{2,0,1:T(8,128)S(1)} %slice_bitcast_fusion.76), channel_id=1, replica_groups=mesh['leaf'=4,'sep'=32] {'leaf'}, use_global_device_ids=true, to_apply=%region_4.5 | all-reduce | flops 2048 | bytes 16384 | tf_op jit(solution)/shard_map/psum | solution.py:42
  254.0 29.4 %all-gather.2 = f32[16,4,1024]{0,1,2:T(4,128)S(1)} all-gather(f32[16,4,32]{0,1,2:T(4,128)S(1)} %copy.94), channel_id=4, replica_groups=mesh['leaf'=4,'sep'=32] {'sep'}, dimensions={2}, use_global_device_ids=true | all-gather | bytes 270336 | tf_op jit(solution)/shard_map/all_gather | solution.py:44
  291.9 11.3 %psum.55 = f32[16,4,32]{2,0,1:T(8,128)S(1)} all-reduce(f32[16,4,32]{2,0,1:T(8,128)S(1)} %slice_bitcast_fusion.74), channel_id=1, replica_groups=mesh['leaf'=4,'sep'=32] {'leaf'}, use_global_device_ids=true, to_apply=%region_5.6 | all-reduce | flops 2048 | bytes 16384 | tf_op jit(solution)/shard_map/psum | solution.py:42
  303.3 26.9 %all-gather.3 = f32[16,4,1024]{0,1,2:T(4,128)S(1)} all-gather(f32[16,4,32]{0,1,2:T(4,128)S(1)} %copy.98), channel_id=5, replica_groups=mesh['leaf'=4,'sep'=32] {'sep'}, dimensions={2}, use_global_device_ids=true | all-gather | bytes 270336 | tf_op jit(solution)/shard_map/all_gather | solution.py:44
  336.2 12.5 %psum.56 = f32[16,4,32]{2,0,1:T(8,128)S(1)} all-reduce(f32[16,4,32]{2,0,1:T(8,128)S(1)} %slice_bitcast_fusion.72), channel_id=1, replica_groups=mesh['leaf'=4,'sep'=32] {'leaf'}, use_global_device_ids=true, to_apply=%region_6.7 | all-reduce | flops 2048 | bytes 16384 | tf_op jit(solution)/shard_map/psum | solution.py:42
  348.8 29.3 %all-gather.4 = f32[16,4,1024]{0,1,2:T(4,128)S(1)} all-gather(f32[16,4,32]{0,1,2:T(4,128)S(1)} %copy.102), channel_id=6, replica_groups=mesh['leaf'=4,'sep'=32] {'sep'}, dimensions={2}, use_global_device_ids=true | all-gather | bytes 270336 | tf_op jit(solution)/shard_map/all_gather | solution.py:44
  392.2 11.3 %psum.57 = f32[16,4,32]{2,0,1:T(8,128)S(1)} all-reduce(f32[16,4,32]{2,0,1:T(8,128)S(1)} %fusion.91), channel_id=1, replica_groups=mesh['leaf'=4,'sep'=32] {'leaf'}, use_global_device_ids=true, to_apply=%region_7.8 | all-reduce | flops 2048 | bytes 16384 | tf_op jit(solution)/shard_map/psum | solution.py:42
  403.6 27.1 %all-gather.5 = f32[16,4,1024]{0,1,2:T(4,128)S(1)} all-gather(f32[16,4,32]{0,1,2:T(4,128)S(1)} %copy.106), channel_id=7, replica_groups=mesh['leaf'=4,'sep'=32] {'sep'}, dimensions={2}, use_global_device_ids=true | all-gather | bytes 270336 | tf_op jit(solution)/shard_map/all_gather | solution.py:44
  433.6 14.9 %psum.58 = f32[16,6,4,32]{3,0,2,1:T(8,128)S(1)} all-reduce(f32[16,6,4,32]{3,0,2,1:T(8,128)} %fusion.89), channel_id=1, replica_groups=mesh['leaf'=4,'sep'=32] {'leaf'}, use_global_device_ids=true, to_apply=%region_8.9 | all-reduce | flops 12288 | bytes 98304 | tf_op jit(solution)/shard_map/psum | solution.py:56
  453.4 76.4 %reduce-scatter.10.cloned.1.call-done = f32[16,1,32]{2,0,1:T(8,128)} async-done(((f32[16,32,32]{2,0,1:T(8,128)}), f32[16,1,32]{2,0,1:T(8,128)}) %reduce-scatter.10.cloned.1.call-update) | async-done | bytes 2064 | tf_op jit(solution)/shard_map/reduce_scatter | solution.py:64
  529.8 9.6 all_gather.45
  551.4 78.0 %reduce-scatter.12.cloned.1.call-done = f32[16,1,32]{2,0,1:T(8,128)} async-done(((f32[16,32,32]{2,0,1:T(8,128)}), f32[16,1,32]{2,0,1:T(8,128)}) %reduce-scatter.12.cloned.1.call-update) | async-done | bytes 2064 | tf_op jit(solution)/shard_map/reduce_scatter | solution.py:64
  629.3 9.5 all_gather.46
  651.1 78.1 %reduce-scatter.14.cloned.1.call-done = f32[16,1,32]{2,0,1:T(8,128)} async-done(((f32[16,32,32]{2,0,1:T(8,128)}), f32[16,1,32]{2,0,1:T(8,128)}) %reduce-scatter.14.cloned.1.call-update) | async-done | bytes 2064 | tf_op jit(solution)/shard_map/reduce_scatter | solution.py:64
  729.2 9.7 all_gather.47
  747.9 77.1 %reduce-scatter.16.cloned.1.call-done = f32[16,1,32]{2,0,1:T(8,128)} async-done(((f32[16,32,32]{2,0,1:T(8,128)}), f32[16,1,32]{2,0,1:T(8,128)}) %reduce-scatter.16.cloned.1.call-update) | async-done | bytes 2064 | tf_op jit(solution)/shard_map/reduce_scatter | solution.py:64
  825.1 9.6 all_gather.48
  841.4 77.1 %reduce-scatter.18.cloned.1.call-done = f32[16,1,32]{2,0,1:T(8,128)} async-done(((f32[16,32,32]{2,0,1:T(8,128)}), f32[16,1,32]{2,0,1:T(8,128)}) %reduce-scatter.18.cloned.1.call-update) | async-done | bytes 2064 | tf_op jit(solution)/shard_map/reduce_scatter | solution.py:64
  918.5 9.6 all_gather.49
  931.9 78.6 %reduce-scatter.20.cloned.1.call-done = f32[16,1,32]{2,0,1:T(8,128)} async-done(((f32[16,32,32]{2,0,1:T(8,128)}), f32[16,1,32]{2,0,1:T(8,128)}) %reduce-scatter.20.cloned.1.call-update) | async-done | bytes 2064 | tf_op jit(solution)/shard_map/reduce_scatter | solution.py:64
  1010.4 9.6 all_gather.50
  1022.0 66.1 %all-gather.9.cloned.1.call-done = f32[16,6,4,1024]{0,2,1,3:T(4,128)} async-done(((f32[16,6,4,32]{0,2,1,3:T(4,128)}), f32[16,6,4,1024]{0,2,1,3:T(4,128)}) %all-gather.9.cloned.1.call-update) | async-done | bytes 1572880 | tf_op jit(solution)/shard_map/all_gather | solution.py:74
  1088.1 11.5 %copy.140 = f32[16,6,4,1024]{0,3,2,1:T(8,128)} copy(f32[16,6,4,1024]{0,2,1,3:T(4,128)} %all-gather.9.cloned.1.call-done) | data formatting | bytes 3145728 | tf_op jit(solution)/shard_map/reshape | solution.py:74
  (140 shorter events, 124.0 us)
Async XLA Ops:
  7.2 2.4 copy-start
  7.2 120.3 %reduce-scatter.8.cloned.1.call-start = ((), (), s32[]{:S(2)}) async-start(), calls=%async_computation.7 | async-start | bytes 6488064 | tf_op jit(solution)/shard_map/reduce_scatter | solution.py:36
  7.2 8.7 copy-start.2
  15.2 0.6 copy-start.15
  39.3 1.9 copy-start.4
  39.4 490.5 %reduce-scatter.10.cloned.1.call-start = ((), (), s32[]{:S(2)}) async-start(), calls=%async_computation.8 | async-start | bytes 270336 | tf_op jit(solution)/shard_map/reduce_scatter | solution.py:64
  176.8 0.8 copy-start.5
  187.7 0.7 copy-start.13
  199.8 31.9 %copy-start.14 = (f32[16,5,4,32]{3,0,2,1:T(8,128)S(1)}, f32[16,5,4,32]{3,0,2,1:T(8,128)}, u32[]{:S(2)}) copy-start(f32[16,5,4,32]{3,0,2,1:T(8,128)} %copy-done.13) | copy-start | bytes 122884
  230.9 0.8 copy-start.6
  283.9 0.8 copy-start.7
  291.2 0.6 copy-start.18
  330.7 0.8 copy-start.9
  348.8 33.3 %copy-start.8 = (f32[16,1,32,32]{0,1,3,2:T(1,128)S(1)}, f32[16,1,32,32]{0,1,3,2:T(1,128)}, u32[]{:S(2)}) copy-start(f32[16,1,32,32]{0,1,3,2:T(1,128)} %copy-done.7) | copy-start | bytes 196612
  348.8 35.7 %copy-start.10 = (f32[16,1,32,32]{0,1,3,2:T(1,128)S(1)}, f32[16,1,32,32]{0,1,3,2:T(1,128)}, u32[]{:S(2)}) copy-start(f32[16,1,32,32]{0,1,3,2:T(1,128)} %copy-done.9) | copy-start | bytes 196612
  448.5 99.2 %copy-start.12 = (f32[16,6,4,32]{3,0,2,1:T(8,128)}, f32[16,6,4,32]{3,0,2,1:T(8,128)S(1)}, u32[]{:S(2)}) copy-start(f32[16,6,4,32]{3,0,2,1:T(8,128)S(1)} %psum.58) | copy-start | bytes 147460
  453.4 175.9 %reduce-scatter.12.cloned.1.call-start = ((), (), s32[]{:S(2)}) async-start(), calls=%async_computation.9 | async-start | bytes 270336 | tf_op jit(solution)/shard_map/reduce_scatter | solution.py:64
  545.5 0.7 copy-start.11
  550.7 178.5 %reduce-scatter.14.cloned.1.call-start = ((), (), s32[]{:S(2)}) async-start(), calls=%async_computation.10 | async-start | bytes 270336 | tf_op jit(solution)/shard_map/reduce_scatter | solution.py:64
  650.5 174.6 %reduce-scatter.16.cloned.1.call-start = ((), (), s32[]{:S(2)}) async-start(), calls=%async_computation.11 | async-start | bytes 270336 | tf_op jit(solution)/shard_map/reduce_scatter | solution.py:64
  740.5 2.2 copy-start.17
  746.4 172.1 %reduce-scatter.18.cloned.1.call-start = ((), (), s32[]{:S(2)}) async-start(), calls=%async_computation.12 | async-start | bytes 270336 | tf_op jit(solution)/shard_map/reduce_scatter | solution.py:64
  839.8 170.6 %reduce-scatter.20.cloned.1.call-start = ((), (), s32[]{:S(2)}) async-start(), calls=%async_computation.13 | async-start | bytes 270336 | tf_op jit(solution)/shard_map/reduce_scatter | solution.py:64
  931.8 156.3 %all-gather.9.cloned.1.call-start = ((), (), s32[]{:S(2)}) async-start(), calls=%async_computation.14 | async-start | bytes 12976128 | tf_op jit(solution)/shard_map/all_gather | solution.py:74
  1022.0 85.0 %copy-start.16 = (f32[16,1024]{1,0:T(8,128)S(1)}, f32[16,1024]{1,0:T(8,128)}, u32[]{:S(2)}) copy-start(f32[16,1024]{1,0:T(8,128)} %copy-done.15) | copy-start | bytes 196612
  1107.0 6.2 copy-start.3
  1107.0 9.0 copy-start.1
Sparse Core Ops, SparseCore 0:
  39.5 87.9 reduce-scatter.7
  453.5 76.2 reduce-scatter.9
  550.8 78.4 reduce-scatter.11
  650.6 78.5 reduce-scatter.13
  746.5 78.5 reduce-scatter.15
  840.0 78.4 reduce-scatter.17
  931.9 78.4 reduce-scatter.19
  1021.2 66.8 all-gather.8
where the time goes:
time: 1130 us; the launch traced here: 1120 us
  waiting for transfers between devices  614 us (54%)
  blocking collectives  319 us (28%)
  matrix products  103 us (9%)
  local copies, waits for them, and re-layouts  57 us (5%)
  between operations  15.8 us (1%)
  other arithmetic  14.6 us (1%)
    reduce_scatter x6, waiting for transfers between devices, per_device(): lax.psum_scatter(column_term.reshape(vectors, sep_count, segment), 'sep',...  465 us
    all_gather x6, blocking collectives, per_device(): lax.all_gather(current[:, :, None, :], 'sep', axis=2, tiled=True)  171 us
    reduce_scatter x1, waiting for transfers between devices, per_device(): lax.psum_scatter(shaped, 'sep', scatter_dimension=3, tiled=True)  82.5 us
    all_gather x1, waiting for transfers between devices, per_device(): lax.all_gather(sep_solution, 'sep', axis=3, tiled=True)  66.1 us
    psum x5, blocking collectives, per_device(): correction = lax.psum(pending[:, level_now], 'leaf')  58.7 us
    all_gather x6, blocking collectives, per_device(): solved = lax.all_gather(own_part, 'leaf', axis=1, tiled=True)  57.5 us
    dot_general x5, matrix products, per_device(): jnp.einsum('rc,mqic->rmqi', own_cols, block_set, precision=precise)  32.4 us
    dot_general x15, matrix products, per_device(): lower_term = jnp.einsum('rqi,qic->rc', solved, coupling, precision=precise)  24.6 us
  transfers between devices with their start and end apart: 8, of which 8 were waited for; matrix products, arithmetic and copies ran while one was open for 1% of the time, Pallas kernels for 0%

commit v1 on v0

v1 whole, which is shorter than its diff:
```python
import functools

import jax
import jax.numpy as jnp
from jax import lax
from jax.experimental import pallas as pl
from jax.experimental.pallas import tpu as pltpu
from jax.sharding import PartitionSpec as P

F32 = jnp.float32
BF16 = jnp.bfloat16
V = 16
LEVELS = 6
ROWS = 128
COLS = 1024
UPD = 1024
ALL = ("leaf", "sep")
VMEM_LIMIT = 40 * 1024 * 1024
NT = (((1,), (1,)), ((), ()))
NN = (((1,), (0,)), ((), ()))


def pair_index(upper, lower):
    return lower * (LEVELS - 1) - lower * (lower - 1) // 2 + upper - lower - 1


def iota(shape, dim):
    return lax.broadcasted_iota(jnp.int32, shape, dim)


def dot(a, b, dims):
    return lax.dot_general(a, b, dims, preferred_element_type=F32)


def split(x):
    high = x.astype(BF16)
    return high, (x - high.astype(F32)).astype(BF16)


def product(x, w, dims):
    xh, xl = split(x)
    wh, wl = split(w)
    m = x.shape[0]
    both = dot(jnp.concatenate([xh, xl], 0), wh, dims)
    return both[:m] + both[m:] + dot(xh, wl, dims)


def exact_rows(x, onehot, dims):
    xh, xl = split(x)
    m = x.shape[0]
    both = dot(jnp.concatenate([xh, xl], 0), onehot, dims)
    return both[:m] + both[m:]


def block_swap(t):
    gap = (iota((16, 128), 1) // 32 - iota((16, 128), 0) // 4) & 3
    out = t
    for d in range(1, 4):
        moved = pltpu.roll(pltpu.roll(t, 32 * d, 1), 16 - 4 * d, 0)
        out = jnp.where(gap == d, moved, out)
    return out


def call(body, out_shape, in_specs, out_specs, grid=(1,), scratch=(), aliases=None, flops=0, nbytes=0):
    return pl.pallas_call(
        body,
        out_shape=out_shape,
        grid=grid,
        in_specs=in_specs,
        out_specs=out_specs,
        scratch_shapes=scratch,
        input_output_aliases=aliases or {},
        compiler_params=pltpu.CompilerParams(vmem_limit_bytes=VMEM_LIMIT),
        cost_estimate=pl.CostEstimate(flops=flops, bytes_accessed=nbytes, transcendentals=0),
    )


def whole(shape):
    return pl.BlockSpec(shape, lambda *_: (0,) * len(shape))


def sds(shape, dtype=F32):
    return jax.ShapeDtypeStruct(shape, dtype)


SMEM = pl.BlockSpec(memory_space=pltpu.SMEM)


def leaf_forward(live_ref, rhs_ref, map_ref, inv_ref, upd_ref, y_ref, msg_ref, t_ref, rank_ref, acc):
    step = pl.program_id(0)

    @pl.when(step == 0)
    def _():
        acc[...] = jnp.zeros_like(acc)
        rows = map_ref[...]
        owner = (rows >> 5) & 127
        hot = (iota((128, UPD), 0) == owner).astype(F32)
        tri = (iota((UPD, UPD), 0) < iota((UPD, UPD), 1)).astype(F32).astype(BF16)
        before = dot(hot.astype(BF16), tri, NN)
        rank = jnp.sum(hot * before, axis=0, keepdims=True).astype(jnp.int32)
        rank_ref[...] = jnp.broadcast_to(rank, rank_ref.shape)
        for half in range(2):
            t_ref[pl.ds(128 * half, 128), :] = jnp.where((rank >> 3) == half, hot, 0.0).astype(BF16)

    y_part = product(rhs_ref[...], inv_ref[...], NT)
    y_ref[...] = y_part
    acc[...] += product(y_part, upd_ref[...], NN)

    @pl.when(step == pl.num_programs(0) - 1)
    def _():
        rows = map_ref[...]
        rank = rank_ref[0:1, :]
        live = iota((1, UPD), 1) < live_ref[0]
        group = iota((128, UPD), 0) >> 4
        spread = jnp.where((group == (rank & 7)) & live, jnp.concatenate([acc[...]] * 8, 0), 0.0)
        parts = jnp.concatenate(split(spread), 0)
        for half in range(2):
            got = dot(t_ref[pl.ds(128 * half, 128), :], parts, NT)
            msg_ref[pl.ds(half, 128, 4), :] = got[:, :128] + got[:, 128:]
        local = (rows >> 12) * 32 + (rows & 31) + 1
        places = jnp.where((iota((128, UPD), 0) == rank) & live, local.astype(F32), 0.0)
        hot = t_ref[pl.ds(0, 128), :].astype(F32) + t_ref[pl.ds(128, 128), :].astype(F32)
        msg_ref[pl.ds(2, 128, 4), :] = dot(hot.astype(BF16), places.astype(BF16), NT)
        msg_ref[pl.ds(3, 128, 4), :] = jnp.zeros((128, 128), F32)


def run_leaf_forward(live, rhs, rows, inv, upd):
    steps, part = 4, 256
    return call(
        leaf_forward,
        (sds((V, UPD)), sds((512, 128)), sds((256, UPD), BF16), sds((8, UPD), jnp.int32)),
        [
            SMEM,
            whole((V, 1024)),
            whole((1, UPD)),
            pl.BlockSpec((None, part, 1024), lambda i: (0, i, 0)),
            pl.BlockSpec((None, part, UPD), lambda i: (0, i, 0)),
        ],
        (pl.BlockSpec((V, part), lambda i: (0, i)), whole((512, 128)), whole((256, UPD)), whole((8, UPD))),
        grid=(steps,),
        scratch=[pltpu.VMEM((V, UPD), F32)],
        flops=2 * 16 * 3 * (2 << 20),
        nbytes=8 << 20,
    )(live, rhs, rows, inv, upd)


def leaf_backward(live_ref, got_ref, t_ref, rank_ref, y_ref, inv_ref, upd_ref, out_ref, mapped):
    step = pl.program_id(0)

    @pl.when(step == 0)
    def _():
        live = iota((1, UPD), 1) < live_ref[0]
        group = iota((128, UPD), 0) >> 4
        total = jnp.zeros((128, UPD), F32)
        for half in range(2):
            values = got_ref[pl.ds(half, 128, 2), :].T
            total += exact_rows(values, t_ref[pl.ds(128 * half, 128), :], NN)
        total = jnp.where((group == (rank_ref[0:1, :] & 7)) & live, total, 0.0)
        out = total[0:16]
        for g in range(1, 8):
            out += total[16 * g : 16 * g + 16]
        mapped[...] = out
        out_ref[...] = jnp.zeros_like(out_ref)

    z = y_ref[...] - product(mapped[...], upd_ref[...], NT)
    out_ref[...] += product(z, inv_ref[...], NN)


def run_leaf_backward(live, got, t, rank, y, inv, upd):
    steps, part = 4, 256
    return call(
        leaf_backward,
        sds((1, V, 1024)),
        [
            SMEM,
            whole((256, 128)),
            whole((256, UPD)),
            whole((8, UPD)),
            pl.BlockSpec((V, part), lambda i: (0, i)),
            pl.BlockSpec((None, part, 1024), lambda i: (0, i, 0)),
            pl.BlockSpec((None, part, UPD), lambda i: (0, i, 0)),
        ],
        pl.BlockSpec((None, V, 1024), lambda i: (0, 0, 0)),
        grid=(steps,),
        scratch=[pltpu.VMEM((V, UPD), F32)],
        flops=2 * 16 * 3 * (2 << 20),
        nbytes=8 << 20,
    )(live, got, t, rank, y, inv, upd)


def own_start(place_ref, got_ref, rhs_ref, pend_ref, msg_ref, index_ref):
    values = [got_ref[pl.ds(half, 128, 4), :].T for half in range(2)]
    index = got_ref[pl.ds(2, 128, 4), :]
    index_ref[...] = index
    column = (iota((128, 256), 1) + 1).astype(F32)
    total = jnp.zeros((V, 256), F32)
    for half in range(2):
        for g in range(8):
            j = 8 * half + g
            hot = jnp.where(index[:, j : j + 1] == column, 1.0, 0.0).astype(BF16)
            total += exact_rows(values[half][16 * g : 16 * g + 16], hot, NN)
    mine = iota((V, 128), 1) // 32 == place_ref[0]
    first = None
    for k in range(LEVELS):
        one = total[:, 32 * k : 32 * k + 32]
        row = jnp.where(mine, rhs_ref[:, 128 * k : 128 * k + 128] - jnp.concatenate([one] * 4, 1), 0.0)
        pend_ref[k] = row
        if k == 0:
            first = row
    turned = block_swap(first)
    chunk = turned[0:4] + turned[4:8] + turned[8:12] + turned[12:16]
    msg_ref[...] = jnp.concatenate([chunk] * 32, 0)


def run_own_start(place, got, rhs):
    return call(
        own_start,
        (sds((LEVELS, V, 128)), sds((128, 128)), sds((128, 128))),
        [SMEM, whole((512, 128)), whole((V, LEVELS * 128))],
        (whole((LEVELS, V, 128)), whole((128, 128)), whole((128, 128))),
        flops=1 << 27,
        nbytes=1 << 19,
    )(place, got, rhs)


def columns_of(got_ref, parts):
    total = got_ref[pl.ds(0, 128), :]
    for p in range(1, parts):
        total += got_ref[pl.ds(128 * p, 128), :]
    return jnp.concatenate([block_swap(total[16 * t : 16 * t + 16]) for t in range(8)], 1)


def row_message(msg_ref, rows):
    turned = block_swap(rows)
    for q in range(4):
        msg_ref[pl.ds(128 * q, 128), :] = jnp.concatenate([turned[4 * q : 4 * q + 4]] * 32, 0)


def forward_first(parts, got_ref, pend_ref, panel_ref, x_ref, msg_ref):
    x = columns_of(got_ref, parts)
    x_ref[...] = x
    row_message(msg_ref, pend_ref[...] - product(x, panel_ref[...].reshape(ROWS, COLS), NT))


def run_forward_first(k, parts, got, pend, panels):
    p = pair_index(k + 1, k)
    return call(
        functools.partial(forward_first, parts),
        (sds((V, COLS)), sds((512, 128))),
        [
            whole((128 * parts, 128)),
            pl.BlockSpec((None, V, 128), lambda i: (k + 1, 0, 0)),
            pl.BlockSpec((None, 4, None, 32, COLS), lambda i: (p, 0, 0, 0, 0)),
        ],
        (whole((V, COLS)), whole((512, 128))),
        flops=1 << 24,
        nbytes=1 << 20,
    )(got, pend, panels)


def forward_rest(x_ref, pend_ref, panel_ref, out_ref):
    out_ref[...] = pend_ref[...] - product(x_ref[...], panel_ref[...].reshape(ROWS, COLS), NT)


def run_forward_rest(k, x, pend, panels):
    first = pair_index(k + 2, k)
    count = LEVELS - 2 - k
    return call(
        forward_rest,
        sds((LEVELS, V, 128)),
        [
            whole((V, COLS)),
            pl.BlockSpec((None, V, 128), lambda i: (k + 2 + i, 0, 0)),
            pl.BlockSpec((None, 4, None, 32, COLS), lambda i: (first + i, 0, 0, 0, 0)),
        ],
        pl.BlockSpec((None, V, 128), lambda i: (k + 2 + i, 0, 0)),
        grid=(count,),
        aliases={1: 0},
        flops=count << 24,
        nbytes=count << 19,
    )(x, pend, panels)


def forward_diag(x_ref, diag_ref, y_ref):
    y_ref[...] = product(x_ref[...], diag_ref[...].reshape(ROWS, COLS), NT)


def diag_spec(k):
    return pl.BlockSpec((None, 4, None, 32, COLS), lambda i: (k, 0, 0, 0, 0))


def run_forward_diag(k, x, diag):
    return call(
        forward_diag,
        sds((V, 128)),
        [whole((V, COLS)), diag_spec(k)],
        whole((V, 128)),
        flops=1 << 24,
        nbytes=1 << 19,
    )(x, diag)


def forward_last(got_ref, y0, y1, y2, y3, y4, diag_ref, msg_ref):
    x = columns_of(got_ref, 4)
    last = product(x, diag_ref[...].reshape(ROWS, COLS), NT)
    for l in range(4):
        for k, one in enumerate((y0, y1, y2, y3, y4)):
            msg_ref[pl.ds(96 * l + 16 * k, 16), :] = one[...]
        msg_ref[pl.ds(96 * l + 80, 16), :] = last


def run_forward_last(got, ys, diag):
    return call(
        forward_last,
        sds((4 * 96, 128)),
        [whole((512, 128))] + [whole((V, 128))] * 5 + [diag_spec(5)],
        whole((4 * 96, 128)),
        flops=1 << 24,
        nbytes=1 << 20,
    )(got, *ys, diag)


def column_message(msg_ref, columns):
    for t in range(8):
        turned = block_swap(columns[:, 128 * t : 128 * t + 128])
        for l in range(4):
            msg_ref[pl.ds(128 * l + 16 * t, 16), :] = turned


def backward_start(got_ref, diag_ref, y_ref, msg_ref):
    y = got_ref[pl.ds(0, 96), :]
    for l in range(1, 4):
        y += got_ref[pl.ds(96 * l, 96), :]
    y_ref[...] = y
    column_message(msg_ref, product(y[80:96], diag_ref[...].reshape(ROWS, COLS), NN))


def run_backward_start(got, diag):
    return call(
        backward_start,
        (sds((96, 128)), sds((512, 128))),
        [whole((4 * 96, 128)), diag_spec(5)],
        (whole((96, 128)), whole((512, 128))),
        flops=1 << 24,
        nbytes=1 << 20,
    )(got, diag)


def backward_diag(y_ref, diag_ref, out_ref):
    out_ref[...] = product(y_ref[...], diag_ref[...].reshape(ROWS, COLS), NN)


def run_backward_diag(y, diag):
    return call(
        backward_diag,
        sds((LEVELS - 1, V, COLS)),
        [
            pl.BlockSpec((V, 128), lambda i: (i, 0)),
            pl.BlockSpec((None, 4, None, 32, COLS), lambda i: (i, 0, 0, 0, 0)),
        ],
        pl.BlockSpec((None, V, COLS), lambda i: (i, 0, 0)),
        grid=(LEVELS - 1,),
        flops=5 << 24,
        nbytes=5 << 19,
    )(y, diag)


def rows_of(got_ref):
    parts = []
    for q in range(4):
        total = got_ref[pl.ds(128 * q, 8), :]
        for t in range(1, 16):
            total += got_ref[pl.ds(128 * q + 8 * t, 8), :]
        parts.append(total[0:4] + total[4:8])
    return block_swap(jnp.concatenate(parts, 0))


def backward_first(got_ref, pend_ref, panel_ref, x_ref, msg_ref):
    x = rows_of(got_ref)
    x_ref[...] = x
    column_message(msg_ref, pend_ref[...] - product(x, panel_ref[...].reshape(ROWS, COLS), NN))


def run_backward_first(k, got, pend, panels):
    p = pair_index(k, k - 1)
    return call(
        backward_first,
        (sds((V, 128)), sds((512, 128))),
        [
            whole((512, 128)),
            pl.BlockSpec((None, V, COLS), lambda i: (k - 1, 0, 0)),
            pl.BlockSpec((None, 4, None, 32, COLS), lambda i: (p, 0, 0, 0, 0)),
        ],
        (whole((V, 128)), whole((512, 128))),
        flops=1 << 24,
        nbytes=1 << 20,
    )(got, pend, panels)


def backward_rest(x_ref, pend_ref, panel_ref, out_ref):
    out_ref[...] = pend_ref[...] - product(x_ref[...], panel_ref[...].reshape(ROWS, COLS), NN)


def run_backward_rest(k, x, pend, panels):
    count = k - 1
    return call(
        backward_rest,
        sds((LEVELS - 1, V, COLS)),
        [
            whole((V, 128)),
            pl.BlockSpec((None, V, COLS), lambda i: (i, 0, 0)),
            pl.BlockSpec((None, 4, None, 32, COLS), lambda i: (pair_index(k, i), 0, 0, 0, 0)),
        ],
        pl.BlockSpec((None, V, COLS), lambda i: (i, 0, 0)),
        grid=(count,),
        aliases={1: 0},
        flops=count << 24,
        nbytes=count << 19,
    )(x, pend, panels)


def own_finish(place_ref, got_ref, x1, x2, x3, x4, x5, index_ref, x_ref, msg_ref):
    x0 = rows_of(got_ref)
    levels = [x0] + [r[...] for r in (x1, x2, x3, x4, x5)]
    mine = []
    for k, x in enumerate(levels):
        x_ref[k] = x
        one = jnp.zeros((V, 32), F32)
        for q in range(4):
            one = jnp.where(place_ref[0] == q, x[:, 32 * q : 32 * q + 32], one)
        mine.append(one)
    rows = jnp.concatenate(mine + [jnp.zeros((V, 64), F32)], 1)
    high, low = split(jnp.concatenate([rows] * 8, 0))
    table = jnp.concatenate([high, low], 0)
    index = index_ref[...]
    column = (iota((128, 256), 1) + 1).astype(F32)
    group = iota((128, 128), 1) >> 4
    for half in range(2):
        out = jnp.zeros((128, 128), F32)
        for g in range(8):
            j = 8 * half + g
            hot = jnp.where(index[:, j : j + 1] == column, 1.0, 0.0).astype(BF16)
            got = dot(hot, table, NT)
            out = jnp.where(group == g, got[:, :128] + got[:, 128:], out)
        msg_ref[pl.ds(half, 128, 2), :] = out


def run_own_finish(place, got, xs, index):
    return call(
        own_finish,
        (sds((LEVELS, V, 128)), sds((256, 128))),
        [SMEM, whole((512, 128))] + [whole((V, 128))] * 5 + [whole((128, 128))],
        (whole((LEVELS, V, 128)), whole((256, 128))),
        flops=1 << 27,
        nbytes=1 << 20,
    )(place, got, *xs, index)


def exchange(message, axis=ALL):
    return lax.all_to_all(message, axis, 0, 0, tiled=True)


def per_device(leaf_rhs, leaf_inv, update_blocks, row_map, live_rows, sep_rhs, inv_diag, panels):
    place = lax.axis_index("leaf").astype(jnp.int32).reshape(1)
    rhs = sep_rhs.reshape(V, LEVELS * 128)
    leaf_y, message, table, rank = run_leaf_forward(live_rows, leaf_rhs[0], row_map, leaf_inv, update_blocks)
    pend, message, index = run_own_start(place, exchange(message), rhs)
    got, parts = exchange(message, "sep"), 1
    ys = []
    for k in range(LEVELS - 1):
        x, message = run_forward_first(k, parts, got, pend, panels)
        got, parts = exchange(message), 4
        if k + 2 < LEVELS:
            pend = run_forward_rest(k, x, pend, panels)
        ys.append(run_forward_diag(k, x, inv_diag))
    message = run_forward_last(got, ys, inv_diag)
    y, message = run_backward_start(exchange(message, "leaf"), inv_diag)
    got = exchange(message)
    pend = run_backward_diag(y, inv_diag)
    xs = []
    for k in range(LEVELS - 1, 0, -1):
        x, message = run_backward_first(k, got, pend, panels)
        xs.insert(0, x)
        got = exchange(message)
        if k > 1:
            pend = run_backward_rest(k, x, pend, panels)
    levels, message = run_own_finish(place, got, xs, index)
    got = exchange(message)
    leaf_x = run_leaf_backward(live_rows, got, table, rank, leaf_y, leaf_inv, update_blocks)
    sep_solution = levels.reshape(LEVELS, V, 4, 1, 32).transpose(1, 0, 2, 3, 4)
    return leaf_x, sep_solution


def solution(mesh):
    in_specs = (
        P(ALL, None, None),
        P(ALL, None, None),
        P(ALL, None, None),
        P(ALL, None),
        P(ALL),
        P(None, None, None, "sep", None),
        P(None, None, "sep", None, "leaf"),
        P(None, None, "sep", None, "leaf"),
    )
    out_specs = (P(ALL, None, None), P(None, None, None, "sep", None))
    return jax.shard_map(per_device, mesh=mesh, in_specs=in_specs, out_specs=out_specs, check_vma=False)
```

time: 1130 us -> 301 us (0.27)
  waiting for transfers between devices: 614 us -> 92.9 us
  blocking collectives: 319 us -> 34.6 us
  matrix products: 103 us -> 0 us
  starting transfers between devices: 0.33 us -> 62.6 us
  Pallas kernels: 0 us -> 31.3 us
  local copies, waits for them, and re-layouts: 57 us -> 74.7 us
  between operations: 15.8 us -> 1.57 us
  other arithmetic: 14.6 us -> 1.22 us
    reduce_scatter x7 -> x0, waiting for transfers between devices: 548 us -> none  [the longest x6 465 us: per_device(): lax.psum_scatter(column_term.reshape(vectors, sep_count, segment), 'sep',...]
    all_gather x12 -> x0, blocking collectives: 228 us -> none  [the longest x6 171 us: per_device(): lax.all_gather(current[:, :, None, :], 'sep', axis=2, tiled=True)]
    dot_general x36 -> x0, matrix products: 103 us -> none  [the longest x5 32.4 us: per_device(): jnp.einsum('rc,mqic->rmqi', own_cols, block_set, precision=precise)]
    all_to_all x0 -> x12, waiting for transfers between devices: none -> 92.9 us  [exchange(): return lax.all_to_all(message, axis, 0, 0, tiled=True)]
    psum x7 -> x0, blocking collectives: 90.3 us -> none  [the longest x5 58.7 us: per_device(): correction = lax.psum(pending[:, level_now], 'leaf')]
    all_gather x1 -> x0, waiting for transfers between devices: 66.1 us -> none  [per_device(): lax.all_gather(sep_solution, 'sep', axis=3, tiled=True)]
    unnamed x44 -> x83, local copies, waits for them, and re-layouts: 8.63 us -> 73.5 us
    all_to_all x0 -> x12, starting transfers between devices: none -> 62.6 us  [exchange(): return lax.all_to_all(message, axis, 0, 0, tiled=True)]
  transfers between devices with their start and end apart: 8 -> 12, of which waited for: 8 -> 12; matrix products, arithmetic and copies ran while one was open for 1% -> 1% of each run, Pallas kernels for 0% -> 2%
where the time goes in v1:
time: 301 us; the launch traced here: 299 us
  waiting for transfers between devices  92.9 us (31%)
  local copies, waits for them, and re-layouts  74.7 us (25%)
  starting transfers between devices  62.6 us (21%)
  blocking collectives  34.6 us (11%)
  Pallas kernels  31.3 us (10%)
    all_to_all x12, waiting for transfers between devices, exchange(): return lax.all_to_all(message, axis, 0, 0, tiled=True)  92.9 us
    unnamed x83, local copies, waits for them, and re-layouts  73.5 us
    all_to_all x12, starting transfers between devices, exchange(): return lax.all_to_all(message, axis, 0, 0, tiled=True)  62.6 us
    all_to_all x3, blocking collectives, exchange(): return lax.all_to_all(message, axis, 0, 0, tiled=True)  34.6 us
  transfers between devices with their start and end apart: 12, of which 12 were waited for; matrix products, arithmetic and copies ran while one was open for 1% of the time, Pallas kernels for 2%

profile of v1, /device:TPU:1, one launch (start us, length us, event | category | flops | bytes accessed | tf_op | source)
XLA Modules:
  0.0 298.8 jit_solution(7637489060771145393)
XLA Ops:
  7.2 5.4 %shard_map.95 = (f32[16,1024]{1,0:T(8,128)S(1)}, f32[512,128]{1,0:T(8,128)}, bf16[256,1024]{1,0:T(8,128)(2,1)S(1)}, s32[8,1024]{1,0:T(8,128)S(1)}) custom-call(s32[1]{0:T(128)S(6)} %copy.29.live_ref, f32[16,1024]{1,0:T(8,128)S(1)} %bitcast.52, s32[1,1024]{1,0:T(1,128)S(1)} %copy-done.37, f32[1,1024,1024]{2,1,0:T(8,128)S(1)} %copy-done.19, ...), custom_call_target="tpu_custom_call" | custom-call | flops 201326592 | bytes 8388608 | tf_op jit(solution)/shard_map/pallas_call | solution.py:129
  14.0 11.5 %all-to-all-start = ((f32[128,4,128]{2,1,0:T(4,128)}), f32[128,4,128]{2,1,0:T(4,128)S(1)}, u32[]{:S(2)}, u32[]{:S(2)}) async-start(f32[128,4,128]{2,1,0:T(4,128)} %bitcast.2), calls=%async_computation | async-start | bytes 524288 | tf_op jit(solution)/shard_map/all_to_all | solution.py:460
  27.4 9.0 %all-to-all-done = f32[128,4,128]{2,1,0:T(4,128)S(1)} async-done(((f32[128,4,128]{2,1,0:T(4,128)}), f32[128,4,128]{2,1,0:T(4,128)S(1)}, u32[]{:S(2)}, u32[]{:S(2)}) %all-to-all-start) | async-done | bytes 262176 | tf_op jit(solution)/shard_map/all_to_all | solution.py:460
  37.1 11.7 %all_to_all.165 = f32[32,4,128]{2,1,0:T(4,128)S(1)} all-to-all(f32[32,4,128]{2,1,0:T(4,128)S(1)} %bitcast.53), channel_id=1, replica_groups=mesh['leaf'=4,'sep'=32] {'sep'}, dimensions={0} | all-to-all | bytes 131072 | tf_op jit(solution)/shard_map/all_to_all | solution.py:460
  48.9 3.2 %copy-done = f32[15,4,1,32,1024]{4,3,2,1,0:T(8,128)S(1)} copy-done((f32[15,4,1,32,1024]{4,3,2,1,0:T(8,128)S(1)}, f32[15,4,1,32,1024]{4,3,2,1,0:T(8,128)}, u32[]{:S(2)}) %copy-start) | copy-done | bytes 7864344
  53.2 3.8 %all-to-all-start.2 = ((f32[128,4,128]{2,1,0:T(4,128)}), f32[128,4,128]{2,1,0:T(4,128)S(1)}, u32[]{:S(2)}, u32[]{:S(2)}) async-start(f32[128,4,128]{2,1,0:T(4,128)} %bitcast.6), calls=%async_computation.2 | async-start | bytes 524288 | tf_op jit(solution)/shard_map/all_to_all | solution.py:460
  61.3 6.7 %all-to-all-done.2 = f32[128,4,128]{2,1,0:T(4,128)S(1)} async-done(((f32[128,4,128]{2,1,0:T(4,128)}), f32[128,4,128]{2,1,0:T(4,128)S(1)}, u32[]{:S(2)}, u32[]{:S(2)}) %all-to-all-start.2) | async-done | bytes 262176 | tf_op jit(solution)/shard_map/all_to_all | solution.py:460
  72.4 4.5 %all-to-all-start.3 = ((f32[128,4,128]{2,1,0:T(4,128)}), f32[128,4,128]{2,1,0:T(4,128)S(1)}, u32[]{:S(2)}, u32[]{:S(2)}) async-start(f32[128,4,128]{2,1,0:T(4,128)} %bitcast.8), calls=%async_computation.3 | async-start | bytes 524288 | tf_op jit(solution)/shard_map/all_to_all | solution.py:460
  80.9 7.0 %all-to-all-done.3 = f32[128,4,128]{2,1,0:T(4,128)S(1)} async-done(((f32[128,4,128]{2,1,0:T(4,128)}), f32[128,4,128]{2,1,0:T(4,128)S(1)}, u32[]{:S(2)}, u32[]{:S(2)}) %all-to-all-start.3) | async-done | bytes 262176 | tf_op jit(solution)/shard_map/all_to_all | solution.py:460
  92.2 4.5 %all-to-all-start.4 = ((f32[128,4,128]{2,1,0:T(4,128)}), f32[128,4,128]{2,1,0:T(4,128)S(1)}, u32[]{:S(2)}, u32[]{:S(2)}) async-start(f32[128,4,128]{2,1,0:T(4,128)} %bitcast.10), calls=%async_computation.4 | async-start | bytes 524288 | tf_op jit(solution)/shard_map/all_to_all | solution.py:460
  100.5 7.2 %all-to-all-done.4 = f32[128,4,128]{2,1,0:T(4,128)S(1)} async-done(((f32[128,4,128]{2,1,0:T(4,128)}), f32[128,4,128]{2,1,0:T(4,128)S(1)}, u32[]{:S(2)}, u32[]{:S(2)}) %all-to-all-start.4) | async-done | bytes 262176 | tf_op jit(solution)/shard_map/all_to_all | solution.py:460
  107.7 3.2 %copy-done.6 = f32[15,4,1,32,1024]{4,3,2,1,0:T(8,128)S(1)} copy-done((f32[15,4,1,32,1024]{4,3,2,1,0:T(8,128)S(1)}, f32[15,4,1,32,1024]{4,3,2,1,0:T(8,128)}, u32[]{:S(2)}) %copy-start.6) | copy-done | bytes 7864344
  112.1 4.5 %all-to-all-start.5 = ((f32[128,4,128]{2,1,0:T(4,128)}), f32[128,4,128]{2,1,0:T(4,128)S(1)}, u32[]{:S(2)}, u32[]{:S(2)}) async-start(f32[128,4,128]{2,1,0:T(4,128)} %bitcast.12), calls=%async_computation.5 | async-start | bytes 524288 | tf_op jit(solution)/shard_map/all_to_all | solution.py:460
  120.1 7.5 %all-to-all-done.5 = f32[128,4,128]{2,1,0:T(4,128)S(1)} async-done(((f32[128,4,128]{2,1,0:T(4,128)}), f32[128,4,128]{2,1,0:T(4,128)S(1)}, u32[]{:S(2)}, u32[]{:S(2)}) %all-to-all-start.5) | async-done | bytes 262176 | tf_op jit(solution)/shard_map/all_to_all | solution.py:460
  132.6 4.5 %all-to-all-start.6 = ((f32[128,4,128]{2,1,0:T(4,128)}), f32[128,4,128]{2,1,0:T(4,128)S(1)}, u32[]{:S(2)}, u32[]{:S(2)}) async-start(f32[128,4,128]{2,1,0:T(4,128)} %bitcast.49), calls=%async_computation.6 | async-start | bytes 524288 | tf_op jit(solution)/shard_map/all_to_all | solution.py:460
  140.1 8.0 %all-to-all-done.6 = f32[128,4,128]{2,1,0:T(4,128)S(1)} async-done(((f32[128,4,128]{2,1,0:T(4,128)}), f32[128,4,128]{2,1,0:T(4,128)S(1)}, u32[]{:S(2)}, u32[]{:S(2)}) %all-to-all-start.6) | async-done | bytes 262176 | tf_op jit(solution)/shard_map/all_to_all | solution.py:460
  148.4 7.6 %all_to_all.166 = f32[4,96,128]{2,1,0:T(8,128)S(1)} all-to-all(f32[4,96,128]{2,1,0:T(8,128)S(1)} %bitcast.44), channel_id=1, replica_groups=mesh['leaf'=4,'sep'=32] {'leaf'}, dimensions={0} | all-to-all | bytes 393216 | tf_op jit(solution)/shard_map/all_to_all | solution.py:460
  157.0 6.7 %all-to-all-start.8 = ((f32[128,4,128]{2,1,0:T(4,128)}), f32[128,4,128]{2,1,0:T(4,128)}, u32[]{:S(2)}, u32[]{:S(2)}) async-start(f32[128,4,128]{2,1,0:T(4,128)} %bitcast.18), calls=%async_computation.8 | async-start | bytes 524288 | tf_op jit(solution)/shard_map/all_to_all | solution.py:460
  164.7 9.7 %all-to-all-done.8 = f32[128,4,128]{2,1,0:T(4,128)} async-done(((f32[128,4,128]{2,1,0:T(4,128)}), f32[128,4,128]{2,1,0:T(4,128)}, u32[]{:S(2)}, u32[]{:S(2)}) %all-to-all-start.8) | async-done | bytes 262176 | tf_op jit(solution)/shard_map/all_to_all | solution.py:460
  174.4 3.2 %copy-done.9 = f32[15,4,1,32,1024]{4,3,2,1,0:T(8,128)S(1)} copy-done((f32[15,4,1,32,1024]{4,3,2,1,0:T(8,128)S(1)}, f32[15,4,1,32,1024]{4,3,2,1,0:T(8,128)}, u32[]{:S(2)}) %copy-start.9) | copy-done | bytes 7864344
  179.7 4.5 %all-to-all-start.9 = ((f32[128,4,128]{2,1,0:T(4,128)}), f32[128,4,128]{2,1,0:T(4,128)S(1)}, u32[]{:S(2)}, u32[]{:S(2)}) async-start(f32[128,4,128]{2,1,0:T(4,128)} %bitcast.20), calls=%async_computation.9 | async-start | bytes 524288 | tf_op jit(solution)/shard_map/all_to_all | solution.py:460
  188.2 6.9 %all-to-all-done.9 = f32[128,4,128]{2,1,0:T(4,128)S(1)} async-done(((f32[128,4,128]{2,1,0:T(4,128)}), f32[128,4,128]{2,1,0:T(4,128)S(1)}, u32[]{:S(2)}, u32[]{:S(2)}) %all-to-all-start.9) | async-done | bytes 262176 | tf_op jit(solution)/shard_map/all_to_all | solution.py:460
  199.5 4.5 %all-to-all-start.10 = ((f32[128,4,128]{2,1,0:T(4,128)}), f32[128,4,128]{2,1,0:T(4,128)S(1)}, u32[]{:S(2)}, u32[]{:S(2)}) async-start(f32[128,4,128]{2,1,0:T(4,128)} %bitcast.22), calls=%async_computation.10 | async-start | bytes 524288 | tf_op jit(solution)/shard_map/all_to_all | solution.py:460
  207.9 7.1 %all-to-all-done.10 = f32[128,4,128]{2,1,0:T(4,128)S(1)} async-done(((f32[128,4,128]{2,1,0:T(4,128)}), f32[128,4,128]{2,1,0:T(4,128)S(1)}, u32[]{:S(2)}, u32[]{:S(2)}) %all-to-all-start.10) | async-done | bytes 262176 | tf_op jit(solution)/shard_map/all_to_all | solution.py:460
  219.3 4.5 %all-to-all-start.11 = ((f32[128,4,128]{2,1,0:T(4,128)}), f32[128,4,128]{2,1,0:T(4,128)S(1)}, u32[]{:S(2)}, u32[]{:S(2)}) async-start(f32[128,4,128]{2,1,0:T(4,128)} %bitcast.24), calls=%async_computation.11 | async-start | bytes 524288 | tf_op jit(solution)/shard_map/all_to_all | solution.py:460
  227.5 7.3 %all-to-all-done.11 = f32[128,4,128]{2,1,0:T(4,128)S(1)} async-done(((f32[128,4,128]{2,1,0:T(4,128)}), f32[128,4,128]{2,1,0:T(4,128)S(1)}, u32[]{:S(2)}, u32[]{:S(2)}) %all-to-all-start.11) | async-done | bytes 262176 | tf_op jit(solution)/shard_map/all_to_all | solution.py:460
  239.1 4.5 %all-to-all-start.12 = ((f32[128,4,128]{2,1,0:T(4,128)}), f32[128,4,128]{2,1,0:T(4,128)S(1)}, u32[]{:S(2)}, u32[]{:S(2)}) async-start(f32[128,4,128]{2,1,0:T(4,128)} %bitcast.26), calls=%async_computation.12 | async-start | bytes 524288 | tf_op jit(solution)/shard_map/all_to_all | solution.py:460
  247.1 7.5 %all-to-all-done.12 = f32[128,4,128]{2,1,0:T(4,128)S(1)} async-done(((f32[128,4,128]{2,1,0:T(4,128)}), f32[128,4,128]{2,1,0:T(4,128)S(1)}, u32[]{:S(2)}, u32[]{:S(2)}) %all-to-all-start.12) | async-done | bytes 262176 | tf_op jit(solution)/shard_map/all_to_all | solution.py:460
  258.3 15.3 %all_to_all.167 = f32[128,4,128]{2,1,0:T(4,128)S(1)} all-to-all(f32[128,4,128]{2,1,0:T(4,128)S(1)} %bitcast.51), channel_id=1, replica_groups=mesh['leaf'=4,'sep'=32] {'leaf','sep'}, dimensions={0} | all-to-all | bytes 524288 | tf_op jit(solution)/shard_map/all_to_all | solution.py:460
  275.4 4.5 %all-to-all-start.14 = ((f32[128,2,128]{2,1,0:T(2,128)}), f32[128,2,128]{2,1,0:T(2,128)S(1)}, u32[]{:S(2)}, u32[]{:S(2)}) async-start(f32[128,2,128]{2,1,0:T(2,128)} %bitcast.30), calls=%async_computation.14 | async-start | bytes 262144 | tf_op jit(solution)/shard_map/all_to_all | solution.py:460
  280.9 8.9 %all-to-all-done.14 = f32[128,2,128]{2,1,0:T(2,128)S(1)} async-done(((f32[128,2,128]{2,1,0:T(2,128)}), f32[128,2,128]{2,1,0:T(2,128)S(1)}, u32[]{:S(2)}, u32[]{:S(2)}) %all-to-all-start.14) | async-done | bytes 131104 | tf_op jit(solution)/shard_map/all_to_all | solution.py:460
  294.2 4.6 %shard_map.124 = f32[1,16,1024]{2,1,0:T(8,128)} custom-call(s32[1]{0:T(128)S(6)} %copy.29.live_ref, f32[256,128]{1,0:T(8,128)S(1)} %bitcast.46, bf16[256,1024]{1,0:T(8,128)(2,1)S(1)} %copy-done.24, s32[8,1024]{1,0:T(8,128)S(1)} %get-tuple-element.61.rank_ref, f32[16,1024]{1,0:T(8,128)S(1)} %copy-done.34, f32[1,1024,1024]{2,1,0:T(8,128)S(1)} %copy-done.20, ...), custom_call_target="tpu_custom_call" | custom-call | flops 201326592 | bytes 8388608 | tf_op jit(solution)/shard_map/pallas_call | solution.py:171
  (112 shorter events, 87.5 us)
Async XLA Ops:
  7.2 18.8 %copy-start.40 = (f32[16,6,4,1,32]{4,3,2,1,0:T(1,128)S(1)}, f32[16,6,4,1,32]{4,3,2,1,0:T(1,128)}, u32[]{:S(2)}) copy-start(f32[16,6,4,1,32]{4,3,2,1,0:T(1,128)} %param.13) | copy-start | bytes 147460
  14.0 22.4 %all-to-all-start = ((f32[128,4,128]{2,1,0:T(4,128)}), f32[128,4,128]{2,1,0:T(4,128)S(1)}, u32[]{:S(2)}, u32[]{:S(2)}) async-start(f32[128,4,128]{2,1,0:T(4,128)} %bitcast.2), calls=%async_computation | async-start | bytes 524288 | tf_op jit(solution)/shard_map/all_to_all | solution.py:460
  37.1 16.1 %copy-start.38 = (f32[128,128]{1,0:T(8,128)}, f32[128,128]{1,0:T(8,128)S(1)}, u32[]{:S(2)}) copy-start(f32[128,128]{1,0:T(8,128)S(1)} %get-tuple-element.58.index_ref) | copy-start | bytes 196612
  48.9 3.2 %copy-start = (f32[15,4,1,32,1024]{4,3,2,1,0:T(8,128)S(1)}, f32[15,4,1,32,1024]{4,3,2,1,0:T(8,128)}, u32[]{:S(2)}) copy-start(f32[15,4,1,32,1024]{4,3,2,1,0:T(8,128)} %panel_ref.35) | copy-start | bytes 23592964
  53.2 14.8 %all-to-all-start.2 = ((f32[128,4,128]{2,1,0:T(4,128)}), f32[128,4,128]{2,1,0:T(4,128)S(1)}, u32[]{:S(2)}, u32[]{:S(2)}) async-start(f32[128,4,128]{2,1,0:T(4,128)} %bitcast.6), calls=%async_computation.2 | async-start | bytes 524288 | tf_op jit(solution)/shard_map/all_to_all | solution.py:460
  57.0 3.2 %copy-start.1 = (f32[15,4,1,32,1024]{4,3,2,1,0:T(8,128)S(1)}, f32[15,4,1,32,1024]{4,3,2,1,0:T(8,128)}, u32[]{:S(2)}) copy-start(f32[15,4,1,32,1024]{4,3,2,1,0:T(8,128)} %panel_ref.35) | copy-start | bytes 23592964
  72.4 8.6 %copy-start.25 = (f32[16,1024]{1,0:T(8,128)}, f32[16,1024]{1,0:T(8,128)S(1)}, u32[]{:S(2)}) copy-start(f32[16,1024]{1,0:T(8,128)S(1)} %get-tuple-element.39.x_ref) | copy-start | bytes 196612
  72.4 15.5 %all-to-all-start.3 = ((f32[128,4,128]{2,1,0:T(4,128)}), f32[128,4,128]{2,1,0:T(4,128)S(1)}, u32[]{:S(2)}, u32[]{:S(2)}) async-start(f32[128,4,128]{2,1,0:T(4,128)} %bitcast.8), calls=%async_computation.3 | async-start | bytes 524288 | tf_op jit(solution)/shard_map/all_to_all | solution.py:460
  76.9 3.2 %copy-start.3 = (f32[15,4,1,32,1024]{4,3,2,1,0:T(8,128)S(1)}, f32[15,4,1,32,1024]{4,3,2,1,0:T(8,128)}, u32[]{:S(2)}) copy-start(f32[15,4,1,32,1024]{4,3,2,1,0:T(8,128)} %panel_ref.35) | copy-start | bytes 23592964
  87.9 3.2 %copy-start.4 = (f32[15,4,1,32,1024]{4,3,2,1,0:T(8,128)S(1)}, f32[15,4,1,32,1024]{4,3,2,1,0:T(8,128)}, u32[]{:S(2)}) copy-start(f32[15,4,1,32,1024]{4,3,2,1,0:T(8,128)} %panel_ref.35) | copy-start | bytes 23592964
  92.2 8.3 %copy-start.27 = (f32[16,1024]{1,0:T(8,128)}, f32[16,1024]{1,0:T(8,128)S(1)}, u32[]{:S(2)}) copy-start(f32[16,1024]{1,0:T(8,128)S(1)} %get-tuple-element.41.x_ref) | copy-start | bytes 196612
  92.2 15.5 %all-to-all-start.4 = ((f32[128,4,128]{2,1,0:T(4,128)}), f32[128,4,128]{2,1,0:T(4,128)S(1)}, u32[]{:S(2)}, u32[]{:S(2)}) async-start(f32[128,4,128]{2,1,0:T(4,128)} %bitcast.10), calls=%async_computation.4 | async-start | bytes 524288 | tf_op jit(solution)/shard_map/all_to_all | solution.py:460
  96.8 3.2 %copy-start.5 = (f32[15,4,1,32,1024]{4,3,2,1,0:T(8,128)S(1)}, f32[15,4,1,32,1024]{4,3,2,1,0:T(8,128)}, u32[]{:S(2)}) copy-start(f32[15,4,1,32,1024]{4,3,2,1,0:T(8,128)} %panel_ref.35) | copy-start | bytes 23592964
  107.7 3.2 %copy-start.6 = (f32[15,4,1,32,1024]{4,3,2,1,0:T(8,128)S(1)}, f32[15,4,1,32,1024]{4,3,2,1,0:T(8,128)}, u32[]{:S(2)}) copy-start(f32[15,4,1,32,1024]{4,3,2,1,0:T(8,128)} %panel_ref.35) | copy-start | bytes 23592964
  112.1 8.0 %copy-start.29 = (f32[16,1024]{1,0:T(8,128)}, f32[16,1024]{1,0:T(8,128)S(1)}, u32[]{:S(2)}) copy-start(f32[16,1024]{1,0:T(8,128)S(1)} %get-tuple-element.43.x_ref) | copy-start | bytes 196612
  112.1 15.5 %all-to-all-start.5 = ((f32[128,4,128]{2,1,0:T(4,128)}), f32[128,4,128]{2,1,0:T(4,128)S(1)}, u32[]{:S(2)}, u32[]{:S(2)}) async-start(f32[128,4,128]{2,1,0:T(4,128)} %bitcast.12), calls=%async_computation.5 | async-start | bytes 524288 | tf_op jit(solution)/shard_map/all_to_all | solution.py:460
  116.6 3.2 %copy-start.7 = (f32[15,4,1,32,1024]{4,3,2,1,0:T(8,128)S(1)}, f32[15,4,1,32,1024]{4,3,2,1,0:T(8,128)}, u32[]{:S(2)}) copy-start(f32[15,4,1,32,1024]{4,3,2,1,0:T(8,128)} %panel_ref.35) | copy-start | bytes 23592964
  130.8 6.3 %copy-start.18 = (f32[6,4,1,32,1024]{4,3,2,1,0:T(8,128)S(1)}, f32[6,4,1,32,1024]{4,3,2,1,0:T(8,128)}, u32[]{:S(2)}) copy-start(f32[6,4,1,32,1024]{4,3,2,1,0:T(8,128)} %diag_ref.15) | copy-start | bytes 9437188
  132.6 15.5 %all-to-all-start.6 = ((f32[128,4,128]{2,1,0:T(4,128)}), f32[128,4,128]{2,1,0:T(4,128)S(1)}, u32[]{:S(2)}, u32[]{:S(2)}) async-start(f32[128,4,128]{2,1,0:T(4,128)} %bitcast.49), calls=%async_computation.6 | async-start | bytes 524288 | tf_op jit(solution)/shard_map/all_to_all | solution.py:460
  157.0 17.4 %all-to-all-start.8 = ((f32[128,4,128]{2,1,0:T(4,128)}), f32[128,4,128]{2,1,0:T(4,128)}, u32[]{:S(2)}, u32[]{:S(2)}) async-start(f32[128,4,128]{2,1,0:T(4,128)} %bitcast.18), calls=%async_computation.8 | async-start | bytes 524288 | tf_op jit(solution)/shard_map/all_to_all | solution.py:460
  179.7 15.5 %all-to-all-start.9 = ((f32[128,4,128]{2,1,0:T(4,128)}), f32[128,4,128]{2,1,0:T(4,128)S(1)}, u32[]{:S(2)}, u32[]{:S(2)}) async-start(f32[128,4,128]{2,1,0:T(4,128)} %bitcast.20), calls=%async_computation.9 | async-start | bytes 524288 | tf_op jit(solution)/shard_map/all_to_all | solution.py:460
  184.2 3.2 %copy-start.10 = (f32[15,4,1,32,1024]{4,3,2,1,0:T(8,128)S(1)}, f32[15,4,1,32,1024]{4,3,2,1,0:T(8,128)}, u32[]{:S(2)}) copy-start(f32[15,4,1,32,1024]{4,3,2,1,0:T(8,128)} %panel_ref.35) | copy-start | bytes 23592964
  199.5 15.5 %all-to-all-start.10 = ((f32[128,4,128]{2,1,0:T(4,128)}), f32[128,4,128]{2,1,0:T(4,128)S(1)}, u32[]{:S(2)}, u32[]{:S(2)}) async-start(f32[128,4,128]{2,1,0:T(4,128)} %bitcast.22), calls=%async_computation.10 | async-start | bytes 524288 | tf_op jit(solution)/shard_map/all_to_all | solution.py:460
  204.0 3.2 %copy-start.12 = (f32[15,4,1,32,1024]{4,3,2,1,0:T(8,128)S(1)}, f32[15,4,1,32,1024]{4,3,2,1,0:T(8,128)}, u32[]{:S(2)}) copy-start(f32[15,4,1,32,1024]{4,3,2,1,0:T(8,128)} %panel_ref.35) | copy-start | bytes 23592964
  219.3 15.5 %all-to-all-start.11 = ((f32[128,4,128]{2,1,0:T(4,128)}), f32[128,4,128]{2,1,0:T(4,128)S(1)}, u32[]{:S(2)}, u32[]{:S(2)}) async-start(f32[128,4,128]{2,1,0:T(4,128)} %bitcast.24), calls=%async_computation.11 | async-start | bytes 524288 | tf_op jit(solution)/shard_map/all_to_all | solution.py:460
  223.8 3.2 %copy-start.14 = (f32[15,4,1,32,1024]{4,3,2,1,0:T(8,128)S(1)}, f32[15,4,1,32,1024]{4,3,2,1,0:T(8,128)}, u32[]{:S(2)}) copy-start(f32[15,4,1,32,1024]{4,3,2,1,0:T(8,128)} %panel_ref.35) | copy-start | bytes 23592964
  239.1 15.5 %all-to-all-start.12 = ((f32[128,4,128]{2,1,0:T(4,128)}), f32[128,4,128]{2,1,0:T(4,128)S(1)}, u32[]{:S(2)}, u32[]{:S(2)}) async-start(f32[128,4,128]{2,1,0:T(4,128)} %bitcast.26), calls=%async_computation.12 | async-start | bytes 524288 | tf_op jit(solution)/shard_map/all_to_all | solution.py:460
  243.7 3.2 %copy-start.16 = (f32[15,4,1,32,1024]{4,3,2,1,0:T(8,128)S(1)}, f32[15,4,1,32,1024]{4,3,2,1,0:T(8,128)}, u32[]{:S(2)}) copy-start(f32[15,4,1,32,1024]{4,3,2,1,0:T(8,128)} %panel_ref.35) | copy-start | bytes 23592964
  257.9 15.7 %copy-start.39 = (f32[128,128]{1,0:T(8,128)S(1)}, f32[128,128]{1,0:T(8,128)}, u32[]{:S(2)}) copy-start(f32[128,128]{1,0:T(8,128)} %copy-done.38) | copy-start | bytes 196612
  257.9 31.9 %copy-start.24 = (bf16[256,1024]{1,0:T(8,128)(2,1)S(1)}, bf16[256,1024]{1,0:T(8,128)(2,1)}, u32[]{:S(2)}) copy-start(bf16[256,1024]{1,0:T(8,128)(2,1)} %copy-done.23) | copy-start | bytes 1572868
  257.9 31.9 %copy-start.34 = (f32[16,1024]{1,0:T(8,128)S(1)}, f32[16,1024]{1,0:T(8,128)}, u32[]{:S(2)}) copy-start(f32[16,1024]{1,0:T(8,128)} %copy-done.33) | copy-start | bytes 196612
  275.4 14.4 %all-to-all-start.14 = ((f32[128,2,128]{2,1,0:T(2,128)}), f32[128,2,128]{2,1,0:T(2,128)S(1)}, u32[]{:S(2)}, u32[]{:S(2)}) async-start(f32[128,2,128]{2,1,0:T(2,128)} %bitcast.30), calls=%async_computation.14 | async-start | bytes 262144 | tf_op jit(solution)/shard_map/all_to_all | solution.py:460
  (21 other events, 41.5 us)

commit v2 on v1

v2 whole, which is shorter than its diff:
```python
import functools

import jax
import jax.numpy as jnp
from jax import lax
from jax.experimental import pallas as pl
from jax.experimental.pallas import tpu as pltpu
from jax.sharding import PartitionSpec as P

F32 = jnp.float32
BF16 = jnp.bfloat16
V = 16
LEVELS = 6
ROWS = 128
COLS = 1024
UPD = 1024
ALL = ("leaf", "sep")
VMEM_LIMIT = 52 * 1024 * 1024
NT = (((1,), (1,)), ((), ()))
NN = (((1,), (0,)), ((), ()))


def pair_index(upper, lower):
    return lower * (LEVELS - 1) - lower * (lower - 1) // 2 + upper - lower - 1


def iota(shape, dim):
    return lax.broadcasted_iota(jnp.int32, shape, dim)


def dot(a, b, dims):
    return lax.dot_general(a, b, dims, preferred_element_type=F32)


def split(x):
    high = x.astype(BF16)
    return high, (x - high.astype(F32)).astype(BF16)


def product(x, w, dims):
    xh, xl = split(x)
    wh, wl = split(w)
    m = x.shape[0]
    both = dot(jnp.concatenate([xh, xl], 0), wh, dims)
    return both[:m] + both[m:] + dot(xh, wl, dims)


def exact_rows(x, onehot, dims):
    xh, xl = split(x)
    m = x.shape[0]
    both = dot(jnp.concatenate([xh, xl], 0), onehot, dims)
    return both[:m] + both[m:]


def block_swap(t):
    gap = (iota((16, 128), 1) // 32 - iota((16, 128), 0) // 4) & 3
    out = t
    for d in range(1, 4):
        moved = pltpu.roll(pltpu.roll(t, 32 * d, 1), 16 - 4 * d, 0)
        out = jnp.where(gap == d, moved, out)
    return out


def call(body, out_shape, in_specs, out_specs, scratch=(), flops=0, nbytes=0, limit=VMEM_LIMIT):
    return pl.pallas_call(
        body,
        out_shape=out_shape,
        in_specs=in_specs,
        out_specs=out_specs,
        scratch_shapes=scratch,
        compiler_params=pltpu.CompilerParams(vmem_limit_bytes=limit),
        cost_estimate=pl.CostEstimate(flops=flops, bytes_accessed=nbytes, transcendentals=0),
    )


def sds(shape, dtype=F32):
    return jax.ShapeDtypeStruct(shape, dtype)


VM = pl.BlockSpec(memory_space=pltpu.VMEM)
SMEM = pl.BlockSpec(memory_space=pltpu.SMEM)
HBM = pl.BlockSpec(memory_space=pltpu.HBM)


def fetch(sources, buffer, sems):
    copies = [pltpu.make_async_copy(src, buffer.at[n], sems.at[n]) for n, src in enumerate(sources)]
    for one in copies:
        one.start()
    return copies


def leaf_forward(live_ref, rhs_hbm, map_hbm, inv_ref, upd_ref, y_ref, msg_ref, t_ref, rank_ref, rhs_ref, map_ref, buffer, sems):
    step = UPD // 4
    small = [pltpu.make_async_copy(map_hbm, map_ref, sems.at[8]), pltpu.make_async_copy(rhs_hbm, rhs_ref, sems.at[9])]
    for one in small:
        one.start()
    sources = []
    for n in range(4):
        for ref in (inv_ref, upd_ref):
            sources.append(ref.at[0, pl.ds(step * n, step), :])
    copies = fetch(sources, buffer, sems)
    small[0].wait()
    rows = map_ref[...]
    owner = (rows >> 5) & 127
    hot = (iota((128, UPD), 0) == owner).astype(F32)
    ones = jnp.where((iota((128, 256), 0) < iota((128, 256), 1)), 1.0, 0.0).astype(BF16)
    carry = jnp.zeros((128, 128), F32)
    before = []
    for n in range(UPD // 128):
        counts = dot(hot[:, 128 * n : 128 * n + 128].astype(BF16), ones, NN)
        before.append(counts[:, :128] + carry)
        carry += counts[:, 128:]
    before = jnp.concatenate(before, 1)
    rank = jnp.sum(hot * before, axis=0, keepdims=True).astype(jnp.int32)
    rank_ref[...] = jnp.broadcast_to(rank, rank_ref.shape)
    for half in range(2):
        t_ref[pl.ds(128 * half, 128), :] = jnp.where((rank >> 3) == half, hot, 0.0).astype(BF16)
    live = iota((1, UPD), 1) < live_ref[0]
    local = (rows >> 12) * 32 + (rows & 31) + 1
    places = jnp.where((iota((128, UPD), 0) == rank) & live, local.astype(F32), 0.0)
    msg_ref[pl.ds(2, 128, 4), :] = dot(hot.astype(BF16), places.astype(BF16), NT)
    msg_ref[pl.ds(3, 128, 4), :] = jnp.zeros((128, 128), F32)
    acc = jnp.zeros((V, UPD), F32)
    small[1].wait()
    for n in range(4):
        copies[2 * n].wait()
        y_part = product(rhs_ref[0], buffer[2 * n], NT)
        y_ref[:, step * n : step * n + step] = y_part
        copies[2 * n + 1].wait()
        acc += product(y_part, buffer[2 * n + 1], NN)
    group = iota((128, UPD), 0) >> 4
    spread = jnp.where((group == (rank & 7)) & live, jnp.concatenate([acc] * 8, 0), 0.0)
    parts = jnp.concatenate(split(spread), 0)
    for half in range(2):
        got = dot(t_ref[pl.ds(128 * half, 128), :], parts, NT)
        msg_ref[pl.ds(half, 128, 4), :] = got[:, :128] + got[:, 128:]


def run_leaf_forward(live, rhs, rows, inv, upd):
    return call(
        leaf_forward,
        (sds((V, UPD)), sds((512, 128)), sds((256, UPD), BF16), sds((8, UPD), jnp.int32)),
        [SMEM, HBM, HBM, HBM, HBM],
        (VM, VM, VM, VM),
        scratch=[
            pltpu.VMEM((1, V, 1024), F32),
            pltpu.VMEM((1, UPD), jnp.int32),
            pltpu.VMEM((8, UPD // 4, 1024), F32),
            pltpu.SemaphoreType.DMA((10,)),
        ],
        flops=2 * 16 * 3 * (2 << 20),
        nbytes=8 << 20,
        limit=60 * 1024 * 1024,
    )(live, rhs, rows, inv, upd)


def leaf_backward(live_ref, got_ref, t_ref, rank_ref, y_ref, inv_ref, upd_ref, out_ref, buffer, sems):
    step = UPD // 4
    sources = []
    for n in range(4):
        for ref in (upd_ref, inv_ref):
            sources.append(ref.at[0, pl.ds(step * n, step), :])
    copies = fetch(sources, buffer, sems)
    live = iota((1, UPD), 1) < live_ref[0]
    group = iota((128, UPD), 0) >> 4
    total = jnp.zeros((128, UPD), F32)
    for half in range(2):
        values = got_ref[pl.ds(half, 128, 2), :].T
        total += exact_rows(values, t_ref[pl.ds(128 * half, 128), :], NN)
    total = jnp.where((group == (rank_ref[0:1, :] & 7)) & live, total, 0.0)
    mapped = total[0:16]
    for g in range(1, 8):
        mapped += total[16 * g : 16 * g + 16]
    out = jnp.zeros((V, 1024), F32)
    for n in range(4):
        copies[2 * n].wait()
        z = y_ref[:, step * n : step * n + step] - product(mapped, buffer[2 * n], NT)
        copies[2 * n + 1].wait()
        out += product(z, buffer[2 * n + 1], NN)
    out_ref[0] = out


def run_leaf_backward(live, got, t, rank, y, inv, upd):
    return call(
        leaf_backward,
        sds((1, V, 1024)),
        [SMEM, VM, VM, VM, VM, HBM, HBM],
        VM,
        scratch=[pltpu.VMEM((8, UPD // 4, 1024), F32), pltpu.SemaphoreType.DMA((8,))],
        flops=2 * 16 * 3 * (2 << 20),
        nbytes=8 << 20,
    )(live, got, t, rank, y, inv, upd)


def own_start(place_ref, got_ref, rhs_ref, pend_ref, msg_ref, index_ref):
    values = [got_ref[pl.ds(half, 128, 4), :].T for half in range(2)]
    index = got_ref[pl.ds(2, 128, 4), :]
    index_ref[...] = index
    column = (iota((128, 256), 1) + 1).astype(F32)
    total = jnp.zeros((V, 256), F32)
    for half in range(2):
        for g in range(8):
            j = 8 * half + g
            hot = jnp.where(index[:, j : j + 1] == column, 1.0, 0.0).astype(BF16)
            total += exact_rows(values[half][16 * g : 16 * g + 16], hot, NN)
    mine = iota((V, 128), 1) // 32 == place_ref[0]
    first = None
    for k in range(LEVELS):
        one = total[:, 32 * k : 32 * k + 32]
        row = jnp.where(mine, rhs_ref[:, 128 * k : 128 * k + 128] - jnp.concatenate([one] * 4, 1), 0.0)
        pend_ref[k] = row
        if k == 0:
            first = row
    turned = block_swap(first)
    chunk = turned[0:4] + turned[4:8] + turned[8:12] + turned[12:16]
    msg_ref[...] = jnp.concatenate([chunk] * 32, 0)


def run_own_start(place, got, rhs):
    return call(
        own_start,
        (sds((LEVELS, V, 128)), sds((128, 128)), sds((128, 128))),
        [SMEM, VM, VM],
        (VM, VM, VM),
        flops=1 << 27,
        nbytes=1 << 19,
    )(place, got, rhs)


def columns_of(got_ref, parts):
    total = got_ref[pl.ds(0, 128), :]
    for p in range(1, parts):
        total += got_ref[pl.ds(128 * p, 128), :]
    return jnp.concatenate([block_swap(total[16 * t : 16 * t + 16]) for t in range(8)], 1)


def row_message(msg_ref, rows):
    turned = block_swap(rows)
    for q in range(4):
        msg_ref[pl.ds(128 * q, 128), :] = jnp.concatenate([turned[4 * q : 4 * q + 4]] * 32, 0)


def block_parts(block):
    return jnp.concatenate(split(block.reshape(ROWS, COLS)), 0)


def times_columns(x, w):
    out = dot(jnp.concatenate(split(x), 0), w, NT)
    return (out[:V, :ROWS] + out[V:, :ROWS]) + (out[:V, ROWS:] + out[V:, ROWS:])


def times_rows(x, w):
    half = jnp.concatenate(split(x), 0)
    out = dot(jnp.concatenate([half, half], 1), w, NN)
    return out[:V] + out[V:]


PARTS = (2 * ROWS, COLS)


def first_block(panels_ref, w_ref, buffer, sems):
    fetch([panels_ref.at[pair_index(1, 0), :, 0]], buffer, sems)[0].wait()
    w_ref[...] = block_parts(buffer[0])


def buffers(count):
    return [pltpu.VMEM((count, 4, 32, COLS), F32), pltpu.SemaphoreType.DMA((count,))]


def run_first_block(panels):
    return call(first_block, sds(PARTS, BF16), [HBM], VM, scratch=buffers(1), flops=1 << 20, nbytes=1 << 20)(panels)


def forward_first(k, parts, got_ref, pend_ref, w_ref, x_ref, msg_ref):
    x = columns_of(got_ref, parts)
    x_ref[...] = x
    row_message(msg_ref, pend_ref[k + 1] - times_columns(x, w_ref[...]))


def run_forward_first(k, parts, got, pend, w):
    return call(
        functools.partial(forward_first, k, parts),
        (sds((V, COLS)), sds((512, 128))),
        [VM, VM, VM],
        (VM, VM),
        flops=1 << 24,
        nbytes=1 << 20,
    )(got, pend, w)


def forward_rest(k, x_ref, pend_ref, panels_ref, diag_ref, out_ref, y_ref, w_ref, buffer, sems):
    later = range(k + 2, LEVELS)
    sources = [panels_ref.at[pair_index(j, k), :, 0] for j in later] + [diag_ref.at[k, :, 0]]
    sources.append(panels_ref.at[pair_index(k + 2, k + 1), :, 0] if k + 2 < LEVELS else diag_ref.at[k + 1, :, 0])
    copies = fetch(sources, buffer, sems)
    x = x_ref[...]
    out_ref[...] = pend_ref[...]
    for n, j in enumerate(later):
        copies[n].wait()
        out_ref[j] = pend_ref[j] - times_columns(x, block_parts(buffer[n]))
    copies[-2].wait()
    y_ref[...] = times_columns(x, block_parts(buffer[len(sources) - 2]))
    copies[-1].wait()
    w_ref[...] = block_parts(buffer[len(sources) - 1])


def run_forward_rest(k, x, pend, panels, diag):
    count = LEVELS - k
    return call(
        functools.partial(forward_rest, k),
        (sds((LEVELS, V, 128)), sds((V, 128)), sds(PARTS, BF16)),
        [VM, VM, HBM, HBM],
        (VM, VM, VM),
        scratch=buffers(count),
        flops=count << 24,
        nbytes=count << 19,
    )(x, pend, panels, diag)


def forward_last(got_ref, y0, y1, y2, y3, y4, w_ref, msg_ref):
    x = columns_of(got_ref, 4)
    last = times_columns(x, w_ref[...])
    for l in range(4):
        for k, one in enumerate((y0, y1, y2, y3, y4)):
            msg_ref[pl.ds(96 * l + 16 * k, 16), :] = one[...]
        msg_ref[pl.ds(96 * l + 80, 16), :] = last


def run_forward_last(got, ys, w):
    return call(
        forward_last,
        sds((4 * 96, 128)),
        [VM] + [VM] * 5 + [VM],
        VM,
        flops=1 << 24,
        nbytes=1 << 20,
    )(got, *ys, w)


def column_message(msg_ref, columns):
    for t in range(8):
        turned = block_swap(columns[:, 128 * t : 128 * t + 128])
        for l in range(4):
            msg_ref[pl.ds(128 * l + 16 * t, 16), :] = turned


def backward_start(got_ref, w_ref, y_ref, msg_ref):
    y = got_ref[pl.ds(0, 96), :]
    for l in range(1, 4):
        y += got_ref[pl.ds(96 * l, 96), :]
    y_ref[...] = y
    column_message(msg_ref, times_rows(y[80:96], w_ref[...]))


def run_backward_start(got, w):
    return call(
        backward_start,
        (sds((96, 128)), sds((512, 128))),
        [VM, VM],
        (VM, VM),
        flops=1 << 24,
        nbytes=1 << 20,
    )(got, w)


def backward_diag(y_ref, panels_ref, diag_ref, out_ref, w_ref, buffer, sems):
    count = LEVELS - 1
    sources = [diag_ref.at[k, :, 0] for k in range(count)] + [panels_ref.at[pair_index(count, count - 1), :, 0]]
    copies = fetch(sources, buffer, sems)
    for k in range(count):
        copies[k].wait()
        out_ref[k] = times_rows(y_ref[pl.ds(16 * k, 16), :], block_parts(buffer[k]))
    copies[count].wait()
    w_ref[...] = block_parts(buffer[count])


def run_backward_diag(y, panels, diag):
    return call(
        backward_diag,
        (sds((LEVELS - 1, V, COLS)), sds(PARTS, BF16)),
        [VM, HBM, HBM],
        (VM, VM),
        scratch=buffers(LEVELS),
        flops=5 << 24,
        nbytes=3 << 20,
    )(y, panels, diag)


def rows_of(got_ref):
    parts = []
    for q in range(4):
        total = got_ref[pl.ds(128 * q, 8), :]
        for t in range(1, 16):
            total += got_ref[pl.ds(128 * q + 8 * t, 8), :]
        parts.append(total[0:4] + total[4:8])
    return block_swap(jnp.concatenate(parts, 0))


def backward_first(k, got_ref, pend_ref, w_ref, x_ref, msg_ref):
    x = rows_of(got_ref)
    x_ref[...] = x
    column_message(msg_ref, pend_ref[k - 1] - times_rows(x, w_ref[...]))


def run_backward_first(k, got, pend, w):
    return call(
        functools.partial(backward_first, k),
        (sds((V, 128)), sds((512, 128))),
        [VM, VM, VM],
        (VM, VM),
        flops=1 << 24,
        nbytes=1 << 20,
    )(got, pend, w)


def backward_rest(k, x_ref, pend_ref, panels_ref, out_ref, w_ref, buffer, sems):
    count = k - 1
    sources = [panels_ref.at[pair_index(k, j), :, 0] for j in range(count)]
    sources.append(panels_ref.at[pair_index(k - 1, k - 2), :, 0])
    copies = fetch(sources, buffer, sems)
    x = x_ref[...]
    for j in range(count):
        copies[j].wait()
        out_ref[j] = pend_ref[j] - times_rows(x, block_parts(buffer[j]))
    copies[count].wait()
    w_ref[...] = block_parts(buffer[count])


def run_backward_rest(k, x, pend, panels):
    count = k - 1
    return call(
        functools.partial(backward_rest, k),
        (sds((count, V, COLS)), sds(PARTS, BF16)),
        [VM, VM, HBM],
        (VM, VM),
        scratch=buffers(count + 1),
        flops=count << 24,
        nbytes=count << 19,
    )(x, pend, panels)


def own_finish(place_ref, got_ref, x1, x2, x3, x4, x5, index_ref, x_ref, msg_ref):
    x0 = rows_of(got_ref)
    levels = [x0] + [r[...] for r in (x1, x2, x3, x4, x5)]
    mine = []
    for k, x in enumerate(levels):
        x_ref[k] = x
        one = jnp.zeros((V, 32), F32)
        for q in range(4):
            one = jnp.where(place_ref[0] == q, x[:, 32 * q : 32 * q + 32], one)
        mine.append(one)
    rows = jnp.concatenate(mine + [jnp.zeros((V, 64), F32)], 1)
    high, low = split(jnp.concatenate([rows] * 8, 0))
    table = jnp.concatenate([high, low], 0)
    index = index_ref[...]
    column = (iota((128, 256), 1) + 1).astype(F32)
    group = iota((128, 128), 1) >> 4
    for half in range(2):
        out = jnp.zeros((128, 128), F32)
        for g in range(8):
            j = 8 * half + g
            hot = jnp.where(index[:, j : j + 1] == column, 1.0, 0.0).astype(BF16)
            got = dot(hot, table, NT)
            out = jnp.where(group == g, got[:, :128] + got[:, 128:], out)
        msg_ref[pl.ds(half, 128, 2), :] = out


def run_own_finish(place, got, xs, index):
    return call(
        own_finish,
        (sds((LEVELS, V, 128)), sds((256, 128))),
        [SMEM, VM] + [VM] * 5 + [VM],
        (VM, VM),
        flops=1 << 27,
        nbytes=1 << 20,
    )(place, got, *xs, index)


def exchange(message, axis=ALL):
    return lax.all_to_all(message, axis, 0, 0, tiled=True)


def per_device(leaf_rhs, leaf_inv, update_blocks, row_map, live_rows, sep_rhs, inv_diag, panels):
    place = lax.axis_index("leaf").astype(jnp.int32).reshape(1)
    rhs = sep_rhs.reshape(V, LEVELS * 128)
    leaf_y, message, table, rank = run_leaf_forward(live_rows, leaf_rhs, row_map, leaf_inv, update_blocks)
    pend, message, index = run_own_start(place, exchange(message), rhs)
    got, parts = exchange(message, "sep"), 1
    w = run_first_block(panels)
    ys = []
    for k in range(LEVELS - 1):
        x, message = run_forward_first(k, parts, got, pend, w)
        got, parts = exchange(message), 4
        pend, y, w = run_forward_rest(k, x, pend, panels, inv_diag)
        ys.append(y)
    y, message = run_backward_start(exchange(run_forward_last(got, ys, w), "leaf"), w)
    got = exchange(message)
    pend, w = run_backward_diag(y, panels, inv_diag)
    xs = []
    for k in range(LEVELS - 1, 0, -1):
        x, message = run_backward_first(k, got, pend, w)
        xs.insert(0, x)
        got = exchange(message)
        if k > 1:
            pend, w = run_backward_rest(k, x, pend, panels)
    levels, message = run_own_finish(place, got, xs, index)
    got = exchange(message)
    leaf_x = run_leaf_backward(live_rows, got, table, rank, leaf_y, leaf_inv, update_blocks)
    sep_solution = levels.reshape(LEVELS, V, 4, 1, 32).transpose(1, 0, 2, 3, 4)
    return leaf_x, sep_solution


def solution(mesh):
    in_specs = (
        P(ALL, None, None),
        P(ALL, None, None),
        P(ALL, None, None),
        P(ALL, None),
        P(ALL),
        P(None, None, None, "sep", None),
        P(None, None, "sep", None, "leaf"),
        P(None, None, "sep", None, "leaf"),
    )
    out_specs = (P(ALL, None, None), P(None, None, None, "sep", None))
    return jax.shard_map(per_device, mesh=mesh, in_specs=in_specs, out_specs=out_specs, check_vma=False)
```

time: 301 us -> 257 us (0.85)
  local copies, waits for them, and re-layouts: 74.7 us -> 1.7 us
  waiting for transfers between devices: 92.9 us -> 113 us
  Pallas kernels: 31.3 us -> 49.2 us
  blocking collectives: 34.6 us -> 22.8 us
  starting transfers between devices: 62.6 us -> 66.6 us
    unnamed x83 -> x9, local copies, waits for them, and re-layouts: 73.5 us -> 0.53 us
    all_to_all x12 -> x13, waiting for transfers between devices: 92.9 us -> 113 us  [exchange(): return lax.all_to_all(message, axis, 0, 0, tiled=True)]
    pallas_call x28 -> x25, Pallas kernels: 25.2 us -> 41.4 us  [the longest x5 12 us: run_forward_rest(): call(functools.partial(forward_rest, k), (sds((LEVELS, V, 128)), sds((V,...]
    all_to_all x3 -> x2, blocking collectives: 34.6 us -> 22.8 us  [exchange(): return lax.all_to_all(message, axis, 0, 0, tiled=True)]
    all_to_all x12 -> x13, starting transfers between devices: 62.6 us -> 66.6 us  [exchange(): return lax.all_to_all(message, axis, 0, 0, tiled=True)]
  transfers between devices with their start and end apart: 12 -> 13, of which waited for: 12 -> 13; matrix products, arithmetic and copies ran while one was open for 1% -> 1% of each run, Pallas kernels for 2% -> 9%
where the time goes in v2:
time: 257 us; the launch traced here: 256 us
  waiting for transfers between devices  113 us (44%)
  starting transfers between devices  66.6 us (26%)
  Pallas kernels  49.2 us (19%)
  blocking collectives  22.8 us (9%)
    all_to_all x13, waiting for transfers between devices, exchange(): return lax.all_to_all(message, axis, 0, 0, tiled=True)  113 us
    all_to_all x13, starting transfers between devices, exchange(): return lax.all_to_all(message, axis, 0, 0, tiled=True)  66.6 us
    all_to_all x2, blocking collectives, exchange(): return lax.all_to_all(message, axis, 0, 0, tiled=True)  22.8 us
    pallas_call x5, Pallas kernels, run_forward_rest(): call(functools.partial(forward_rest, k), (sds((LEVELS, V, 128)), sds((V,...  12 us
    pallas_call x4, Pallas kernels, run_backward_rest(): call(functools.partial(backward_rest, k), (sds((count, V, COLS)), sds(PAR...  6.76 us
    pallas_call x1, Pallas kernels, run_leaf_forward(): call(leaf_forward, (sds((V, UPD)), sds((512, 128)), sds((256, UPD), BF16)...  6.44 us
    pallas_call x1, Pallas kernels, run_leaf_backward(): call(leaf_backward, sds((1, V, 1024)), [SMEM, VM, VM, VM, VM, HBM, HBM],...  6 us
    pallas_call x5, Pallas kernels, run_forward_first(): call(functools.partial(forward_first, k, parts), (sds((V, COLS)), sds((51...  5.54 us
  transfers between devices with their start and end apart: 13, of which 13 were waited for; matrix products, arithmetic and copies ran while one was open for 1% of the time, Pallas kernels for 9%

profile of v2, /device:TPU:1, one launch (start us, length us, event | category | flops | bytes accessed | tf_op | source)
XLA Modules:
  0.0 256.4 jit_solution(7911246801674541421)
XLA Ops:
  1.3 6.4 %shard_map.95 = (f32[16,1024]{1,0:T(8,128)}, f32[512,128]{1,0:T(8,128)}, bf16[256,1024]{1,0:T(8,128)(2,1)}, s32[8,1024]{1,0:T(8,128)}) custom-call(s32[1]{0:T(128)S(6)} %copy.13.live_ref, f32[1,16,1024]{2,1,0:T(8,128)} %rhs_hbm.1, s32[1,1024]{1,0:T(1,128)} %map_hbm.1, f32[1,1024,1024]{2,1,0:T(8,128)} %inv_ref.3, f32[1,1024,1024]{2,1,0:T(8,128)} %upd_ref.3), custom_call_target="tpu_custom_call" | custom-call | flops 201326592 | bytes 8388608 | tf_op jit(solution)/shard_map/pallas_call | solution.py:140
  7.7 11.5 %all-to-all-start = ((f32[128,4,128]{2,1,0:T(4,128)}), f32[128,4,128]{2,1,0:T(4,128)S(1)}, u32[]{:S(2)}, u32[]{:S(2)}) async-start(f32[128,4,128]{2,1,0:T(4,128)} %bitcast.51), calls=%async_computation | async-start | bytes 524288 | tf_op jit(solution)/shard_map/all_to_all | solution.py:480
  21.2 9.0 %all-to-all-done = f32[128,4,128]{2,1,0:T(4,128)S(1)} async-done(((f32[128,4,128]{2,1,0:T(4,128)}), f32[128,4,128]{2,1,0:T(4,128)S(1)}, u32[]{:S(2)}, u32[]{:S(2)}) %all-to-all-start) | async-done | bytes 262176 | tf_op jit(solution)/shard_map/all_to_all | solution.py:480
  31.5 4.6 %all-to-all-start.1 = ((f32[32,4,128]{2,1,0:T(4,128)}), f32[32,4,128]{2,1,0:T(4,128)S(1)}, u32[]{:S(2)}, u32[]{:S(2)}) async-start(f32[32,4,128]{2,1,0:T(4,128)} %bitcast.3), calls=%async_computation.1 | async-start | bytes 131072 | tf_op jit(solution)/shard_map/all_to_all | solution.py:480
  37.3 6.3 %all-to-all-done.1 = f32[32,4,128]{2,1,0:T(4,128)S(1)} async-done(((f32[32,4,128]{2,1,0:T(4,128)}), f32[32,4,128]{2,1,0:T(4,128)S(1)}, u32[]{:S(2)}, u32[]{:S(2)}) %all-to-all-start.1) | async-done | bytes 65568 | tf_op jit(solution)/shard_map/all_to_all | solution.py:480
  44.7 3.8 %all-to-all-start.2 = ((f32[128,4,128]{2,1,0:T(4,128)}), f32[128,4,128]{2,1,0:T(4,128)S(1)}, u32[]{:S(2)}, u32[]{:S(2)}) async-start(f32[128,4,128]{2,1,0:T(4,128)} %bitcast.5), calls=%async_computation.2 | async-start | bytes 524288 | tf_op jit(solution)/shard_map/all_to_all | solution.py:480
  48.5 3.0 %shard_map.99 = (f32[6,16,128]{2,1,0:T(8,128)S(1)}, f32[16,128]{1,0:T(8,128)S(1)}, bf16[256,1024]{1,0:T(8,128)(2,1)S(1)}) custom-call(f32[16,1024]{1,0:T(8,128)S(1)} %get-tuple-element.61.x_ref, f32[6,16,128]{2,1,0:T(8,128)S(1)} %get-tuple-element.59.pend_ref, f32[15,4,1,32,1024]{4,3,2,1,0:T(8,128)} %panels_ref.21, f32[6,4,1,32,1024]{4,3,2,1,0:T(8,128)} %diag_ref.11), custom_call_target="tpu_custom_call" | custom-call | flops 100663296 | bytes 3145728 | tf_op jit(solution)/shard_map/pallas_call | solution.py:309
  51.6 8.0 %all-to-all-done.2 = f32[128,4,128]{2,1,0:T(4,128)S(1)} async-done(((f32[128,4,128]{2,1,0:T(4,128)}), f32[128,4,128]{2,1,0:T(4,128)S(1)}, u32[]{:S(2)}, u32[]{:S(2)}) %all-to-all-start.2) | async-done | bytes 262176 | tf_op jit(solution)/shard_map/all_to_all | solution.py:480
  60.6 4.5 %all-to-all-start.3 = ((f32[128,4,128]{2,1,0:T(4,128)}), f32[128,4,128]{2,1,0:T(4,128)S(1)}, u32[]{:S(2)}, u32[]{:S(2)}) async-start(f32[128,4,128]{2,1,0:T(4,128)} %bitcast.7), calls=%async_computation.3 | async-start | bytes 524288 | tf_op jit(solution)/shard_map/all_to_all | solution.py:480
  65.2 2.8 %shard_map.101 = (f32[6,16,128]{2,1,0:T(8,128)S(1)}, f32[16,128]{1,0:T(8,128)S(1)}, bf16[256,1024]{1,0:T(8,128)(2,1)S(1)}) custom-call(f32[16,1024]{1,0:T(8,128)S(1)} %get-tuple-element.65.x_ref, f32[6,16,128]{2,1,0:T(8,128)S(1)} %get-tuple-element.62.pend_ref, f32[15,4,1,32,1024]{4,3,2,1,0:T(8,128)} %panels_ref.21, f32[6,4,1,32,1024]{4,3,2,1,0:T(8,128)} %diag_ref.11), custom_call_target="tpu_custom_call" | custom-call | flops 83886080 | bytes 2621440 | tf_op jit(solution)/shard_map/pallas_call | solution.py:309
  67.9 8.2 %all-to-all-done.3 = f32[128,4,128]{2,1,0:T(4,128)S(1)} async-done(((f32[128,4,128]{2,1,0:T(4,128)}), f32[128,4,128]{2,1,0:T(4,128)S(1)}, u32[]{:S(2)}, u32[]{:S(2)}) %all-to-all-start.3) | async-done | bytes 262176 | tf_op jit(solution)/shard_map/all_to_all | solution.py:480
  77.3 4.5 %all-to-all-start.4 = ((f32[128,4,128]{2,1,0:T(4,128)}), f32[128,4,128]{2,1,0:T(4,128)S(1)}, u32[]{:S(2)}, u32[]{:S(2)}) async-start(f32[128,4,128]{2,1,0:T(4,128)} %bitcast.9), calls=%async_computation.4 | async-start | bytes 524288 | tf_op jit(solution)/shard_map/all_to_all | solution.py:480
  84.1 8.8 %all-to-all-done.4 = f32[128,4,128]{2,1,0:T(4,128)S(1)} async-done(((f32[128,4,128]{2,1,0:T(4,128)}), f32[128,4,128]{2,1,0:T(4,128)S(1)}, u32[]{:S(2)}, u32[]{:S(2)}) %all-to-all-start.4) | async-done | bytes 262176 | tf_op jit(solution)/shard_map/all_to_all | solution.py:480
  93.9 4.5 %all-to-all-start.5 = ((f32[128,4,128]{2,1,0:T(4,128)}), f32[128,4,128]{2,1,0:T(4,128)S(1)}, u32[]{:S(2)}, u32[]{:S(2)}) async-start(f32[128,4,128]{2,1,0:T(4,128)} %bitcast.11), calls=%async_computation.5 | async-start | bytes 524288 | tf_op jit(solution)/shard_map/all_to_all | solution.py:480
  100.4 9.0 %all-to-all-done.5 = f32[128,4,128]{2,1,0:T(4,128)S(1)} async-done(((f32[128,4,128]{2,1,0:T(4,128)}), f32[128,4,128]{2,1,0:T(4,128)S(1)}, u32[]{:S(2)}, u32[]{:S(2)}) %all-to-all-start.5) | async-done | bytes 262176 | tf_op jit(solution)/shard_map/all_to_all | solution.py:480
  110.6 4.7 %all-to-all-start.6 = ((f32[128,4,128]{2,1,0:T(4,128)}), f32[128,4,128]{2,1,0:T(4,128)S(1)}, u32[]{:S(2)}, u32[]{:S(2)}) async-start(f32[128,4,128]{2,1,0:T(4,128)} %bitcast.13), calls=%async_computation.6 | async-start | bytes 524288 | tf_op jit(solution)/shard_map/all_to_all | solution.py:480
  117.2 9.1 %all-to-all-done.6 = f32[128,4,128]{2,1,0:T(4,128)S(1)} async-done(((f32[128,4,128]{2,1,0:T(4,128)}), f32[128,4,128]{2,1,0:T(4,128)S(1)}, u32[]{:S(2)}, u32[]{:S(2)}) %all-to-all-start.6) | async-done | bytes 262176 | tf_op jit(solution)/shard_map/all_to_all | solution.py:480
  126.6 7.5 %all_to_all.165 = f32[4,96,128]{2,1,0:T(8,128)S(1)} all-to-all(f32[4,96,128]{2,1,0:T(8,128)S(1)} %bitcast.45), channel_id=1, replica_groups=mesh['leaf'=4,'sep'=32] {'leaf'}, dimensions={0} | all-to-all | bytes 393216 | tf_op jit(solution)/shard_map/all_to_all | solution.py:480
  135.1 5.8 %all-to-all-start.8 = ((f32[128,4,128]{2,1,0:T(4,128)}), f32[128,4,128]{2,1,0:T(4,128)S(1)}, u32[]{:S(2)}, u32[]{:S(2)}) async-start(f32[128,4,128]{2,1,0:T(4,128)} %bitcast.17), calls=%async_computation.8 | async-start | bytes 524288 | tf_op jit(solution)/shard_map/all_to_all | solution.py:480
  143.1 8.7 %all-to-all-done.8 = f32[128,4,128]{2,1,0:T(4,128)S(1)} async-done(((f32[128,4,128]{2,1,0:T(4,128)}), f32[128,4,128]{2,1,0:T(4,128)S(1)}, u32[]{:S(2)}, u32[]{:S(2)}) %all-to-all-start.8) | async-done | bytes 262176 | tf_op jit(solution)/shard_map/all_to_all | solution.py:480
  152.9 4.5 %all-to-all-start.9 = ((f32[128,4,128]{2,1,0:T(4,128)}), f32[128,4,128]{2,1,0:T(4,128)S(1)}, u32[]{:S(2)}, u32[]{:S(2)}) async-start(f32[128,4,128]{2,1,0:T(4,128)} %bitcast.19), calls=%async_computation.9 | async-start | bytes 524288 | tf_op jit(solution)/shard_map/all_to_all | solution.py:480
  159.4 9.0 %all-to-all-done.9 = f32[128,4,128]{2,1,0:T(4,128)S(1)} async-done(((f32[128,4,128]{2,1,0:T(4,128)}), f32[128,4,128]{2,1,0:T(4,128)S(1)}, u32[]{:S(2)}, u32[]{:S(2)}) %all-to-all-start.9) | async-done | bytes 262176 | tf_op jit(solution)/shard_map/all_to_all | solution.py:480
  169.5 4.5 %all-to-all-start.10 = ((f32[128,4,128]{2,1,0:T(4,128)}), f32[128,4,128]{2,1,0:T(4,128)S(1)}, u32[]{:S(2)}, u32[]{:S(2)}) async-start(f32[128,4,128]{2,1,0:T(4,128)} %bitcast.21), calls=%async_computation.10 | async-start | bytes 524288 | tf_op jit(solution)/shard_map/all_to_all | solution.py:480
  175.8 9.2 %all-to-all-done.10 = f32[128,4,128]{2,1,0:T(4,128)S(1)} async-done(((f32[128,4,128]{2,1,0:T(4,128)}), f32[128,4,128]{2,1,0:T(4,128)S(1)}, u32[]{:S(2)}, u32[]{:S(2)}) %all-to-all-start.10) | async-done | bytes 262176 | tf_op jit(solution)/shard_map/all_to_all | solution.py:480
  186.1 4.5 %all-to-all-start.11 = ((f32[128,4,128]{2,1,0:T(4,128)}), f32[128,4,128]{2,1,0:T(4,128)S(1)}, u32[]{:S(2)}, u32[]{:S(2)}) async-start(f32[128,4,128]{2,1,0:T(4,128)} %bitcast.23), calls=%async_computation.11 | async-start | bytes 524288 | tf_op jit(solution)/shard_map/all_to_all | solution.py:480
  192.2 9.4 %all-to-all-done.11 = f32[128,4,128]{2,1,0:T(4,128)S(1)} async-done(((f32[128,4,128]{2,1,0:T(4,128)}), f32[128,4,128]{2,1,0:T(4,128)S(1)}, u32[]{:S(2)}, u32[]{:S(2)}) %all-to-all-start.11) | async-done | bytes 262176 | tf_op jit(solution)/shard_map/all_to_all | solution.py:480
  202.7 4.5 %all-to-all-start.12 = ((f32[128,4,128]{2,1,0:T(4,128)}), f32[128,4,128]{2,1,0:T(4,128)S(1)}, u32[]{:S(2)}, u32[]{:S(2)}) async-start(f32[128,4,128]{2,1,0:T(4,128)} %bitcast.25), calls=%async_computation.12 | async-start | bytes 524288 | tf_op jit(solution)/shard_map/all_to_all | solution.py:480
  208.7 9.5 %all-to-all-done.12 = f32[128,4,128]{2,1,0:T(4,128)S(1)} async-done(((f32[128,4,128]{2,1,0:T(4,128)}), f32[128,4,128]{2,1,0:T(4,128)S(1)}, u32[]{:S(2)}, u32[]{:S(2)}) %all-to-all-start.12) | async-done | bytes 262176 | tf_op jit(solution)/shard_map/all_to_all | solution.py:480
  218.6 15.3 %all_to_all.166 = f32[128,4,128]{2,1,0:T(4,128)S(1)} all-to-all(f32[128,4,128]{2,1,0:T(4,128)S(1)} %bitcast.50), channel_id=1, replica_groups=mesh['leaf'=4,'sep'=32] {'leaf','sep'}, dimensions={0} | all-to-all | bytes 524288 | tf_op jit(solution)/shard_map/all_to_all | solution.py:480
  235.8 4.5 %all-to-all-start.14 = ((f32[128,2,128]{2,1,0:T(2,128)}), f32[128,2,128]{2,1,0:T(2,128)S(1)}, u32[]{:S(2)}, u32[]{:S(2)}) async-start(f32[128,2,128]{2,1,0:T(2,128)} %bitcast.29), calls=%async_computation.14 | async-start | bytes 262144 | tf_op jit(solution)/shard_map/all_to_all | solution.py:480
  241.3 8.9 %all-to-all-done.14 = f32[128,2,128]{2,1,0:T(2,128)S(1)} async-done(((f32[128,2,128]{2,1,0:T(2,128)}), f32[128,2,128]{2,1,0:T(2,128)S(1)}, u32[]{:S(2)}, u32[]{:S(2)}) %all-to-all-start.14) | async-done | bytes 131104 | tf_op jit(solution)/shard_map/all_to_all | solution.py:480
  250.2 6.0 %shard_map.121 = f32[1,16,1024]{2,1,0:T(8,128)} custom-call(s32[1]{0:T(128)S(6)} %copy.13.live_ref, f32[256,128]{1,0:T(8,128)S(1)} %bitcast.46, bf16[256,1024]{1,0:T(8,128)(2,1)S(1)} %copy-done, s32[8,1024]{1,0:T(8,128)S(1)} %copy-done.2, f32[16,1024]{1,0:T(8,128)S(1)} %copy-done.1, f32[1,1024,1024]{2,1,0:T(8,128)} %inv_ref.3, f32[1,1024,1024]{2,1,0:T(8,128)} %upd_ref.3), custom_call_target="tpu_custom_call" | custom-call | flops 201326592 | bytes 8388608 | tf_op jit(solution)/shard_map/pallas_call | solution.py:184
  (36 shorter events, 33.9 us)
Async XLA Ops:
  1.3 18.5 %copy-start.3 = (f32[16,6,4,1,32]{4,3,2,1,0:T(1,128)S(1)}, f32[16,6,4,1,32]{4,3,2,1,0:T(1,128)}, u32[]{:S(2)}) copy-start(f32[16,6,4,1,32]{4,3,2,1,0:T(1,128)} %param.13) | copy-start | bytes 147460
  7.7 22.4 %all-to-all-start = ((f32[128,4,128]{2,1,0:T(4,128)}), f32[128,4,128]{2,1,0:T(4,128)S(1)}, u32[]{:S(2)}, u32[]{:S(2)}) async-start(f32[128,4,128]{2,1,0:T(4,128)} %bitcast.51), calls=%async_computation | async-start | bytes 524288 | tf_op jit(solution)/shard_map/all_to_all | solution.py:480
  31.5 12.1 %all-to-all-start.1 = ((f32[32,4,128]{2,1,0:T(4,128)}), f32[32,4,128]{2,1,0:T(4,128)S(1)}, u32[]{:S(2)}, u32[]{:S(2)}) async-start(f32[32,4,128]{2,1,0:T(4,128)} %bitcast.3), calls=%async_computation.1 | async-start | bytes 131072 | tf_op jit(solution)/shard_map/all_to_all | solution.py:480
  44.7 14.8 %all-to-all-start.2 = ((f32[128,4,128]{2,1,0:T(4,128)}), f32[128,4,128]{2,1,0:T(4,128)S(1)}, u32[]{:S(2)}, u32[]{:S(2)}) async-start(f32[128,4,128]{2,1,0:T(4,128)} %bitcast.5), calls=%async_computation.2 | async-start | bytes 524288 | tf_op jit(solution)/shard_map/all_to_all | solution.py:480
  60.6 15.5 %all-to-all-start.3 = ((f32[128,4,128]{2,1,0:T(4,128)}), f32[128,4,128]{2,1,0:T(4,128)S(1)}, u32[]{:S(2)}, u32[]{:S(2)}) async-start(f32[128,4,128]{2,1,0:T(4,128)} %bitcast.7), calls=%async_computation.3 | async-start | bytes 524288 | tf_op jit(solution)/shard_map/all_to_all | solution.py:480
  77.3 15.5 %all-to-all-start.4 = ((f32[128,4,128]{2,1,0:T(4,128)}), f32[128,4,128]{2,1,0:T(4,128)S(1)}, u32[]{:S(2)}, u32[]{:S(2)}) async-start(f32[128,4,128]{2,1,0:T(4,128)} %bitcast.9), calls=%async_computation.4 | async-start | bytes 524288 | tf_op jit(solution)/shard_map/all_to_all | solution.py:480
  93.9 15.5 %all-to-all-start.5 = ((f32[128,4,128]{2,1,0:T(4,128)}), f32[128,4,128]{2,1,0:T(4,128)S(1)}, u32[]{:S(2)}, u32[]{:S(2)}) async-start(f32[128,4,128]{2,1,0:T(4,128)} %bitcast.11), calls=%async_computation.5 | async-start | bytes 524288 | tf_op jit(solution)/shard_map/all_to_all | solution.py:480
  110.6 15.7 %all-to-all-start.6 = ((f32[128,4,128]{2,1,0:T(4,128)}), f32[128,4,128]{2,1,0:T(4,128)S(1)}, u32[]{:S(2)}, u32[]{:S(2)}) async-start(f32[128,4,128]{2,1,0:T(4,128)} %bitcast.13), calls=%async_computation.6 | async-start | bytes 524288 | tf_op jit(solution)/shard_map/all_to_all | solution.py:480
  135.1 16.7 %all-to-all-start.8 = ((f32[128,4,128]{2,1,0:T(4,128)}), f32[128,4,128]{2,1,0:T(4,128)S(1)}, u32[]{:S(2)}, u32[]{:S(2)}) async-start(f32[128,4,128]{2,1,0:T(4,128)} %bitcast.17), calls=%async_computation.8 | async-start | bytes 524288 | tf_op jit(solution)/shard_map/all_to_all | solution.py:480
  152.9 15.5 %all-to-all-start.9 = ((f32[128,4,128]{2,1,0:T(4,128)}), f32[128,4,128]{2,1,0:T(4,128)S(1)}, u32[]{:S(2)}, u32[]{:S(2)}) async-start(f32[128,4,128]{2,1,0:T(4,128)} %bitcast.19), calls=%async_computation.9 | async-start | bytes 524288 | tf_op jit(solution)/shard_map/all_to_all | solution.py:480
  169.5 15.5 %all-to-all-start.10 = ((f32[128,4,128]{2,1,0:T(4,128)}), f32[128,4,128]{2,1,0:T(4,128)S(1)}, u32[]{:S(2)}, u32[]{:S(2)}) async-start(f32[128,4,128]{2,1,0:T(4,128)} %bitcast.21), calls=%async_computation.10 | async-start | bytes 524288 | tf_op jit(solution)/shard_map/all_to_all | solution.py:480
  186.1 15.5 %all-to-all-start.11 = ((f32[128,4,128]{2,1,0:T(4,128)}), f32[128,4,128]{2,1,0:T(4,128)S(1)}, u32[]{:S(2)}, u32[]{:S(2)}) async-start(f32[128,4,128]{2,1,0:T(4,128)} %bitcast.23), calls=%async_computation.11 | async-start | bytes 524288 | tf_op jit(solution)/shard_map/all_to_all | solution.py:480
  202.7 15.5 %all-to-all-start.12 = ((f32[128,4,128]{2,1,0:T(4,128)}), f32[128,4,128]{2,1,0:T(4,128)S(1)}, u32[]{:S(2)}, u32[]{:S(2)}) async-start(f32[128,4,128]{2,1,0:T(4,128)} %bitcast.25), calls=%async_computation.12 | async-start | bytes 524288 | tf_op jit(solution)/shard_map/all_to_all | solution.py:480
  207.3 42.9 %copy-start = (bf16[256,1024]{1,0:T(8,128)(2,1)S(1)}, bf16[256,1024]{1,0:T(8,128)(2,1)}, u32[]{:S(2)}) copy-start(bf16[256,1024]{1,0:T(8,128)(2,1)} %get-tuple-element.108.t_ref) | copy-start | bytes 1572868
  207.3 42.9 %copy-start.1 = (f32[16,1024]{1,0:T(8,128)S(1)}, f32[16,1024]{1,0:T(8,128)}, u32[]{:S(2)}) copy-start(f32[16,1024]{1,0:T(8,128)} %get-tuple-element.110.y_ref) | copy-start | bytes 196612
  207.3 42.9 %copy-start.2 = (s32[8,1024]{1,0:T(8,128)S(1)}, s32[8,1024]{1,0:T(8,128)}, u32[]{:S(2)}) copy-start(s32[8,1024]{1,0:T(8,128)} %get-tuple-element.109.rank_ref) | copy-start | bytes 98308
  235.8 14.4 %all-to-all-start.14 = ((f32[128,2,128]{2,1,0:T(2,128)}), f32[128,2,128]{2,1,0:T(2,128)S(1)}, u32[]{:S(2)}, u32[]{:S(2)}) async-start(f32[128,2,128]{2,1,0:T(2,128)} %bitcast.29), calls=%async_computation.14 | async-start | bytes 262144 | tf_op jit(solution)/shard_map/all_to_all | solution.py:480

commit v3 on v2

--- a/solution.py
+++ b/solution.py
@@ -14,8 +14,9 @@
 ROWS = 128
 COLS = 1024
 UPD = 1024
+CHUNKS = 2
 ALL = ("leaf", "sep")
-VMEM_LIMIT = 52 * 1024 * 1024
+VMEM_LIMIT = 51 * 1024 * 1024
 NT = (((1,), (1,)), ((), ()))
 NN = (((1,), (0,)), ((), ()))
 
@@ -79,6 +80,7 @@
 
 VM = pl.BlockSpec(memory_space=pltpu.VMEM)
 SMEM = pl.BlockSpec(memory_space=pltpu.SMEM)
+ANY = pl.BlockSpec(memory_space=pl.ANY)
 HBM = pl.BlockSpec(memory_space=pltpu.HBM)
 
 
@@ -90,12 +92,12 @@
 
 
 def leaf_forward(live_ref, rhs_hbm, map_hbm, inv_ref, upd_ref, y_ref, msg_ref, t_ref, rank_ref, rhs_ref, map_ref, buffer, sems):
-    step = UPD // 4
-    small = [pltpu.make_async_copy(map_hbm, map_ref, sems.at[8]), pltpu.make_async_copy(rhs_hbm, rhs_ref, sems.at[9])]
+    step = UPD // CHUNKS
+    small = [pltpu.make_async_copy(map_hbm, map_ref, sems.at[2 * CHUNKS]), pltpu.make_async_copy(rhs_hbm, rhs_ref, sems.at[2 * CHUNKS + 1])]
     for one in small:
         one.start()
     sources = []
-    for n in range(4):
+    for n in range(CHUNKS):
         for ref in (inv_ref, upd_ref):
             sources.append(ref.at[0, pl.ds(step * n, step), :])
     copies = fetch(sources, buffer, sems)
@@ -122,7 +124,7 @@
     msg_ref[pl.ds(3, 128, 4), :] = jnp.zeros((128, 128), F32)
     acc = jnp.zeros((V, UPD), F32)
     small[1].wait()
-    for n in range(4):
+    for n in range(CHUNKS):
         copies[2 * n].wait()
         y_part = product(rhs_ref[0], buffer[2 * n], NT)
         y_ref[:, step * n : step * n + step] = y_part
@@ -145,8 +147,8 @@
         scratch=[
             pltpu.VMEM((1, V, 1024), F32),
             pltpu.VMEM((1, UPD), jnp.int32),
-            pltpu.VMEM((8, UPD // 4, 1024), F32),
-            pltpu.SemaphoreType.DMA((10,)),
+            pltpu.VMEM((2 * CHUNKS, UPD // CHUNKS, 1024), F32),
+            pltpu.SemaphoreType.DMA((2 * CHUNKS + 2,)),
         ],
         flops=2 * 16 * 3 * (2 << 20),
         nbytes=8 << 20,
@@ -155,9 +157,9 @@
 
 
 def leaf_backward(live_ref, got_ref, t_ref, rank_ref, y_ref, inv_ref, upd_ref, out_ref, buffer, sems):
-    step = UPD // 4
+    step = UPD // CHUNKS
     sources = []
-    for n in range(4):
+    for n in range(CHUNKS):
         for ref in (upd_ref, inv_ref):
             sources.append(ref.at[0, pl.ds(step * n, step), :])
     copies = fetch(sources, buffer, sems)
@@ -172,7 +174,7 @@
     for g in range(1, 8):
         mapped += total[16 * g : 16 * g + 16]
     out = jnp.zeros((V, 1024), F32)
-    for n in range(4):
+    for n in range(CHUNKS):
         copies[2 * n].wait()
         z = y_ref[:, step * n : step * n + step] - product(mapped, buffer[2 * n], NT)
         copies[2 * n + 1].wait()
@@ -186,23 +188,24 @@
         sds((1, V, 1024)),
         [SMEM, VM, VM, VM, VM, HBM, HBM],
         VM,
-        scratch=[pltpu.VMEM((8, UPD // 4, 1024), F32), pltpu.SemaphoreType.DMA((8,))],
+        scratch=[pltpu.VMEM((2 * CHUNKS, UPD // CHUNKS, 1024), F32), pltpu.SemaphoreType.DMA((2 * CHUNKS,))],
         flops=2 * 16 * 3 * (2 << 20),
         nbytes=8 << 20,
     )(live, got, t, rank, y, inv, upd)
 
 
-def own_start(place_ref, got_ref, rhs_ref, pend_ref, msg_ref, index_ref):
+def own_start(place_ref, got_ref, rhs_ref, after_ref, pend_ref, msg_ref, index_ref):
     values = [got_ref[pl.ds(half, 128, 4), :].T for half in range(2)]
     index = got_ref[pl.ds(2, 128, 4), :]
     index_ref[...] = index
     column = (iota((128, 256), 1) + 1).astype(F32)
-    total = jnp.zeros((V, 256), F32)
+    hot, rows = [], []
     for half in range(2):
         for g in range(8):
             j = 8 * half + g
-            hot = jnp.where(index[:, j : j + 1] == column, 1.0, 0.0).astype(BF16)
-            total += exact_rows(values[half][16 * g : 16 * g + 16], hot, NN)
+            hot.append(jnp.where(index[:, j : j + 1] == column, 1.0, 0.0).astype(BF16))
+            rows.append(values[half][16 * g : 16 * g + 16])
+    total = exact_rows(jnp.concatenate(rows, 1), jnp.concatenate(hot, 0), NN)
     mine = iota((V, 128), 1) // 32 == place_ref[0]
     first = None
     for k in range(LEVELS):
@@ -216,15 +219,15 @@
     msg_ref[...] = jnp.concatenate([chunk] * 32, 0)
 
 
-def run_own_start(place, got, rhs):
+def run_own_start(place, got, rhs, after):
     return call(
         own_start,
         (sds((LEVELS, V, 128)), sds((128, 128)), sds((128, 128))),
-        [SMEM, VM, VM],
+        [SMEM, VM, VM, ANY],
         (VM, VM, VM),
         flops=1 << 27,
         nbytes=1 << 19,
-    )(place, got, rhs)
+    )(place, got, rhs, after)
 
 
 def columns_of(got_ref, parts):
@@ -258,63 +261,86 @@
 PARTS = (2 * ROWS, COLS)
 
 
-def first_block(panels_ref, w_ref, buffer, sems):
+def buffers(count):
+    return [pltpu.VMEM((count, 4, 32, COLS), F32), pltpu.SemaphoreType.DMA((count,))]
+
+
+def block_of(panels_ref, diag_ref, upper, lower):
+    return diag_ref.at[lower, :, 0] if upper == lower else panels_ref.at[pair_index(upper, lower), :, 0]
+
+
+def first_block(after_ref, panels_ref, w_ref, buffer, sems):
     fetch([panels_ref.at[pair_index(1, 0), :, 0]], buffer, sems)[0].wait()
     w_ref[...] = block_parts(buffer[0])
 
 
-def buffers(count):
-    return [pltpu.VMEM((count, 4, 32, COLS), F32), pltpu.SemaphoreType.DMA((count,))]
-
-
-def run_first_block(panels):
-    return call(first_block, sds(PARTS, BF16), [HBM], VM, scratch=buffers(1), flops=1 << 20, nbytes=1 << 20)(panels)
-
-
-def forward_first(k, parts, got_ref, pend_ref, w_ref, x_ref, msg_ref):
+def run_first_block(after, panels):
+    return call(first_block, sds(PARTS, BF16), [ANY, HBM], VM, scratch=buffers(1), flops=1 << 20, nbytes=1 << 20)(
+        after, panels
+    )
+
+
+def forward_step(level, parts, count, *refs):
+    got_ref, pend_ref = refs[:2]
+    earlier, blocks, (x_ref, msg_ref) = refs[2 : 1 + count], refs[1 + count : 1 + 2 * count], refs[-2:]
     x = columns_of(got_ref, parts)
     x_ref[...] = x
-    row_message(msg_ref, pend_ref[k + 1] - times_columns(x, w_ref[...]))
-
-
-def run_forward_first(k, parts, got, pend, w):
-    return call(
-        functools.partial(forward_first, k, parts),
+    rows = pend_ref[level]
+    for one, w_ref in zip([r[...] for r in earlier] + [x], blocks):
+        rows -= times_columns(one, w_ref[...])
+    row_message(msg_ref, rows)
+
+
+def run_forward_step(level, parts, got, pend, earlier, blocks):
+    return call(
+        functools.partial(forward_step, level, parts, len(blocks)),
         (sds((V, COLS)), sds((512, 128))),
-        [VM, VM, VM],
+        [VM] * (2 + len(earlier) + len(blocks)),
         (VM, VM),
-        flops=1 << 24,
-        nbytes=1 << 20,
-    )(got, pend, w)
-
-
-def forward_rest(k, x_ref, pend_ref, panels_ref, diag_ref, out_ref, y_ref, w_ref, buffer, sems):
-    later = range(k + 2, LEVELS)
-    sources = [panels_ref.at[pair_index(j, k), :, 0] for j in later] + [diag_ref.at[k, :, 0]]
-    sources.append(panels_ref.at[pair_index(k + 2, k + 1), :, 0] if k + 2 < LEVELS else diag_ref.at[k + 1, :, 0])
-    copies = fetch(sources, buffer, sems)
-    x = x_ref[...]
+        flops=len(blocks) << 24,
+        nbytes=len(blocks) << 20,
+    )(got, pend, *earlier, *blocks)
+
+
+def forward_rest(levels, wanted, *refs):
+    n = len(levels)
+    x_refs, (pend_ref, panels_ref, diag_ref), refs = refs[:n], refs[n : n + 3], refs[n + 3 :]
+    out_ref, y_refs, w_refs, (buffer, sems) = refs[0], refs[1 : 1 + n], refs[1 + n : -2], refs[-2:]
+    later = range(levels[-1] + 2, LEVELS)
+    pairs = [(j, k) for j in later for k in levels] + [(k, k) for k in levels] + list(wanted)
+    copies = fetch([block_of(panels_ref, diag_ref, *pair) for pair in pairs], buffer, sems)
     out_ref[...] = pend_ref[...]
-    for n, j in enumerate(later):
-        copies[n].wait()
-        out_ref[j] = pend_ref[j] - times_columns(x, block_parts(buffer[n]))
-    copies[-2].wait()
-    y_ref[...] = times_columns(x, block_parts(buffer[len(sources) - 2]))
-    copies[-1].wait()
-    w_ref[...] = block_parts(buffer[len(sources) - 1])
-
-
-def run_forward_rest(k, x, pend, panels, diag):
-    count = LEVELS - k
-    return call(
-        functools.partial(forward_rest, k),
-        (sds((LEVELS, V, 128)), sds((V, 128)), sds(PARTS, BF16)),
-        [VM, VM, HBM, HBM],
-        (VM, VM, VM),
+    slot = 0
+    for j in later:
+        rows = pend_ref[j]
+        for x_ref in x_refs:
+            copies[slot].wait()
+            rows -= times_columns(x_ref[...], block_parts(buffer[slot]))
+            slot += 1
+        out_ref[j] = rows
+    for x_ref, y_ref in zip(x_refs, y_refs):
+        copies[slot].wait()
+        y_ref[...] = times_columns(x_ref[...], block_parts(buffer[slot]))
+        slot += 1
+    for w_ref in w_refs:
+        copies[slot].wait()
+        w_ref[...] = block_parts(buffer[slot])
+        slot += 1
+
+
+def run_forward_rest(levels, xs, pend, panels, diag, wanted):
+    n = len(levels)
+    count = n * (LEVELS - 1 - levels[-1]) + len(wanted)
+    out = call(
+        functools.partial(forward_rest, levels, wanted),
+        (sds((LEVELS, V, 128)), *[sds((V, 128))] * n, *[sds(PARTS, BF16)] * len(wanted)),
+        [VM] * n + [VM, HBM, HBM],
+        (VM,) * (1 + n + len(wanted)),
         scratch=buffers(count),
         flops=count << 24,
         nbytes=count << 19,
-    )(x, pend, panels, diag)
+    )(*xs, pend, panels, diag)
+    return out[0], out[1 : 1 + n], out[1 + n :]
 
 
 def forward_last(got_ref, y0, y1, y2, y3, y4, w_ref, msg_ref):
@@ -363,27 +389,30 @@
     )(got, w)
 
 
-def backward_diag(y_ref, panels_ref, diag_ref, out_ref, w_ref, buffer, sems):
+def backward_diag(wanted, y_ref, panels_ref, diag_ref, out_ref, *refs):
+    w_refs, (buffer, sems) = refs[:-2], refs[-2:]
     count = LEVELS - 1
-    sources = [diag_ref.at[k, :, 0] for k in range(count)] + [panels_ref.at[pair_index(count, count - 1), :, 0]]
-    copies = fetch(sources, buffer, sems)
+    pairs = [(k, k) for k in range(count)] + list(wanted)
+    copies = fetch([block_of(panels_ref, diag_ref, *pair) for pair in pairs], buffer, sems)
     for k in range(count):
         copies[k].wait()
         out_ref[k] = times_rows(y_ref[pl.ds(16 * k, 16), :], block_parts(buffer[k]))
-    copies[count].wait()
-    w_ref[...] = block_parts(buffer[count])
-
-
-def run_backward_diag(y, panels, diag):
-    return call(
-        backward_diag,
-        (sds((LEVELS - 1, V, COLS)), sds(PARTS, BF16)),
+    for n, w_ref in enumerate(w_refs):
+        copies[count + n].wait()
+        w_ref[...] = block_parts(buffer[count + n])
+
+
+def run_backward_diag(y, panels, diag, wanted):
+    out = call(
+        functools.partial(backward_diag, wanted),
+        (sds((LEVELS - 1, V, COLS)), *[sds(PARTS, BF16)] * len(wanted)),
         [VM, HBM, HBM],
-        (VM, VM),
-        scratch=buffers(LEVELS),
-        flops=5 << 24,
-        nbytes=3 << 20,
+        (VM,) * (1 + len(wanted)),
+        scratch=buffers(LEVELS - 1 + len(wanted)),
+        flops=8 << 24,
+        nbytes=4 << 20,
     )(y, panels, diag)
+    return out[0], out[1:]
 
 
 def rows_of(got_ref):
@@ -396,47 +425,62 @@
     return block_swap(jnp.concatenate(parts, 0))
 
 
-def backward_first(k, got_ref, pend_ref, w_ref, x_ref, msg_ref):
+def backward_step(level, count, *refs):
+    got_ref, pend_ref = refs[:2]
+    earlier, blocks, (x_ref, msg_ref) = refs[2 : 1 + count], refs[1 + count : 1 + 2 * count], refs[-2:]
     x = rows_of(got_ref)
     x_ref[...] = x
-    column_message(msg_ref, pend_ref[k - 1] - times_rows(x, w_ref[...]))
-
-
-def run_backward_first(k, got, pend, w):
-    return call(
-        functools.partial(backward_first, k),
+    columns = pend_ref[level]
+    for one, w_ref in zip([r[...] for r in earlier] + [x], blocks):
+        columns -= times_rows(one, w_ref[...])
+    column_message(msg_ref, columns)
+
+
+def run_backward_step(level, got, pend, earlier, blocks):
+    return call(
+        functools.partial(backward_step, level, len(blocks)),
         (sds((V, 128)), sds((512, 128))),
-        [VM, VM, VM],
+        [VM] * (2 + len(earlier) + len(blocks)),
         (VM, VM),
-        flops=1 << 24,
-        nbytes=1 << 20,
-    )(got, pend, w)
-
-
-def backward_rest(k, x_ref, pend_ref, panels_ref, out_ref, w_ref, buffer, sems):
-    count = k - 1
-    sources = [panels_ref.at[pair_index(k, j), :, 0] for j in range(count)]
-    sources.append(panels_ref.at[pair_index(k - 1, k - 2), :, 0])
-    copies = fetch(sources, buffer, sems)
-    x = x_ref[...]
-    for j in range(count):
-        copies[j].wait()
-        out_ref[j] = pend_ref[j] - times_rows(x, block_parts(buffer[j]))
-    copies[count].wait()
-    w_ref[...] = block_parts(buffer[count])
-
-
-def run_backward_rest(k, x, pend, panels):
-    count = k - 1
-    return call(
-        functools.partial(backward_rest, k),
-        (sds((count, V, COLS)), sds(PARTS, BF16)),
-        [VM, VM, HBM],
-        (VM, VM),
-        scratch=buffers(count + 1),
+        flops=len(blocks) << 24,
+        nbytes=len(blocks) << 20,
+    )(got, pend, *earlier, *blocks)
+
+
+def backward_rest(levels, wanted, *refs):
+    n = len(levels)
+    x_refs, (pend_ref, panels_ref), refs = refs[:n], refs[n : n + 2], refs[n + 2 :]
+    out_ref, w_refs, (buffer, sems) = refs[0], refs[1:-2], refs[-2:]
+    lower = range(levels[-1] - 2, -1, -1)
+    pairs = [(k, j) for j in lower for k in levels] + list(wanted)
+    copies = fetch([block_of(panels_ref, None, *pair) for pair in pairs], buffer, sems)
+    slot = 0
+    for j in lower:
+        columns = pend_ref[j]
+        for x_ref in x_refs:
+            copies[slot].wait()
+            columns -= times_rows(x_ref[...], block_parts(buffer[slot]))
+            slot += 1
+        out_ref[j] = columns
+    for w_ref in w_refs:
+        copies[slot].wait()
+        w_ref[...] = block_parts(buffer[slot])
+        slot += 1
+
+
+def run_backward_rest(levels, xs, pend, panels, wanted):
+    n, lower = len(levels), levels[-1] - 1
+    count = n * lower + len(wanted)
+    out = call(
+        functools.partial(backward_rest, levels, wanted),
+        (sds((lower, V, COLS)), *[sds(PARTS, BF16)] * len(wanted)),
+        [VM] * n + [VM, HBM],
+        (VM,) * (1 + len(wanted)),
+        scratch=buffers(count),
         flops=count << 24,
         nbytes=count << 19,
-    )(x, pend, panels)
+    )(*xs, pend, panels)
+    return out[0], out[1:]
 
 
 def own_finish(place_ref, got_ref, x1, x2, x3, x4, x5, index_ref, x_ref, msg_ref):
@@ -444,9 +488,9 @@
     levels = [x0] + [r[...] for r in (x1, x2, x3, x4, x5)]
     mine = []
     for k, x in enumerate(levels):
-        x_ref[k] = x
         one = jnp.zeros((V, 32), F32)
         for q in range(4):
+            x_ref[pl.ds(4 * k + q, V, 4 * LEVELS), :] = x[:, 32 * q : 32 * q + 32]
             one = jnp.where(place_ref[0] == q, x[:, 32 * q : 32 * q + 32], one)
         mine.append(one)
     rows = jnp.concatenate(mine + [jnp.zeros((V, 64), F32)], 1)
@@ -468,7 +512,7 @@
 def run_own_finish(place, got, xs, index):
     return call(
         own_finish,
-        (sds((LEVELS, V, 128)), sds((256, 128))),
+        (sds((V * LEVELS * 4, 32)), sds((256, 128))),
         [SMEM, VM] + [VM] * 5 + [VM],
         (VM, VM),
         flops=1 << 27,
@@ -484,29 +528,42 @@
     place = lax.axis_index("leaf").astype(jnp.int32).reshape(1)
     rhs = sep_rhs.reshape(V, LEVELS * 128)
     leaf_y, message, table, rank = run_leaf_forward(live_rows, leaf_rhs, row_map, leaf_inv, update_blocks)
-    pend, message, index = run_own_start(place, exchange(message), rhs)
-    got, parts = exchange(message, "sep"), 1
-    w = run_first_block(panels)
-    ys = []
-    for k in range(LEVELS - 1):
-        x, message = run_forward_first(k, parts, got, pend, w)
-        got, parts = exchange(message), 4
-        pend, y, w = run_forward_rest(k, x, pend, panels, inv_diag)
-        ys.append(y)
-    y, message = run_backward_start(exchange(run_forward_last(got, ys, w), "leaf"), w)
-    got = exchange(message)
-    pend, w = run_backward_diag(y, panels, inv_diag)
-    xs = []
-    for k in range(LEVELS - 1, 0, -1):
-        x, message = run_backward_first(k, got, pend, w)
-        xs.insert(0, x)
-        got = exchange(message)
-        if k > 1:
-            pend, w = run_backward_rest(k, x, pend, panels)
-    levels, message = run_own_finish(place, got, xs, index)
+    got = exchange(message)
+    block = run_first_block(leaf_y, panels)
+    pend, message, index = run_own_start(place, got, rhs, block)
+    got = exchange(message, "sep")
+    x0, message = run_forward_step(1, 1, got, pend, [], [block])
+    got = exchange(message)
+    pend, (y0,), (near, far, last) = run_forward_rest((0,), [x0], pend, panels, inv_diag, ((2, 1), (3, 1), (3, 2)))
+    x1, message = run_forward_step(2, 4, got, pend, [], [near])
+    x2, message = run_forward_step(3, 4, exchange(message), pend, [x1], [far, last])
+    got = exchange(message)
+    pend, (y1, y2), (near, far, last) = run_forward_rest(
+        (1, 2), [x1, x2], pend, panels, inv_diag, ((4, 3), (5, 3), (5, 4))
+    )
+    x3, message = run_forward_step(4, 4, got, pend, [], [near])
+    x4, message = run_forward_step(5, 4, exchange(message), pend, [x3], [far, last])
+    got = exchange(message)
+    _, (y3, y4), (block,) = run_forward_rest((3, 4), [x3, x4], pend, panels, inv_diag, ((5, 5),))
+    message = run_forward_last(got, [y0, y1, y2, y3, y4], block)
+    y, message = run_backward_start(exchange(message, "leaf"), block)
+    got = exchange(message)
+    pend, (near, far, last) = run_backward_diag(y, panels, inv_diag, ((5, 4), (5, 3), (4, 3)))
+    s5, message = run_backward_step(4, got, pend, [], [near])
+    s4, message = run_backward_step(3, exchange(message), pend, [s5], [far, last])
+    got = exchange(message)
+    pend, (near, far, last) = run_backward_rest((5, 4), [s5, s4], pend, panels, ((3, 2), (3, 1), (2, 1)))
+    s3, message = run_backward_step(2, got, pend, [], [near])
+    s2, message = run_backward_step(1, exchange(message), pend, [s3], [far, last])
+    got = exchange(message)
+    pend, (block,) = run_backward_rest((3, 2), [s3, s2], pend, panels, ((1, 0),))
+    s1, message = run_backward_step(0, got, pend, [], [block])
+    got = exchange(message)
+    xs = [s1, s2, s3, s4, s5]
+    rows, message = run_own_finish(place, got, xs, index)
     got = exchange(message)
     leaf_x = run_leaf_backward(live_rows, got, table, rank, leaf_y, leaf_inv, update_blocks)
-    sep_solution = levels.reshape(LEVELS, V, 4, 1, 32).transpose(1, 0, 2, 3, 4)
+    sep_solution = rows.reshape(V, LEVELS, 4, 1, 32)
     return leaf_x, sep_solution
 
 

time: 257 us -> 250 us (0.973)
  blocking collectives: 22.8 us -> 110 us
  waiting for transfers between devices: 113 us -> 56.7 us
  starting transfers between devices: 66.6 us -> 39.2 us
  Pallas kernels: 49.2 us -> 39.3 us
    all_to_all x2 -> x8, blocking collectives: 22.8 us -> 110 us  [exchange(): return lax.all_to_all(message, axis, 0, 0, tiled=True)]
    all_to_all x13 -> x7, waiting for transfers between devices: 113 us -> 56.7 us  [exchange(): return lax.all_to_all(message, axis, 0, 0, tiled=True)]
    all_to_all x13 -> x7, starting transfers between devices: 66.6 us -> 39.2 us  [exchange(): return lax.all_to_all(message, axis, 0, 0, tiled=True)]
    pallas_call x22 -> x18, Pallas kernels: 34.1 us -> 26.6 us  [the longest x3 9.52 us: run_forward_rest(): call(functools.partial(forward_rest, levels, wanted), (sds((LEVELS, V, 12...]
  transfers between devices with their start and end apart: 13 -> 7, of which waited for: 13 -> 7; matrix products, arithmetic and copies ran while one was open for 1% -> 1% of each run, Pallas kernels for 9% -> 7%
where the time goes in v3:
time: 250 us
  blocking collectives  110 us (44%)
  waiting for transfers between devices  56.7 us (23%)
  Pallas kernels  39.3 us (16%)
  starting transfers between devices  39.2 us (16%)
    all_to_all x8, blocking collectives, exchange(): return lax.all_to_all(message, axis, 0, 0, tiled=True)  110 us
    all_to_all x7, waiting for transfers between devices, exchange(): return lax.all_to_all(message, axis, 0, 0, tiled=True)  56.7 us
    all_to_all x7, starting transfers between devices, exchange(): return lax.all_to_all(message, axis, 0, 0, tiled=True)  39.2 us
    pallas_call x3, Pallas kernels, run_forward_rest(): call(functools.partial(forward_rest, levels, wanted), (sds((LEVELS, V, 12...  9.52 us
    pallas_call x1, Pallas kernels, run_leaf_forward(): call(leaf_forward, (sds((V, UPD)), sds((512, 128)), sds((256, UPD), BF16)...  5.71 us
  transfers between devices with their start and end apart: 7, of which 7 were waited for; matrix products, arithmetic and copies ran while one was open for 1% of the time, Pallas kernels for 7%

profile of v3, /device:TPU:1, one launch (start us, length us, event | category | flops | bytes accessed | tf_op | source)
XLA Modules:
  0.0 249.5 jit_solution(818994547354679988)
XLA Ops:
  1.3 5.7 %shard_map.95 = (f32[16,1024]{1,0:T(8,128)}, f32[512,128]{1,0:T(8,128)}, bf16[256,1024]{1,0:T(8,128)(2,1)}, s32[8,1024]{1,0:T(8,128)}) custom-call(s32[1]{0:T(128)S(6)} %copy.11.live_ref, f32[1,16,1024]{2,1,0:T(8,128)} %rhs_hbm.1, s32[1,1024]{1,0:T(1,128)} %map_hbm.1, f32[1,1024,1024]{2,1,0:T(8,128)} %inv_ref.3, f32[1,1024,1024]{2,1,0:T(8,128)} %upd_ref.3), custom_call_target="tpu_custom_call" | custom-call | flops 201326592 | bytes 8388608 | tf_op jit(solution)/shard_map/pallas_call | solution.py:142
  7.0 11.5 %all-to-all-start = ((f32[128,4,128]{2,1,0:T(4,128)}), f32[128,4,128]{2,1,0:T(4,128)S(1)}, u32[]{:S(2)}, u32[]{:S(2)}) async-start(f32[128,4,128]{2,1,0:T(4,128)} %bitcast.57), calls=%async_computation | async-start | bytes 524288 | tf_op jit(solution)/shard_map/all_to_all | solution.py:524
  19.0 1.2 reduce.3
  22.4 7.0 %all-to-all-done = f32[128,4,128]{2,1,0:T(4,128)S(1)} async-done(((f32[128,4,128]{2,1,0:T(4,128)}), f32[128,4,128]{2,1,0:T(4,128)S(1)}, u32[]{:S(2)}, u32[]{:S(2)}) %all-to-all-start) | async-done | bytes 262176 | tf_op jit(solution)/shard_map/all_to_all | solution.py:524
  30.1 11.7 %all_to_all.165 = f32[32,4,128]{2,1,0:T(4,128)S(1)} all-to-all(f32[32,4,128]{2,1,0:T(4,128)S(1)} %bitcast.56), channel_id=1, replica_groups=mesh['leaf'=4,'sep'=32] {'sep'}, dimensions={0} | all-to-all | bytes 131072 | tf_op jit(solution)/shard_map/all_to_all | solution.py:524
  42.9 3.8 %all-to-all-start.2 = ((f32[128,4,128]{2,1,0:T(4,128)}), f32[128,4,128]{2,1,0:T(4,128)S(1)}, u32[]{:S(2)}, u32[]{:S(2)}) async-start(f32[128,4,128]{2,1,0:T(4,128)} %bitcast.5), calls=%async_computation.2 | async-start | bytes 524288 | tf_op jit(solution)/shard_map/all_to_all | solution.py:524
  46.8 3.3 %shard_map.99 = (f32[6,16,128]{2,1,0:T(8,128)S(1)}, f32[16,128]{1,0:T(8,128)S(1)}, bf16[256,1024]{1,0:T(8,128)(2,1)S(1)}, bf16[256,1024]{1,0:T(8,128)(2,1)S(1)}, bf16[256,1024]{1,0:T(8,128)(2,1)S(1)}) custom-call(f32[16,1024]{1,0:T(8,128)S(1)} %get-tuple-element.62.refs_0_, f32[6,16,128]{2,1,0:T(8,128)S(1)} %get-tuple-element.60.refs_1_, ...), custom_call_target="tpu_custom_call" | custom-call | flops 134217728 | bytes 4194304 | tf_op jit(solution)/shard_map/pallas_call | solution.py:334
  50.0 7.8 %all-to-all-done.2 = f32[128,4,128]{2,1,0:T(4,128)S(1)} async-done(((f32[128,4,128]{2,1,0:T(4,128)}), f32[128,4,128]{2,1,0:T(4,128)S(1)}, u32[]{:S(2)}, u32[]{:S(2)}) %all-to-all-start.2) | async-done | bytes 262176 | tf_op jit(solution)/shard_map/all_to_all | solution.py:524
  58.2 15.3 %all_to_all.166 = f32[128,4,128]{2,1,0:T(4,128)S(1)} all-to-all(f32[128,4,128]{2,1,0:T(4,128)S(1)} %bitcast.51), channel_id=1, replica_groups=mesh['leaf'=4,'sep'=32] {'leaf','sep'}, dimensions={0} | all-to-all | bytes 524288 | tf_op jit(solution)/shard_map/all_to_all | solution.py:524
  74.6 4.5 %all-to-all-start.4 = ((f32[128,4,128]{2,1,0:T(4,128)}), f32[128,4,128]{2,1,0:T(4,128)S(1)}, u32[]{:S(2)}, u32[]{:S(2)}) async-start(f32[128,4,128]{2,1,0:T(4,128)} %bitcast.9), calls=%async_computation.4 | async-start | bytes 524288 | tf_op jit(solution)/shard_map/all_to_all | solution.py:524
  79.1 3.8 %shard_map.102 = (f32[6,16,128]{2,1,0:T(8,128)S(1)}, f32[16,128]{1,0:T(8,128)S(1)}, f32[16,128]{1,0:T(8,128)S(1)}, bf16[256,1024]{1,0:T(8,128)(2,1)S(1)}, bf16[2...) custom-call(f32[16,1024]{1,0:T(8,128)S(1)} %get-tuple-element.66.refs_2_.refs_0_, ...), custom_call_target="tpu_custom_call" | custom-call | flops 150994944 | bytes 4718592 | tf_op jit(solution)/shard_map/pallas_call | solution.py:334
  82.9 7.2 %all-to-all-done.4 = f32[128,4,128]{2,1,0:T(4,128)S(1)} async-done(((f32[128,4,128]{2,1,0:T(4,128)}), f32[128,4,128]{2,1,0:T(4,128)S(1)}, u32[]{:S(2)}, u32[]{:S(2)}) %all-to-all-start.4) | async-done | bytes 262176 | tf_op jit(solution)/shard_map/all_to_all | solution.py:524
  90.5 15.3 %all_to_all.167 = f32[128,4,128]{2,1,0:T(4,128)S(1)} all-to-all(f32[128,4,128]{2,1,0:T(4,128)S(1)} %bitcast.52), channel_id=1, replica_groups=mesh['leaf'=4,'sep'=32] {'leaf','sep'}, dimensions={0} | all-to-all | bytes 524288 | tf_op jit(solution)/shard_map/all_to_all | solution.py:524
  107.0 4.7 %all-to-all-start.6 = ((f32[128,4,128]{2,1,0:T(4,128)}), f32[128,4,128]{2,1,0:T(4,128)S(1)}, u32[]{:S(2)}, u32[]{:S(2)}) async-start(f32[128,4,128]{2,1,0:T(4,128)} %bitcast.13), calls=%async_computation.6 | async-start | bytes 524288 | tf_op jit(solution)/shard_map/all_to_all | solution.py:524
  111.7 2.5 shard_map.105
  114.2 8.5 %all-to-all-done.6 = f32[128,4,128]{2,1,0:T(4,128)S(1)} async-done(((f32[128,4,128]{2,1,0:T(4,128)}), f32[128,4,128]{2,1,0:T(4,128)S(1)}, u32[]{:S(2)}, u32[]{:S(2)}) %all-to-all-start.6) | async-done | bytes 262176 | tf_op jit(solution)/shard_map/all_to_all | solution.py:524
  123.0 7.5 %all_to_all.168 = f32[4,96,128]{2,1,0:T(8,128)S(1)} all-to-all(f32[4,96,128]{2,1,0:T(8,128)S(1)} %bitcast.46), channel_id=1, replica_groups=mesh['leaf'=4,'sep'=32] {'leaf'}, dimensions={0} | all-to-all | bytes 393216 | tf_op jit(solution)/shard_map/all_to_all | solution.py:524
  131.5 5.8 %all-to-all-start.8 = ((f32[128,4,128]{2,1,0:T(4,128)}), f32[128,4,128]{2,1,0:T(4,128)S(1)}, u32[]{:S(2)}, u32[]{:S(2)}) async-start(f32[128,4,128]{2,1,0:T(4,128)} %bitcast.17), calls=%async_computation.8 | async-start | bytes 524288 | tf_op jit(solution)/shard_map/all_to_all | solution.py:524
  137.3 2.4 shard_map.108
  139.7 8.5 %all-to-all-done.8 = f32[128,4,128]{2,1,0:T(4,128)S(1)} async-done(((f32[128,4,128]{2,1,0:T(4,128)}), f32[128,4,128]{2,1,0:T(4,128)S(1)}, u32[]{:S(2)}, u32[]{:S(2)}) %all-to-all-start.8) | async-done | bytes 262176 | tf_op jit(solution)/shard_map/all_to_all | solution.py:524
  148.6 15.3 %all_to_all.169 = f32[128,4,128]{2,1,0:T(4,128)S(1)} all-to-all(f32[128,4,128]{2,1,0:T(4,128)S(1)} %bitcast.53), channel_id=1, replica_groups=mesh['leaf'=4,'sep'=32] {'leaf','sep'}, dimensions={0} | all-to-all | bytes 524288 | tf_op jit(solution)/shard_map/all_to_all | solution.py:524
  164.9 4.5 %all-to-all-start.10 = ((f32[128,4,128]{2,1,0:T(4,128)}), f32[128,4,128]{2,1,0:T(4,128)S(1)}, u32[]{:S(2)}, u32[]{:S(2)}) async-start(f32[128,4,128]{2,1,0:T(4,128)} %bitcast.21), calls=%async_computation.10 | async-start | bytes 524288 | tf_op jit(solution)/shard_map/all_to_all | solution.py:524
  169.4 2.6 %shard_map.111 = (f32[3,16,1024]{2,1,0:T(8,128)S(1)}, bf16[256,1024]{1,0:T(8,128)(2,1)S(1)}, bf16[256,1024]{1,0:T(8,128)(2,1)S(1)}, bf16[256,1024]{1,0:T(8,128)(2,1)S(1)}) custom-call(f32[16,128]{1,0:T(8,128)S(1)} %get-tuple-element.90.refs_2_.refs_0_.x5, f32[16,128]{1,0:T(8,128)S(1)} %get-tuple-element.94.refs_1_.x4, ...), custom_call_target="tpu_custom_call" | custom-call | flops 150994944 | bytes 4718592 | tf_op jit(solution)/shard_map/pallas_call | solution.py:474
  172.1 8.4 %all-to-all-done.10 = f32[128,4,128]{2,1,0:T(4,128)S(1)} async-done(((f32[128,4,128]{2,1,0:T(4,128)}), f32[128,4,128]{2,1,0:T(4,128)S(1)}, u32[]{:S(2)}, u32[]{:S(2)}) %all-to-all-start.10) | async-done | bytes 262176 | tf_op jit(solution)/shard_map/all_to_all | solution.py:524
  180.8 15.3 %all_to_all.170 = f32[128,4,128]{2,1,0:T(4,128)S(1)} all-to-all(f32[128,4,128]{2,1,0:T(4,128)S(1)} %bitcast.54), channel_id=1, replica_groups=mesh['leaf'=4,'sep'=32] {'leaf','sep'}, dimensions={0} | all-to-all | bytes 524288 | tf_op jit(solution)/shard_map/all_to_all | solution.py:524
  197.2 4.5 %all-to-all-start.12 = ((f32[128,4,128]{2,1,0:T(4,128)}), f32[128,4,128]{2,1,0:T(4,128)S(1)}, u32[]{:S(2)}, u32[]{:S(2)}) async-start(f32[128,4,128]{2,1,0:T(4,128)} %bitcast.25), calls=%async_computation.12 | async-start | bytes 524288 | tf_op jit(solution)/shard_map/all_to_all | solution.py:524
  201.7 1.6 shard_map.114
  203.3 9.3 %all-to-all-done.12 = f32[128,4,128]{2,1,0:T(4,128)S(1)} async-done(((f32[128,4,128]{2,1,0:T(4,128)}), f32[128,4,128]{2,1,0:T(4,128)S(1)}, u32[]{:S(2)}, u32[]{:S(2)}) %all-to-all-start.12) | async-done | bytes 262176 | tf_op jit(solution)/shard_map/all_to_all | solution.py:524
  213.0 15.3 %all_to_all.171 = f32[128,4,128]{2,1,0:T(4,128)S(1)} all-to-all(f32[128,4,128]{2,1,0:T(4,128)S(1)} %bitcast.50), channel_id=1, replica_groups=mesh['leaf'=4,'sep'=32] {'leaf','sep'}, dimensions={0} | all-to-all | bytes 524288 | tf_op jit(solution)/shard_map/all_to_all | solution.py:524
  228.3 1.8 shard_map.116
  230.1 14.3 %all_to_all.172 = f32[128,2,128]{2,1,0:T(2,128)S(1)} all-to-all(f32[128,2,128]{2,1,0:T(2,128)S(1)} %bitcast.55), channel_id=1, replica_groups=mesh['leaf'=4,'sep'=32] {'leaf','sep'}, dimensions={0} | all-to-all | bytes 262144 | tf_op jit(solution)/shard_map/all_to_all | solution.py:524
  244.4 5.0 %shard_map.117 = f32[1,16,1024]{2,1,0:T(8,128)} custom-call(s32[1]{0:T(128)S(6)} %copy.11.live_ref, f32[256,128]{1,0:T(8,128)S(1)} %bitcast.47, bf16[256,1024]{1,0:T(8,128)(2,1)S(1)} %copy-done, s32[8,1024]{1,0:T(8,128)S(1)} %copy-done.3, f32[16,1024]{1,0:T(8,128)S(1)} %copy-done.2, f32[1,1024,1024]{2,1,0:T(8,128)} %inv_ref.3, f32[1,1024,1024]{2,1,0:T(8,128)} %upd_ref.3), custom_call_target="tpu_custom_call" | custom-call | flops 201326592 | bytes 8388608 | tf_op jit(solution)/shard_map/pallas_call | solution.py:186
  (26 shorter events, 12.1 us)
Async XLA Ops:
  1.3 17.8 %copy-start.4 = (f32[16,6,4,1,32]{4,3,2,1,0:T(1,128)S(1)}, f32[16,6,4,1,32]{4,3,2,1,0:T(1,128)}, u32[]{:S(2)}) copy-start(f32[16,6,4,1,32]{4,3,2,1,0:T(1,128)} %param.13) | copy-start | bytes 147460
  7.0 22.4 %all-to-all-start = ((f32[128,4,128]{2,1,0:T(4,128)}), f32[128,4,128]{2,1,0:T(4,128)S(1)}, u32[]{:S(2)}, u32[]{:S(2)}) async-start(f32[128,4,128]{2,1,0:T(4,128)} %bitcast.57), calls=%async_computation | async-start | bytes 524288 | tf_op jit(solution)/shard_map/all_to_all | solution.py:524
  20.4 0.8 copy-start.1
  42.9 14.8 %all-to-all-start.2 = ((f32[128,4,128]{2,1,0:T(4,128)}), f32[128,4,128]{2,1,0:T(4,128)S(1)}, u32[]{:S(2)}, u32[]{:S(2)}) async-start(f32[128,4,128]{2,1,0:T(4,128)} %bitcast.5), calls=%async_computation.2 | async-start | bytes 524288 | tf_op jit(solution)/shard_map/all_to_all | solution.py:524
  74.6 15.5 %all-to-all-start.4 = ((f32[128,4,128]{2,1,0:T(4,128)}), f32[128,4,128]{2,1,0:T(4,128)S(1)}, u32[]{:S(2)}, u32[]{:S(2)}) async-start(f32[128,4,128]{2,1,0:T(4,128)} %bitcast.9), calls=%async_computation.4 | async-start | bytes 524288 | tf_op jit(solution)/shard_map/all_to_all | solution.py:524
  107.0 15.7 %all-to-all-start.6 = ((f32[128,4,128]{2,1,0:T(4,128)}), f32[128,4,128]{2,1,0:T(4,128)S(1)}, u32[]{:S(2)}, u32[]{:S(2)}) async-start(f32[128,4,128]{2,1,0:T(4,128)} %bitcast.13), calls=%async_computation.6 | async-start | bytes 524288 | tf_op jit(solution)/shard_map/all_to_all | solution.py:524
  131.5 16.7 %all-to-all-start.8 = ((f32[128,4,128]{2,1,0:T(4,128)}), f32[128,4,128]{2,1,0:T(4,128)S(1)}, u32[]{:S(2)}, u32[]{:S(2)}) async-start(f32[128,4,128]{2,1,0:T(4,128)} %bitcast.17), calls=%async_computation.8 | async-start | bytes 524288 | tf_op jit(solution)/shard_map/all_to_all | solution.py:524
  164.9 15.5 %all-to-all-start.10 = ((f32[128,4,128]{2,1,0:T(4,128)}), f32[128,4,128]{2,1,0:T(4,128)S(1)}, u32[]{:S(2)}, u32[]{:S(2)}) async-start(f32[128,4,128]{2,1,0:T(4,128)} %bitcast.21), calls=%async_computation.10 | async-start | bytes 524288 | tf_op jit(solution)/shard_map/all_to_all | solution.py:524
  197.2 15.5 %all-to-all-start.12 = ((f32[128,4,128]{2,1,0:T(4,128)}), f32[128,4,128]{2,1,0:T(4,128)S(1)}, u32[]{:S(2)}, u32[]{:S(2)}) async-start(f32[128,4,128]{2,1,0:T(4,128)} %bitcast.25), calls=%async_computation.12 | async-start | bytes 524288 | tf_op jit(solution)/shard_map/all_to_all | solution.py:524
  201.7 42.7 %copy-start = (bf16[256,1024]{1,0:T(8,128)(2,1)S(1)}, bf16[256,1024]{1,0:T(8,128)(2,1)}, u32[]{:S(2)}) copy-start(bf16[256,1024]{1,0:T(8,128)(2,1)} %get-tuple-element.109.t_ref) | copy-start | bytes 1572868
  201.7 42.7 %copy-start.2 = (f32[16,1024]{1,0:T(8,128)S(1)}, f32[16,1024]{1,0:T(8,128)}, u32[]{:S(2)}) copy-start(f32[16,1024]{1,0:T(8,128)} %get-tuple-element.58.after_ref.y_ref) | copy-start | bytes 196612
  201.7 42.7 %copy-start.3 = (s32[8,1024]{1,0:T(8,128)S(1)}, s32[8,1024]{1,0:T(8,128)}, u32[]{:S(2)}) copy-start(s32[8,1024]{1,0:T(8,128)} %get-tuple-element.110.rank_ref) | copy-start | bytes 98308

commit v4 on v3

--- a/solution.py
+++ b/solution.py
@@ -269,15 +269,28 @@
     return diag_ref.at[lower, :, 0] if upper == lower else panels_ref.at[pair_index(upper, lower), :, 0]
 
 
-def first_block(after_ref, panels_ref, w_ref, buffer, sems):
-    fetch([panels_ref.at[pair_index(1, 0), :, 0]], buffer, sems)[0].wait()
-    w_ref[...] = block_parts(buffer[0])
-
-
-def run_first_block(after, panels):
-    return call(first_block, sds(PARTS, BF16), [ANY, HBM], VM, scratch=buffers(1), flops=1 << 20, nbytes=1 << 20)(
-        after, panels
-    )
+FIRST = ((1, 0), (2, 0), (2, 1))
+
+
+def first_blocks(after_ref, panels_ref, *refs):
+    w_refs, (buffer, sems) = refs[:-2], refs[-2:]
+    copies = fetch([block_of(panels_ref, None, *pair) for pair in FIRST], buffer, sems)
+    for n, w_ref in enumerate(w_refs):
+        copies[n].wait()
+        w_ref[...] = block_parts(buffer[n])
+
+
+def run_first_blocks(after, panels):
+    n = len(FIRST)
+    return call(
+        first_blocks,
+        [sds(PARTS, BF16)] * n,
+        [ANY, HBM],
+        [VM] * n,
+        scratch=buffers(n),
+        flops=n << 20,
+        nbytes=n << 20,
+    )(after, panels)
 
 
 def forward_step(level, parts, count, *refs):
@@ -343,24 +356,25 @@
     return out[0], out[1 : 1 + n], out[1 + n :]
 
 
-def forward_last(got_ref, y0, y1, y2, y3, y4, w_ref, msg_ref):
-    x = columns_of(got_ref, 4)
-    last = times_columns(x, w_ref[...])
+def forward_last(got_ref, y0, y1, y2, y3, x4_ref, w4_ref, w5_ref, msg_ref):
+    y4 = times_columns(x4_ref[...], w4_ref[...])
+    y5 = times_columns(columns_of(got_ref, 4), w5_ref[...])
     for l in range(4):
-        for k, one in enumerate((y0, y1, y2, y3, y4)):
+        for k, one in enumerate((y0, y1, y2, y3)):
             msg_ref[pl.ds(96 * l + 16 * k, 16), :] = one[...]
-        msg_ref[pl.ds(96 * l + 80, 16), :] = last
-
-
-def run_forward_last(got, ys, w):
+        msg_ref[pl.ds(96 * l + 64, 16), :] = y4
+        msg_ref[pl.ds(96 * l + 80, 16), :] = y5
+
+
+def run_forward_last(got, ys, x4, w4, w5):
     return call(
         forward_last,
         sds((4 * 96, 128)),
-        [VM] + [VM] * 5 + [VM],
+        [VM] * 8,
         VM,
-        flops=1 << 24,
+        flops=2 << 24,
         nbytes=1 << 20,
-    )(got, *ys, w)
+    )(got, *ys, x4, w4, w5)
 
 
 def column_message(msg_ref, columns):
@@ -387,32 +401,6 @@
         flops=1 << 24,
         nbytes=1 << 20,
     )(got, w)
-
-
-def backward_diag(wanted, y_ref, panels_ref, diag_ref, out_ref, *refs):
-    w_refs, (buffer, sems) = refs[:-2], refs[-2:]
-    count = LEVELS - 1
-    pairs = [(k, k) for k in range(count)] + list(wanted)
-    copies = fetch([block_of(panels_ref, diag_ref, *pair) for pair in pairs], buffer, sems)
-    for k in range(count):
-        copies[k].wait()
-        out_ref[k] = times_rows(y_ref[pl.ds(16 * k, 16), :], block_parts(buffer[k]))
-    for n, w_ref in enumerate(w_refs):
-        copies[count + n].wait()
-        w_ref[...] = block_parts(buffer[count + n])
-
-
-def run_backward_diag(y, panels, diag, wanted):
-    out = call(
-        functools.partial(backward_diag, wanted),
-        (sds((LEVELS - 1, V, COLS)), *[sds(PARTS, BF16)] * len(wanted)),
-        [VM, HBM, HBM],
-        (VM,) * (1 + len(wanted)),
-        scratch=buffers(LEVELS - 1 + len(wanted)),
-        flops=8 << 24,
-        nbytes=4 << 20,
-    )(y, panels, diag)
-    return out[0], out[1:]
 
 
 def rows_of(got_ref):
@@ -445,6 +433,51 @@
         flops=len(blocks) << 24,
         nbytes=len(blocks) << 20,
     )(got, pend, *earlier, *blocks)
+
+
+def backward_next(got_ref, y_ref, diag_ref, w_ref, x_ref, msg_ref):
+    x = rows_of(got_ref)
+    x_ref[...] = x
+    column_message(msg_ref, times_rows(y_ref[64:80, :], diag_ref[...]) - times_rows(x, w_ref[...]))
+
+
+def run_backward_next(got, y, diag, w):
+    return call(
+        backward_next,
+        (sds((V, 128)), sds((512, 128))),
+        [VM] * 4,
+        (VM, VM),
+        flops=2 << 24,
+        nbytes=1 << 20,
+    )(got, y, diag, w)
+
+
+def backward_diag(wanted, y_ref, x_ref, panels_ref, diag_ref, out_ref, *refs):
+    w_refs, (buffer, sems) = refs[:-2], refs[-2:]
+    pairs = [(up, k) for k in range(LEVELS - 2) for up in (k, LEVELS - 1)] + list(wanted)
+    copies = fetch([block_of(panels_ref, diag_ref, *pair) for pair in pairs], buffer, sems)
+    for k in range(LEVELS - 2):
+        copies[2 * k].wait()
+        columns = times_rows(y_ref[pl.ds(16 * k, 16), :], block_parts(buffer[2 * k]))
+        copies[2 * k + 1].wait()
+        out_ref[k] = columns - times_rows(x_ref[...], block_parts(buffer[2 * k + 1]))
+    for n, w_ref in enumerate(w_refs):
+        slot = 2 * (LEVELS - 2) + n
+        copies[slot].wait()
+        w_ref[...] = block_parts(buffer[slot])
+
+
+def run_backward_diag(y, x, panels, diag, wanted):
+    out = call(
+        functools.partial(backward_diag, wanted),
+        (sds((LEVELS - 2, V, COLS)), *[sds(PARTS, BF16)] * len(wanted)),
+        [VM, VM, HBM, HBM],
+        (VM,) * (1 + len(wanted)),
+        scratch=buffers(2 * (LEVELS - 2) + len(wanted)),
+        flops=11 << 24,
+        nbytes=6 << 20,
+    )(y, x, panels, diag)
+    return out[0], out[1:]
 
 
 def backward_rest(levels, wanted, *refs):
@@ -495,18 +528,19 @@
         mine.append(one)
     rows = jnp.concatenate(mine + [jnp.zeros((V, 64), F32)], 1)
     high, low = split(jnp.concatenate([rows] * 8, 0))
-    table = jnp.concatenate([high, low], 0)
+    table = jnp.concatenate([high, low], 0).astype(F32)
     index = index_ref[...]
     column = (iota((128, 256), 1) + 1).astype(F32)
-    group = iota((128, 128), 1) >> 4
+    group = (iota((256, 256), 0) >> 4) & 7
+    hot, tables = [], []
+    for g in range(8):
+        pair = [jnp.where(index[:, j : j + 1] == column, 1.0, 0.0) for j in (g, 8 + g)]
+        hot.append(jnp.concatenate(pair, 0).astype(BF16))
+        tables.append(jnp.where(group == g, table, 0.0).astype(BF16))
+    got = dot(jnp.concatenate(hot, 1), jnp.concatenate(tables, 1), NT)
     for half in range(2):
-        out = jnp.zeros((128, 128), F32)
-        for g in range(8):
-            j = 8 * half + g
-            hot = jnp.where(index[:, j : j + 1] == column, 1.0, 0.0).astype(BF16)
-            got = dot(hot, table, NT)
-            out = jnp.where(group == g, got[:, :128] + got[:, 128:], out)
-        msg_ref[pl.ds(half, 128, 2), :] = out
+        part = got[128 * half : 128 * half + 128]
+        msg_ref[pl.ds(half, 128, 2), :] = part[:, :128] + part[:, 128:]
 
 
 def run_own_finish(place, got, xs, index):
@@ -529,35 +563,33 @@
     rhs = sep_rhs.reshape(V, LEVELS * 128)
     leaf_y, message, table, rank = run_leaf_forward(live_rows, leaf_rhs, row_map, leaf_inv, update_blocks)
     got = exchange(message)
-    block = run_first_block(leaf_y, panels)
-    pend, message, index = run_own_start(place, got, rhs, block)
+    first, far, near = run_first_blocks(leaf_y, panels)
+    pend, message, index = run_own_start(place, got, rhs, near)
     got = exchange(message, "sep")
-    x0, message = run_forward_step(1, 1, got, pend, [], [block])
+    x0, message = run_forward_step(1, 1, got, pend, [], [first])
+    x1, message = run_forward_step(2, 4, exchange(message), pend, [x0], [far, near])
     got = exchange(message)
-    pend, (y0,), (near, far, last) = run_forward_rest((0,), [x0], pend, panels, inv_diag, ((2, 1), (3, 1), (3, 2)))
-    x1, message = run_forward_step(2, 4, got, pend, [], [near])
-    x2, message = run_forward_step(3, 4, exchange(message), pend, [x1], [far, last])
+    pend, (y0, y1), (first, far, near) = run_forward_rest(
+        (0, 1), [x0, x1], pend, panels, inv_diag, ((3, 2), (4, 2), (4, 3))
+    )
+    x2, message = run_forward_step(3, 4, got, pend, [], [first])
+    x3, message = run_forward_step(4, 4, exchange(message), pend, [x2], [far, near])
     got = exchange(message)
-    pend, (y1, y2), (near, far, last) = run_forward_rest(
-        (1, 2), [x1, x2], pend, panels, inv_diag, ((4, 3), (5, 3), (5, 4))
+    pend, (y2, y3), (first, d4, d5) = run_forward_rest(
+        (2, 3), [x2, x3], pend, panels, inv_diag, ((5, 4), (4, 4), (5, 5))
     )
-    x3, message = run_forward_step(4, 4, got, pend, [], [near])
-    x4, message = run_forward_step(5, 4, exchange(message), pend, [x3], [far, last])
+    x4, message = run_forward_step(5, 4, got, pend, [], [first])
+    message = run_forward_last(exchange(message), [y0, y1, y2, y3], x4, d4, d5)
+    y, message = run_backward_start(exchange(message, "leaf"), d5)
+    s5, message = run_backward_next(exchange(message), y, d4, first)
     got = exchange(message)
-    _, (y3, y4), (block,) = run_forward_rest((3, 4), [x3, x4], pend, panels, inv_diag, ((5, 5),))
-    message = run_forward_last(got, [y0, y1, y2, y3, y4], block)
-    y, message = run_backward_start(exchange(message, "leaf"), block)
+    pend, (first, far, near) = run_backward_diag(y, s5, panels, inv_diag, ((4, 3), (4, 2), (3, 2)))
+    s4, message = run_backward_step(3, got, pend, [], [first])
+    s3, message = run_backward_step(2, exchange(message), pend, [s4], [far, near])
     got = exchange(message)
-    pend, (near, far, last) = run_backward_diag(y, panels, inv_diag, ((5, 4), (5, 3), (4, 3)))
-    s5, message = run_backward_step(4, got, pend, [], [near])
-    s4, message = run_backward_step(3, exchange(message), pend, [s5], [far, last])
-    got = exchange(message)
-    pend, (near, far, last) = run_backward_rest((5, 4), [s5, s4], pend, panels, ((3, 2), (3, 1), (2, 1)))
-    s3, message = run_backward_step(2, got, pend, [], [near])
-    s2, message = run_backward_step(1, exchange(message), pend, [s3], [far, last])
-    got = exchange(message)
-    pend, (block,) = run_backward_rest((3, 2), [s3, s2], pend, panels, ((1, 0),))
-    s1, message = run_backward_step(0, got, pend, [], [block])
+    pend, (first, far, near) = run_backward_rest((4, 3), [s4, s3], pend, panels, ((2, 1), (2, 0), (1, 0)))
+    s2, message = run_backward_step(1, got, pend, [], [first])
+    s1, message = run_backward_step(0, exchange(message), pend, [s2], [far, near])
     got = exchange(message)
     xs = [s1, s2, s3, s4, s5]
     rows, message = run_own_finish(place, got, xs, index)

time: 250 us -> 247 us (0.988)
  blocking collectives: 110 us -> 141 us
  waiting for transfers between devices: 56.7 us -> 37.8 us
  starting transfers between devices: 39.2 us -> 29.4 us
  Pallas kernels: 39.3 us -> 34.4 us
    all_to_all x8 -> x10, blocking collectives: 110 us -> 141 us  [exchange(): return lax.all_to_all(message, axis, 0, 0, tiled=True)]
    all_to_all x7 -> x5, waiting for transfers between devices: 56.7 us -> 37.8 us  [exchange(): return lax.all_to_all(message, axis, 0, 0, tiled=True)]
    all_to_all x7 -> x5, starting transfers between devices: 39.2 us -> 29.4 us  [exchange(): return lax.all_to_all(message, axis, 0, 0, tiled=True)]
    pallas_call x3 -> x4, Pallas kernels: 3.82 us -> 6 us  [the longest x1 3.04 us: run_backward_diag(): call(functools.partial(backward_diag, wanted), (sds((LEVELS - 2, V, COLS)...]
    pallas_call x3 -> x2, Pallas kernels: 9.52 us -> 7.56 us  [run_forward_rest(): call(functools.partial(forward_rest, levels, wanted), (sds((LEVELS, V, 12...]
  transfers between devices with their start and end apart: 7 -> 5, of which waited for: 7 -> 5; matrix products, arithmetic and copies ran while one was open for 1% -> 1% of each run, Pallas kernels for 7% -> 6%
where the time goes in v4:
time: 247 us
  blocking collectives  141 us (57%)
  waiting for transfers between devices  37.8 us (15%)
  Pallas kernels  34.4 us (14%)
  starting transfers between devices  29.4 us (12%)
    all_to_all x10, blocking collectives, exchange(): return lax.all_to_all(message, axis, 0, 0, tiled=True)  141 us
    all_to_all x5, waiting for transfers between devices, exchange(): return lax.all_to_all(message, axis, 0, 0, tiled=True)  37.8 us
    all_to_all x5, starting transfers between devices, exchange(): return lax.all_to_all(message, axis, 0, 0, tiled=True)  29.4 us
    pallas_call x2, Pallas kernels, run_forward_rest(): call(functools.partial(forward_rest, levels, wanted), (sds((LEVELS, V, 12...  7.56 us
    pallas_call x1, Pallas kernels, run_leaf_forward(): call(leaf_forward, (sds((V, UPD)), sds((512, 128)), sds((256, UPD), BF16)...  5.72 us
    pallas_call x1, Pallas kernels, run_leaf_backward(): call(leaf_backward, sds((1, V, 1024)), [SMEM, VM, VM, VM, VM, HBM, HBM],...  4.98 us
  transfers between devices with their start and end apart: 5, of which 5 were waited for; matrix products, arithmetic and copies ran while one was open for 1% of the time, Pallas kernels for 6%

profile of v4, /device:TPU:1, one launch (start us, length us, event | category | flops | bytes accessed | tf_op | source)
XLA Modules:
  0.0 246.7 jit_solution(2364359216828048539)
XLA Ops:
  1.3 5.7 %shard_map.95 = (f32[16,1024]{1,0:T(8,128)}, f32[512,128]{1,0:T(8,128)}, bf16[256,1024]{1,0:T(8,128)(2,1)}, s32[8,1024]{1,0:T(8,128)}) custom-call(s32[1]{0:T(128)S(6)} %copy.11.live_ref, f32[1,16,1024]{2,1,0:T(8,128)} %rhs_hbm.1, s32[1,1024]{1,0:T(1,128)} %map_hbm.1, f32[1,1024,1024]{2,1,0:T(8,128)} %inv_ref.3, f32[1,1024,1024]{2,1,0:T(8,128)} %upd_ref.3), custom_call_target="tpu_custom_call" | custom-call | flops 201326592 | bytes 8388608 | tf_op jit(solution)/shard_map/pallas_call | solution.py:142
  7.0 11.5 %all-to-all-start = ((f32[128,4,128]{2,1,0:T(4,128)}), f32[128,4,128]{2,1,0:T(4,128)S(1)}, u32[]{:S(2)}, u32[]{:S(2)}) async-start(f32[128,4,128]{2,1,0:T(4,128)} %bitcast.59), calls=%async_computation | async-start | bytes 524288 | tf_op jit(solution)/shard_map/all_to_all | solution.py:558
  19.1 1.2 reduce.3
  21.3 1.5 shard_map.96
  22.7 6.7 %all-to-all-done = f32[128,4,128]{2,1,0:T(4,128)S(1)} async-done(((f32[128,4,128]{2,1,0:T(4,128)}), f32[128,4,128]{2,1,0:T(4,128)S(1)}, u32[]{:S(2)}, u32[]{:S(2)}) %all-to-all-start) | async-done | bytes 262176 | tf_op jit(solution)/shard_map/all_to_all | solution.py:558
  30.2 11.7 %all_to_all.165 = f32[32,4,128]{2,1,0:T(4,128)S(1)} all-to-all(f32[32,4,128]{2,1,0:T(4,128)S(1)} %bitcast.58), channel_id=1, replica_groups=mesh['leaf'=4,'sep'=32] {'sep'}, dimensions={0} | all-to-all | bytes 131072 | tf_op jit(solution)/shard_map/all_to_all | solution.py:558
  42.3 14.4 %all_to_all.166 = f32[128,4,128]{2,1,0:T(4,128)S(1)} all-to-all(f32[128,4,128]{2,1,0:T(4,128)S(1)} %bitcast.51), channel_id=1, replica_groups=mesh['leaf'=4,'sep'=32] {'leaf','sep'}, dimensions={0} | all-to-all | bytes 524288 | tf_op jit(solution)/shard_map/all_to_all | solution.py:558
  56.7 1.2 shard_map.99
  57.9 4.5 %all-to-all-start.3 = ((f32[128,4,128]{2,1,0:T(4,128)}), f32[128,4,128]{2,1,0:T(4,128)S(1)}, u32[]{:S(2)}, u32[]{:S(2)}) async-start(f32[128,4,128]{2,1,0:T(4,128)} %bitcast.7), calls=%async_computation.3 | async-start | bytes 524288 | tf_op jit(solution)/shard_map/all_to_all | solution.py:558
  62.4 4.6 %shard_map.100 = (f32[6,16,128]{2,1,0:T(8,128)S(1)}, f32[16,128]{1,0:T(8,128)S(1)}, f32[16,128]{1,0:T(8,128)S(1)}, bf16[256,1024]{1,0:T(8,128)(2,1)S(1)}, bf16[2...) custom-call(f32[16,1024]{1,0:T(8,128)S(1)} %get-tuple-element.63.refs_2_.refs_0_, ...), custom_call_target="tpu_custom_call" | custom-call | flops 184549376 | bytes 5767168 | tf_op jit(solution)/shard_map/pallas_call | solution.py:347
  67.0 6.4 %all-to-all-done.3 = f32[128,4,128]{2,1,0:T(4,128)S(1)} async-done(((f32[128,4,128]{2,1,0:T(4,128)}), f32[128,4,128]{2,1,0:T(4,128)S(1)}, u32[]{:S(2)}, u32[]{:S(2)}) %all-to-all-start.3) | async-done | bytes 262176 | tf_op jit(solution)/shard_map/all_to_all | solution.py:558
  73.8 15.3 %all_to_all.167 = f32[128,4,128]{2,1,0:T(4,128)S(1)} all-to-all(f32[128,4,128]{2,1,0:T(4,128)S(1)} %bitcast.52), channel_id=1, replica_groups=mesh['leaf'=4,'sep'=32] {'leaf','sep'}, dimensions={0} | all-to-all | bytes 524288 | tf_op jit(solution)/shard_map/all_to_all | solution.py:558
  89.1 1.2 shard_map.102
  90.3 4.5 %all-to-all-start.5 = ((f32[128,4,128]{2,1,0:T(4,128)}), f32[128,4,128]{2,1,0:T(4,128)S(1)}, u32[]{:S(2)}, u32[]{:S(2)}) async-start(f32[128,4,128]{2,1,0:T(4,128)} %bitcast.11), calls=%async_computation.5 | async-start | bytes 524288 | tf_op jit(solution)/shard_map/all_to_all | solution.py:558
  94.8 3.0 %shard_map.103 = (f32[6,16,128]{2,1,0:T(8,128)S(1)}, f32[16,128]{1,0:T(8,128)S(1)}, f32[16,128]{1,0:T(8,128)S(1)}, bf16[256,1024]{1,0:T(8,128)(2,1)S(1)}, bf16[2...) custom-call(f32[16,1024]{1,0:T(8,128)S(1)} %get-tuple-element.70.refs_2_.refs_0_, ...), custom_call_target="tpu_custom_call" | custom-call | flops 117440512 | bytes 3670016 | tf_op jit(solution)/shard_map/pallas_call | solution.py:347
  97.7 8.0 %all-to-all-done.5 = f32[128,4,128]{2,1,0:T(4,128)S(1)} async-done(((f32[128,4,128]{2,1,0:T(4,128)}), f32[128,4,128]{2,1,0:T(4,128)S(1)}, u32[]{:S(2)}, u32[]{:S(2)}) %all-to-all-start.5) | async-done | bytes 262176 | tf_op jit(solution)/shard_map/all_to_all | solution.py:558
  106.2 15.3 %all_to_all.168 = f32[128,4,128]{2,1,0:T(4,128)S(1)} all-to-all(f32[128,4,128]{2,1,0:T(4,128)S(1)} %bitcast.53), channel_id=1, replica_groups=mesh['leaf'=4,'sep'=32] {'leaf','sep'}, dimensions={0} | all-to-all | bytes 524288 | tf_op jit(solution)/shard_map/all_to_all | solution.py:558
  121.8 7.6 %all_to_all.169 = f32[4,96,128]{2,1,0:T(8,128)S(1)} all-to-all(f32[4,96,128]{2,1,0:T(8,128)S(1)} %bitcast.45), channel_id=1, replica_groups=mesh['leaf'=4,'sep'=32] {'leaf'}, dimensions={0} | all-to-all | bytes 393216 | tf_op jit(solution)/shard_map/all_to_all | solution.py:558
  129.7 16.5 %all_to_all.170 = f32[128,4,128]{2,1,0:T(4,128)S(1)} all-to-all(f32[128,4,128]{2,1,0:T(4,128)S(1)} %bitcast.54), channel_id=1, replica_groups=mesh['leaf'=4,'sep'=32] {'leaf','sep'}, dimensions={0} | all-to-all | bytes 524288 | tf_op jit(solution)/shard_map/all_to_all | solution.py:558
  146.2 1.1 shard_map.107
  147.3 4.5 %all-to-all-start.9 = ((f32[128,4,128]{2,1,0:T(4,128)}), f32[128,4,128]{2,1,0:T(4,128)S(1)}, u32[]{:S(2)}, u32[]{:S(2)}) async-start(f32[128,4,128]{2,1,0:T(4,128)} %bitcast.19), calls=%async_computation.9 | async-start | bytes 524288 | tf_op jit(solution)/shard_map/all_to_all | solution.py:558
  151.8 3.0 %shard_map.108 = (f32[4,16,1024]{2,1,0:T(8,128)S(1)}, bf16[256,1024]{1,0:T(8,128)(2,1)S(1)}, bf16[256,1024]{1,0:T(8,128)(2,1)S(1)}, bf16[256,1024]{1,0:T(8,128)(2,1)S(1)}) custom-call(f32[96,128]{1,0:T(8,128)S(1)} %get-tuple-element.86.y_ref, f32[16,128]{1,0:T(8,128)S(1)} %get-tuple-element.88.x_ref.x5, f32[15,4,1,32,1024]{4,3,2,1,0:T(8,128)} %refs_3_.5, ...), custom_call_target="tpu_custom_call" | custom-call | flops 184549376 | bytes 6291456 | tf_op jit(solution)/shard_map/pallas_call | solution.py:471
  154.8 8.0 %all-to-all-done.9 = f32[128,4,128]{2,1,0:T(4,128)S(1)} async-done(((f32[128,4,128]{2,1,0:T(4,128)}), f32[128,4,128]{2,1,0:T(4,128)S(1)}, u32[]{:S(2)}, u32[]{:S(2)}) %all-to-all-start.9) | async-done | bytes 262176 | tf_op jit(solution)/shard_map/all_to_all | solution.py:558
  163.1 15.3 %all_to_all.171 = f32[128,4,128]{2,1,0:T(4,128)S(1)} all-to-all(f32[128,4,128]{2,1,0:T(4,128)S(1)} %bitcast.55), channel_id=1, replica_groups=mesh['leaf'=4,'sep'=32] {'leaf','sep'}, dimensions={0} | all-to-all | bytes 524288 | tf_op jit(solution)/shard_map/all_to_all | solution.py:558
  178.4 1.1 shard_map.110
  179.5 4.5 %all-to-all-start.11 = ((f32[128,4,128]{2,1,0:T(4,128)}), f32[128,4,128]{2,1,0:T(4,128)S(1)}, u32[]{:S(2)}, u32[]{:S(2)}) async-start(f32[128,4,128]{2,1,0:T(4,128)} %bitcast.23), calls=%async_computation.11 | async-start | bytes 524288 | tf_op jit(solution)/shard_map/all_to_all | solution.py:558
  184.0 2.3 shard_map.111
  186.3 8.7 %all-to-all-done.11 = f32[128,4,128]{2,1,0:T(4,128)S(1)} async-done(((f32[128,4,128]{2,1,0:T(4,128)}), f32[128,4,128]{2,1,0:T(4,128)S(1)}, u32[]{:S(2)}, u32[]{:S(2)}) %all-to-all-start.11) | async-done | bytes 262176 | tf_op jit(solution)/shard_map/all_to_all | solution.py:558
  195.4 15.3 %all_to_all.172 = f32[128,4,128]{2,1,0:T(4,128)S(1)} all-to-all(f32[128,4,128]{2,1,0:T(4,128)S(1)} %bitcast.56), channel_id=1, replica_groups=mesh['leaf'=4,'sep'=32] {'leaf','sep'}, dimensions={0} | all-to-all | bytes 524288 | tf_op jit(solution)/shard_map/all_to_all | solution.py:558
  211.0 15.2 %all_to_all.173 = f32[128,4,128]{2,1,0:T(4,128)S(1)} all-to-all(f32[128,4,128]{2,1,0:T(4,128)S(1)} %bitcast.50), channel_id=1, replica_groups=mesh['leaf'=4,'sep'=32] {'leaf','sep'}, dimensions={0} | all-to-all | bytes 524288 | tf_op jit(solution)/shard_map/all_to_all | solution.py:558
  227.3 14.3 %all_to_all.174 = f32[128,2,128]{2,1,0:T(2,128)S(1)} all-to-all(f32[128,2,128]{2,1,0:T(2,128)S(1)} %bitcast.57), channel_id=1, replica_groups=mesh['leaf'=4,'sep'=32] {'leaf','sep'}, dimensions={0} | all-to-all | bytes 262144 | tf_op jit(solution)/shard_map/all_to_all | solution.py:558
  241.6 5.0 %shard_map.115 = f32[1,16,1024]{2,1,0:T(8,128)} custom-call(s32[1]{0:T(128)S(6)} %copy.11.live_ref, f32[256,128]{1,0:T(8,128)S(1)} %bitcast.47, bf16[256,1024]{1,0:T(8,128)(2,1)S(1)} %copy-done, s32[8,1024]{1,0:T(8,128)S(1)} %copy-done.3, f32[16,1024]{1,0:T(8,128)S(1)} %copy-done.2, f32[1,1024,1024]{2,1,0:T(8,128)} %inv_ref.3, f32[1,1024,1024]{2,1,0:T(8,128)} %upd_ref.3), custom_call_target="tpu_custom_call" | custom-call | flops 201326592 | bytes 8388608 | tf_op jit(solution)/shard_map/pallas_call | solution.py:186
  (22 shorter events, 6.2 us)
Async XLA Ops:
  1.3 17.8 %copy-start.4 = (f32[16,6,4,1,32]{4,3,2,1,0:T(1,128)S(1)}, f32[16,6,4,1,32]{4,3,2,1,0:T(1,128)}, u32[]{:S(2)}) copy-start(f32[16,6,4,1,32]{4,3,2,1,0:T(1,128)} %param.13) | copy-start | bytes 147460
  7.0 22.4 %all-to-all-start = ((f32[128,4,128]{2,1,0:T(4,128)}), f32[128,4,128]{2,1,0:T(4,128)S(1)}, u32[]{:S(2)}, u32[]{:S(2)}) async-start(f32[128,4,128]{2,1,0:T(4,128)} %bitcast.59), calls=%async_computation | async-start | bytes 524288 | tf_op jit(solution)/shard_map/all_to_all | solution.py:558
  20.4 0.8 copy-start.1
  57.9 15.5 %all-to-all-start.3 = ((f32[128,4,128]{2,1,0:T(4,128)}), f32[128,4,128]{2,1,0:T(4,128)S(1)}, u32[]{:S(2)}, u32[]{:S(2)}) async-start(f32[128,4,128]{2,1,0:T(4,128)} %bitcast.7), calls=%async_computation.3 | async-start | bytes 524288 | tf_op jit(solution)/shard_map/all_to_all | solution.py:558
  90.3 15.5 %all-to-all-start.5 = ((f32[128,4,128]{2,1,0:T(4,128)}), f32[128,4,128]{2,1,0:T(4,128)S(1)}, u32[]{:S(2)}, u32[]{:S(2)}) async-start(f32[128,4,128]{2,1,0:T(4,128)} %bitcast.11), calls=%async_computation.5 | async-start | bytes 524288 | tf_op jit(solution)/shard_map/all_to_all | solution.py:558
  147.3 15.5 %all-to-all-start.9 = ((f32[128,4,128]{2,1,0:T(4,128)}), f32[128,4,128]{2,1,0:T(4,128)S(1)}, u32[]{:S(2)}, u32[]{:S(2)}) async-start(f32[128,4,128]{2,1,0:T(4,128)} %bitcast.19), calls=%async_computation.9 | async-start | bytes 524288 | tf_op jit(solution)/shard_map/all_to_all | solution.py:558
  179.5 15.5 %all-to-all-start.11 = ((f32[128,4,128]{2,1,0:T(4,128)}), f32[128,4,128]{2,1,0:T(4,128)S(1)}, u32[]{:S(2)}, u32[]{:S(2)}) async-start(f32[128,4,128]{2,1,0:T(4,128)} %bitcast.23), calls=%async_computation.11 | async-start | bytes 524288 | tf_op jit(solution)/shard_map/all_to_all | solution.py:558
  184.0 57.6 %copy-start = (bf16[256,1024]{1,0:T(8,128)(2,1)S(1)}, bf16[256,1024]{1,0:T(8,128)(2,1)}, u32[]{:S(2)}) copy-start(bf16[256,1024]{1,0:T(8,128)(2,1)} %get-tuple-element.107.t_ref) | copy-start | bytes 1572868
  184.0 57.6 %copy-start.2 = (f32[16,1024]{1,0:T(8,128)S(1)}, f32[16,1024]{1,0:T(8,128)}, u32[]{:S(2)}) copy-start(f32[16,1024]{1,0:T(8,128)} %get-tuple-element.57.after_ref.y_ref) | copy-start | bytes 196612
  184.0 57.6 %copy-start.3 = (s32[8,1024]{1,0:T(8,128)S(1)}, s32[8,1024]{1,0:T(8,128)}, u32[]{:S(2)}) copy-start(s32[8,1024]{1,0:T(8,128)} %get-tuple-element.108.rank_ref) | copy-start | bytes 98308

commit v5 on v4

--- a/solution.py
+++ b/solution.py
@@ -91,7 +91,7 @@
     return copies
 
 
-def leaf_forward(live_ref, rhs_hbm, map_hbm, inv_ref, upd_ref, y_ref, msg_ref, t_ref, rank_ref, rhs_ref, map_ref, buffer, sems):
+def leaf_forward(live_ref, rhs_hbm, map_hbm, inv_ref, upd_ref, y_ref, msg_ref, t_hbm, rank_hbm, t_ref, rank_ref, rhs_ref, map_ref, buffer, sems):
     step = UPD // CHUNKS
     small = [pltpu.make_async_copy(map_hbm, map_ref, sems.at[2 * CHUNKS]), pltpu.make_async_copy(rhs_hbm, rhs_ref, sems.at[2 * CHUNKS + 1])]
     for one in small:
@@ -117,6 +117,12 @@
     rank_ref[...] = jnp.broadcast_to(rank, rank_ref.shape)
     for half in range(2):
         t_ref[pl.ds(128 * half, 128), :] = jnp.where((rank >> 3) == half, hot, 0.0).astype(BF16)
+    tables = [
+        pltpu.make_async_copy(t_ref, t_hbm, sems.at[2 * CHUNKS + 2]),
+        pltpu.make_async_copy(rank_ref, rank_hbm, sems.at[2 * CHUNKS + 3]),
+    ]
+    for one in tables:
+        one.start()
     live = iota((1, UPD), 1) < live_ref[0]
     local = (rows >> 12) * 32 + (rows & 31) + 1
     places = jnp.where((iota((128, UPD), 0) == rank) & live, local.astype(F32), 0.0)
@@ -136,6 +142,8 @@
     for half in range(2):
         got = dot(t_ref[pl.ds(128 * half, 128), :], parts, NT)
         msg_ref[pl.ds(half, 128, 4), :] = got[:, :128] + got[:, 128:]
+    for one in tables:
+        one.wait()
 
 
 def run_leaf_forward(live, rhs, rows, inv, upd):
@@ -143,12 +151,14 @@
         leaf_forward,
         (sds((V, UPD)), sds((512, 128)), sds((256, UPD), BF16), sds((8, UPD), jnp.int32)),
         [SMEM, HBM, HBM, HBM, HBM],
-        (VM, VM, VM, VM),
+        (VM, VM, HBM, HBM),
         scratch=[
+            pltpu.VMEM((256, UPD), BF16),
+            pltpu.VMEM((8, UPD), jnp.int32),
             pltpu.VMEM((1, V, 1024), F32),
             pltpu.VMEM((1, UPD), jnp.int32),
             pltpu.VMEM((2 * CHUNKS, UPD // CHUNKS, 1024), F32),
-            pltpu.SemaphoreType.DMA((2 * CHUNKS + 2,)),
+            pltpu.SemaphoreType.DMA((2 * CHUNKS + 4,)),
         ],
         flops=2 * 16 * 3 * (2 << 20),
         nbytes=8 << 20,
@@ -377,10 +387,10 @@
     )(got, *ys, x4, w4, w5)
 
 
-def column_message(msg_ref, columns):
+def column_message(msg_ref, columns, copies=4):
     for t in range(8):
         turned = block_swap(columns[:, 128 * t : 128 * t + 128])
-        for l in range(4):
+        for l in range(copies):
             msg_ref[pl.ds(128 * l + 16 * t, 16), :] = turned
 
 
@@ -421,13 +431,13 @@
     columns = pend_ref[level]
     for one, w_ref in zip([r[...] for r in earlier] + [x], blocks):
         columns -= times_rows(one, w_ref[...])
-    column_message(msg_ref, columns)
+    column_message(msg_ref, columns, 4 if level else 1)
 
 
 def run_backward_step(level, got, pend, earlier, blocks):
     return call(
         functools.partial(backward_step, level, len(blocks)),
-        (sds((V, 128)), sds((512, 128))),
+        (sds((V, 128)), sds((512 if level else 128, 128))),
         [VM] * (2 + len(earlier) + len(blocks)),
         (VM, VM),
         flops=len(blocks) << 24,
@@ -516,14 +526,16 @@
     return out[0], out[1:]
 
 
-def own_finish(place_ref, got_ref, x1, x2, x3, x4, x5, index_ref, x_ref, msg_ref):
-    x0 = rows_of(got_ref)
-    levels = [x0] + [r[...] for r in (x1, x2, x3, x4, x5)]
-    mine = []
-    for k, x in enumerate(levels):
+def own_finish(place_ref, got_ref, x1, x2, x3, x4, x5, index_ref, chunk_ref, msg_ref):
+    total = got_ref[pl.ds(0, 8), :]
+    for t in range(1, 16):
+        total += got_ref[pl.ds(8 * t, 8), :]
+    chunk = total[0:4] + total[4:8]
+    chunk_ref[...] = jnp.concatenate([chunk] * 2, 0)
+    mine = [block_swap(jnp.concatenate([chunk] * 4, 0))[:, :32]]
+    for x in [r[...] for r in (x1, x2, x3, x4, x5)]:
         one = jnp.zeros((V, 32), F32)
         for q in range(4):
-            x_ref[pl.ds(4 * k + q, V, 4 * LEVELS), :] = x[:, 32 * q : 32 * q + 32]
             one = jnp.where(place_ref[0] == q, x[:, 32 * q : 32 * q + 32], one)
         mine.append(one)
     rows = jnp.concatenate(mine + [jnp.zeros((V, 64), F32)], 1)
@@ -546,12 +558,36 @@
 def run_own_finish(place, got, xs, index):
     return call(
         own_finish,
-        (sds((V * LEVELS * 4, 32)), sds((256, 128))),
+        (sds((8, 128)), sds((256, 128))),
         [SMEM, VM] + [VM] * 5 + [VM],
         (VM, VM),
         flops=1 << 27,
         nbytes=1 << 20,
     )(place, got, *xs, index)
+
+
+def write_rows(place_ref, c0, c1, c2, c3, x1, x2, x3, x4, x5, out_ref):
+    chunks = [r[0:4, :] for r in (c0, c1, c2, c3)]
+    parts = []
+    for q in range(4):
+        one = jnp.zeros((4, 128), F32)
+        for d in range(4):
+            one = jnp.where(((place_ref[0] + d) & 3) == q, chunks[d], one)
+        parts.append(one)
+    for k, x in enumerate([block_swap(jnp.concatenate(parts, 0))] + [r[...] for r in (x1, x2, x3, x4, x5)]):
+        for q in range(4):
+            out_ref[pl.ds(4 * k + q, V, 4 * LEVELS), :] = x[:, 32 * q : 32 * q + 32]
+
+
+def run_write_rows(place, chunks, xs):
+    return call(
+        write_rows,
+        sds((V * LEVELS * 4, 32)),
+        [SMEM] + [VM] * 9,
+        VM,
+        flops=1 << 20,
+        nbytes=1 << 18,
+    )(place, *chunks, *xs)
 
 
 def exchange(message, axis=ALL):
@@ -590,10 +626,13 @@
     pend, (first, far, near) = run_backward_rest((4, 3), [s4, s3], pend, panels, ((2, 1), (2, 0), (1, 0)))
     s2, message = run_backward_step(1, got, pend, [], [first])
     s1, message = run_backward_step(0, exchange(message), pend, [s2], [far, near])
+    xs = [s1, s2, s3, s4, s5]
+    chunk, message = run_own_finish(place, exchange(message, "sep"), xs, index)
     got = exchange(message)
-    xs = [s1, s2, s3, s4, s5]
-    rows, message = run_own_finish(place, got, xs, index)
-    got = exchange(message)
+    chunks = [chunk]
+    for d in range(1, 4):
+        chunks.append(lax.ppermute(chunk, "leaf", [((l + d) % 4, l) for l in range(4)]))
+    rows = run_write_rows(place, chunks, xs)
     leaf_x = run_leaf_backward(live_rows, got, table, rank, leaf_y, leaf_inv, update_blocks)
     sep_solution = rows.reshape(V, LEVELS, 4, 1, 32)
     return leaf_x, sep_solution

time: 247 us -> 244 us (0.988)
  blocking collectives: 141 us -> 123 us
  starting transfers between devices: 29.4 us -> 38.4 us
  waiting for transfers between devices: 37.8 us -> 41.8 us
    all_to_all x10 -> x9, blocking collectives: 141 us -> 123 us  [exchange(): return lax.all_to_all(message, axis, 0, 0, tiled=True)]
    ppermute x0 -> x3, starting transfers between devices: none -> 5.16 us  [per_device(): lax.ppermute(chunk, 'leaf', [((l + d) % 4, l) for l in range(4)])]
    all_to_all x5 -> x6, starting transfers between devices: 29.4 us -> 33.2 us  [exchange(): return lax.all_to_all(message, axis, 0, 0, tiled=True)]
    all_to_all x5 -> x6, waiting for transfers between devices: 37.8 us -> 40.1 us  [exchange(): return lax.all_to_all(message, axis, 0, 0, tiled=True)]
  transfers between devices with their start and end apart: 5 -> 9, of which waited for: 5 -> 8; matrix products, arithmetic and copies ran while one was open for 1% -> 1% of each run, Pallas kernels for 6% -> 6%
where the time goes in v5:
time: 244 us; the launch traced here: 243 us
  blocking collectives  123 us (50%)
  waiting for transfers between devices  41.8 us (17%)
  starting transfers between devices  38.4 us (16%)
  Pallas kernels  35.6 us (15%)
    all_to_all x9, blocking collectives, exchange(): return lax.all_to_all(message, axis, 0, 0, tiled=True)  123 us
    all_to_all x6, waiting for transfers between devices, exchange(): return lax.all_to_all(message, axis, 0, 0, tiled=True)  40.1 us
    all_to_all x6, starting transfers between devices, exchange(): return lax.all_to_all(message, axis, 0, 0, tiled=True)  33.2 us
    pallas_call x2, Pallas kernels, run_forward_rest(): call(functools.partial(forward_rest, levels, wanted), (sds((LEVELS, V, 12...  7.56 us
    pallas_call x1, Pallas kernels, run_leaf_forward(): call(leaf_forward, (sds((V, UPD)), sds((512, 128)), sds((256, UPD), BF16)...  5.76 us
    ppermute x3, starting transfers between devices, per_device(): lax.ppermute(chunk, 'leaf', [((l + d) % 4, l) for l in range(4)])  5.16 us
    pallas_call x1, Pallas kernels, run_leaf_backward(): call(leaf_backward, sds((1, V, 1024)), [SMEM, VM, VM, VM, VM, HBM, HBM],...  4.98 us
  transfers between devices with their start and end apart: 9, of which 8 were waited for; matrix products, arithmetic and copies ran while one was open for 1% of the time, Pallas kernels for 6%

profile of v5, /device:TPU:1, one launch (start us, length us, event | category | flops | bytes accessed | tf_op | source)
XLA Modules:
  0.0 243.0 jit_solution(10237260328888942342)
XLA Ops:
  1.3 5.8 %shard_map.95 = (f32[16,1024]{1,0:T(8,128)}, f32[512,128]{1,0:T(8,128)}, bf16[256,1024]{1,0:T(8,128)(2,1)}, s32[8,1024]{1,0:T(8,128)}) custom-call(s32[1]{0:T(128)S(6)} %copy.11.live_ref, f32[1,16,1024]{2,1,0:T(8,128)} %rhs_hbm.1, s32[1,1024]{1,0:T(1,128)} %map_hbm.1, f32[1,1024,1024]{2,1,0:T(8,128)} %inv_ref.3, f32[1,1024,1024]{2,1,0:T(8,128)} %upd_ref.3), custom_call_target="tpu_custom_call" | custom-call | flops 201326592 | bytes 8388608 | tf_op jit(solution)/shard_map/pallas_call | solution.py:150
  7.0 11.5 %all-to-all-start = ((f32[128,4,128]{2,1,0:T(4,128)}), f32[128,4,128]{2,1,0:T(4,128)S(1)}, u32[]{:S(2)}, u32[]{:S(2)}) async-start(f32[128,4,128]{2,1,0:T(4,128)} %bitcast.58), calls=%async_computation | async-start | bytes 524288 | tf_op jit(solution)/shard_map/all_to_all | solution.py:594
  19.1 1.2 reduce.3
  21.3 1.5 shard_map.96
  22.8 6.7 %all-to-all-done = f32[128,4,128]{2,1,0:T(4,128)S(1)} async-done(((f32[128,4,128]{2,1,0:T(4,128)}), f32[128,4,128]{2,1,0:T(4,128)S(1)}, u32[]{:S(2)}, u32[]{:S(2)}) %all-to-all-start) | async-done | bytes 262176 | tf_op jit(solution)/shard_map/all_to_all | solution.py:594
  30.2 11.7 %all_to_all.165 = f32[32,4,128]{2,1,0:T(4,128)S(1)} all-to-all(f32[32,4,128]{2,1,0:T(4,128)S(1)} %bitcast.57), channel_id=1, replica_groups=mesh['leaf'=4,'sep'=32] {'sep'}, dimensions={0} | all-to-all | bytes 131072 | tf_op jit(solution)/shard_map/all_to_all | solution.py:594
  42.3 14.4 %all_to_all.166 = f32[128,4,128]{2,1,0:T(4,128)S(1)} all-to-all(f32[128,4,128]{2,1,0:T(4,128)S(1)} %bitcast.49), channel_id=1, replica_groups=mesh['leaf'=4,'sep'=32] {'leaf','sep'}, dimensions={0} | all-to-all | bytes 524288 | tf_op jit(solution)/shard_map/all_to_all | solution.py:594
  57.9 4.5 %all-to-all-start.3 = ((f32[128,4,128]{2,1,0:T(4,128)}), f32[128,4,128]{2,1,0:T(4,128)S(1)}, u32[]{:S(2)}, u32[]{:S(2)}) async-start(f32[128,4,128]{2,1,0:T(4,128)} %bitcast.7), calls=%async_computation.3 | async-start | bytes 524288 | tf_op jit(solution)/shard_map/all_to_all | solution.py:594
  62.4 4.6 %shard_map.100 = (f32[6,16,128]{2,1,0:T(8,128)S(1)}, f32[16,128]{1,0:T(8,128)S(1)}, f32[16,128]{1,0:T(8,128)S(1)}, bf16[256,1024]{1,0:T(8,128)(2,1)S(1)}, bf16[2...) custom-call(f32[16,1024]{1,0:T(8,128)S(1)} %get-tuple-element.63.refs_2_.refs_0_, ...), custom_call_target="tpu_custom_call" | custom-call | flops 184549376 | bytes 5767168 | tf_op jit(solution)/shard_map/pallas_call | solution.py:357
  67.0 6.4 %all-to-all-done.3 = f32[128,4,128]{2,1,0:T(4,128)S(1)} async-done(((f32[128,4,128]{2,1,0:T(4,128)}), f32[128,4,128]{2,1,0:T(4,128)S(1)}, u32[]{:S(2)}, u32[]{:S(2)}) %all-to-all-start.3) | async-done | bytes 262176 | tf_op jit(solution)/shard_map/all_to_all | solution.py:594
  73.8 15.3 %all_to_all.167 = f32[128,4,128]{2,1,0:T(4,128)S(1)} all-to-all(f32[128,4,128]{2,1,0:T(4,128)S(1)} %bitcast.50), channel_id=1, replica_groups=mesh['leaf'=4,'sep'=32] {'leaf','sep'}, dimensions={0} | all-to-all | bytes 524288 | tf_op jit(solution)/shard_map/all_to_all | solution.py:594
  90.3 4.5 %all-to-all-start.5 = ((f32[128,4,128]{2,1,0:T(4,128)}), f32[128,4,128]{2,1,0:T(4,128)S(1)}, u32[]{:S(2)}, u32[]{:S(2)}) async-start(f32[128,4,128]{2,1,0:T(4,128)} %bitcast.11), calls=%async_computation.5 | async-start | bytes 524288 | tf_op jit(solution)/shard_map/all_to_all | solution.py:594
  94.8 3.0 %shard_map.103 = (f32[6,16,128]{2,1,0:T(8,128)S(1)}, f32[16,128]{1,0:T(8,128)S(1)}, f32[16,128]{1,0:T(8,128)S(1)}, bf16[256,1024]{1,0:T(8,128)(2,1)S(1)}, bf16[2...) custom-call(f32[16,1024]{1,0:T(8,128)S(1)} %get-tuple-element.70.refs_2_.refs_0_, ...), custom_call_target="tpu_custom_call" | custom-call | flops 117440512 | bytes 3670016 | tf_op jit(solution)/shard_map/pallas_call | solution.py:357
  97.7 8.0 %all-to-all-done.5 = f32[128,4,128]{2,1,0:T(4,128)S(1)} async-done(((f32[128,4,128]{2,1,0:T(4,128)}), f32[128,4,128]{2,1,0:T(4,128)S(1)}, u32[]{:S(2)}, u32[]{:S(2)}) %all-to-all-start.5) | async-done | bytes 262176 | tf_op jit(solution)/shard_map/all_to_all | solution.py:594
  106.2 15.3 %all_to_all.168 = f32[128,4,128]{2,1,0:T(4,128)S(1)} all-to-all(f32[128,4,128]{2,1,0:T(4,128)S(1)} %bitcast.51), channel_id=1, replica_groups=mesh['leaf'=4,'sep'=32] {'leaf','sep'}, dimensions={0} | all-to-all | bytes 524288 | tf_op jit(solution)/shard_map/all_to_all | solution.py:594
  121.8 7.6 %all_to_all.169 = f32[4,96,128]{2,1,0:T(8,128)S(1)} all-to-all(f32[4,96,128]{2,1,0:T(8,128)S(1)} %bitcast.45), channel_id=1, replica_groups=mesh['leaf'=4,'sep'=32] {'leaf'}, dimensions={0} | all-to-all | bytes 393216 | tf_op jit(solution)/shard_map/all_to_all | solution.py:594
  129.7 16.5 %all_to_all.170 = f32[128,4,128]{2,1,0:T(4,128)S(1)} all-to-all(f32[128,4,128]{2,1,0:T(4,128)S(1)} %bitcast.52), channel_id=1, replica_groups=mesh['leaf'=4,'sep'=32] {'leaf','sep'}, dimensions={0} | all-to-all | bytes 524288 | tf_op jit(solution)/shard_map/all_to_all | solution.py:594
  147.3 4.5 %all-to-all-start.9 = ((f32[128,4,128]{2,1,0:T(4,128)}), f32[128,4,128]{2,1,0:T(4,128)S(1)}, u32[]{:S(2)}, u32[]{:S(2)}) async-start(f32[128,4,128]{2,1,0:T(4,128)} %bitcast.19), calls=%async_computation.9 | async-start | bytes 524288 | tf_op jit(solution)/shard_map/all_to_all | solution.py:594
  151.8 3.0 %shard_map.108 = (f32[4,16,1024]{2,1,0:T(8,128)S(1)}, bf16[256,1024]{1,0:T(8,128)(2,1)S(1)}, bf16[256,1024]{1,0:T(8,128)(2,1)S(1)}, bf16[256,1024]{1,0:T(8,128)(2,1)S(1)}) custom-call(f32[96,128]{1,0:T(8,128)S(1)} %get-tuple-element.86.y_ref, f32[16,128]{1,0:T(8,128)S(1)} %get-tuple-element.88.x_ref.x5, f32[15,4,1,32,1024]{4,3,2,1,0:T(8,128)} %refs_3_.5, ...), custom_call_target="tpu_custom_call" | custom-call | flops 184549376 | bytes 6291456 | tf_op jit(solution)/shard_map/pallas_call | solution.py:481
  154.8 8.0 %all-to-all-done.9 = f32[128,4,128]{2,1,0:T(4,128)S(1)} async-done(((f32[128,4,128]{2,1,0:T(4,128)}), f32[128,4,128]{2,1,0:T(4,128)S(1)}, u32[]{:S(2)}, u32[]{:S(2)}) %all-to-all-start.9) | async-done | bytes 262176 | tf_op jit(solution)/shard_map/all_to_all | solution.py:594
  163.1 15.3 %all_to_all.171 = f32[128,4,128]{2,1,0:T(4,128)S(1)} all-to-all(f32[128,4,128]{2,1,0:T(4,128)S(1)} %bitcast.53), channel_id=1, replica_groups=mesh['leaf'=4,'sep'=32] {'leaf','sep'}, dimensions={0} | all-to-all | bytes 524288 | tf_op jit(solution)/shard_map/all_to_all | solution.py:594
  179.5 4.5 %all-to-all-start.11 = ((f32[128,4,128]{2,1,0:T(4,128)}), f32[128,4,128]{2,1,0:T(4,128)S(1)}, u32[]{:S(2)}, u32[]{:S(2)}) async-start(f32[128,4,128]{2,1,0:T(4,128)} %bitcast.23), calls=%async_computation.11 | async-start | bytes 524288 | tf_op jit(solution)/shard_map/all_to_all | solution.py:594
  184.0 2.3 shard_map.111
  186.3 8.7 %all-to-all-done.11 = f32[128,4,128]{2,1,0:T(4,128)S(1)} async-done(((f32[128,4,128]{2,1,0:T(4,128)}), f32[128,4,128]{2,1,0:T(4,128)S(1)}, u32[]{:S(2)}, u32[]{:S(2)}) %all-to-all-start.11) | async-done | bytes 262176 | tf_op jit(solution)/shard_map/all_to_all | solution.py:594
  195.4 15.3 %all_to_all.172 = f32[128,4,128]{2,1,0:T(4,128)S(1)} all-to-all(f32[128,4,128]{2,1,0:T(4,128)S(1)} %bitcast.54), channel_id=1, replica_groups=mesh['leaf'=4,'sep'=32] {'leaf','sep'}, dimensions={0} | all-to-all | bytes 524288 | tf_op jit(solution)/shard_map/all_to_all | solution.py:594
  211.0 11.7 %all_to_all.173 = f32[32,4,128]{2,1,0:T(4,128)S(1)} all-to-all(f32[32,4,128]{2,1,0:T(4,128)S(1)} %bitcast.55), channel_id=1, replica_groups=mesh['leaf'=4,'sep'=32] {'sep'}, dimensions={0} | all-to-all | bytes 131072 | tf_op jit(solution)/shard_map/all_to_all | solution.py:594
  222.7 1.4 shard_map.114
  224.1 3.8 %all-to-all-start.14 = ((f32[128,2,128]{2,1,0:T(2,128)}), f32[128,2,128]{2,1,0:T(2,128)S(1)}, u32[]{:S(2)}, u32[]{:S(2)}) async-start(f32[128,2,128]{2,1,0:T(2,128)} %bitcast.29), calls=%async_computation.14 | async-start | bytes 262144 | tf_op jit(solution)/shard_map/all_to_all | solution.py:594
  227.9 1.5 collective-permute-start.2
  229.4 2.5 %collective-permute-start.1 = (f32[8,128]{1,0:T(8,128)S(1)}, f32[8,128]{1,0:T(8,128)S(1)}, u32[]{:S(2)}, u32[]{:S(2)}) collective-permute-start(f32[8,128]{1,0:T(8,128)S(1)} %get-tuple-element.109.c0), channel_id=1, source_target_pairs={{64,0},{96,32},{0,64},{32,96},{65,1},{97,33},{1,65},{33,97},{66,2}... | collective-permute-start | bytes 12296 | tf_op jit(solution)/shard_map/ppermute | solution.py:634
  235.6 2.3 all-to-all-done.14
  237.9 5.0 %shard_map.115 = f32[1,16,1024]{2,1,0:T(8,128)} custom-call(s32[1]{0:T(128)S(6)} %copy.11.live_ref, f32[256,128]{1,0:T(8,128)S(1)} %bitcast.47, bf16[256,1024]{1,0:T(8,128)(2,1)S(1)} %copy-done, s32[8,1024]{1,0:T(8,128)S(1)} %copy-done.3, f32[16,1024]{1,0:T(8,128)S(1)} %copy-done.2, f32[1,1024,1024]{2,1,0:T(8,128)} %inv_ref.3, f32[1,1024,1024]{2,1,0:T(8,128)} %upd_ref.3), custom_call_target="tpu_custom_call" | custom-call | flops 201326592 | bytes 8388608 | tf_op jit(solution)/shard_map/pallas_call | solution.py:196
  (30 shorter events, 13.3 us)
Async XLA Ops:
  1.3 17.8 %copy-start.4 = (f32[16,6,4,1,32]{4,3,2,1,0:T(1,128)S(1)}, f32[16,6,4,1,32]{4,3,2,1,0:T(1,128)}, u32[]{:S(2)}) copy-start(f32[16,6,4,1,32]{4,3,2,1,0:T(1,128)} %param.13) | copy-start | bytes 147460
  7.0 22.4 %all-to-all-start = ((f32[128,4,128]{2,1,0:T(4,128)}), f32[128,4,128]{2,1,0:T(4,128)S(1)}, u32[]{:S(2)}, u32[]{:S(2)}) async-start(f32[128,4,128]{2,1,0:T(4,128)} %bitcast.58), calls=%async_computation | async-start | bytes 524288 | tf_op jit(solution)/shard_map/all_to_all | solution.py:594
  20.5 0.8 copy-start.1
  57.9 15.5 %all-to-all-start.3 = ((f32[128,4,128]{2,1,0:T(4,128)}), f32[128,4,128]{2,1,0:T(4,128)S(1)}, u32[]{:S(2)}, u32[]{:S(2)}) async-start(f32[128,4,128]{2,1,0:T(4,128)} %bitcast.7), calls=%async_computation.3 | async-start | bytes 524288 | tf_op jit(solution)/shard_map/all_to_all | solution.py:594
  90.3 15.5 %all-to-all-start.5 = ((f32[128,4,128]{2,1,0:T(4,128)}), f32[128,4,128]{2,1,0:T(4,128)S(1)}, u32[]{:S(2)}, u32[]{:S(2)}) async-start(f32[128,4,128]{2,1,0:T(4,128)} %bitcast.11), calls=%async_computation.5 | async-start | bytes 524288 | tf_op jit(solution)/shard_map/all_to_all | solution.py:594
  147.3 15.5 %all-to-all-start.9 = ((f32[128,4,128]{2,1,0:T(4,128)}), f32[128,4,128]{2,1,0:T(4,128)S(1)}, u32[]{:S(2)}, u32[]{:S(2)}) async-start(f32[128,4,128]{2,1,0:T(4,128)} %bitcast.19), calls=%async_computation.9 | async-start | bytes 524288 | tf_op jit(solution)/shard_map/all_to_all | solution.py:594
  179.5 15.5 %all-to-all-start.11 = ((f32[128,4,128]{2,1,0:T(4,128)}), f32[128,4,128]{2,1,0:T(4,128)S(1)}, u32[]{:S(2)}, u32[]{:S(2)}) async-start(f32[128,4,128]{2,1,0:T(4,128)} %bitcast.23), calls=%async_computation.11 | async-start | bytes 524288 | tf_op jit(solution)/shard_map/all_to_all | solution.py:594
  184.0 53.9 %copy-start = (bf16[256,1024]{1,0:T(8,128)(2,1)S(1)}, bf16[256,1024]{1,0:T(8,128)(2,1)}, u32[]{:S(2)}) copy-start(bf16[256,1024]{1,0:T(8,128)(2,1)} %get-tuple-element.107.t_ref) | copy-start | bytes 1572868
  184.0 53.9 %copy-start.2 = (f32[16,1024]{1,0:T(8,128)S(1)}, f32[16,1024]{1,0:T(8,128)}, u32[]{:S(2)}) copy-start(f32[16,1024]{1,0:T(8,128)} %get-tuple-element.57.after_ref.y_ref) | copy-start | bytes 196612
  184.0 53.9 %copy-start.3 = (s32[8,1024]{1,0:T(8,128)S(1)}, s32[8,1024]{1,0:T(8,128)}, u32[]{:S(2)}) copy-start(s32[8,1024]{1,0:T(8,128)} %get-tuple-element.108.rank_ref) | copy-start | bytes 98308
  224.1 13.8 %all-to-all-start.14 = ((f32[128,2,128]{2,1,0:T(2,128)}), f32[128,2,128]{2,1,0:T(2,128)S(1)}, u32[]{:S(2)}, u32[]{:S(2)}) async-start(f32[128,2,128]{2,1,0:T(2,128)} %bitcast.29), calls=%async_computation.14 | async-start | bytes 262144 | tf_op jit(solution)/shard_map/all_to_all | solution.py:594
  227.9 5.2 %collective-permute-start.2 = (f32[8,128]{1,0:T(8,128)S(1)}, f32[8,128]{1,0:T(8,128)S(1)}, u32[]{:S(2)}, u32[]{:S(2)}) collective-permute-start(f32[8,128]{1,0:T(8,128)S(1)} %get-tuple-element.109.c0), channel_id=1, source_target_pairs={{96,0},{0,32},{32,64},{64,96},{97,1},{1,33},{33,65},{65,97},{98,2}... | collective-permute-start | bytes 12296 | tf_op jit(solution)/shard_map/ppermute | solution.py:634
  229.4 4.3 %collective-permute-start.1 = (f32[8,128]{1,0:T(8,128)S(1)}, f32[8,128]{1,0:T(8,128)S(1)}, u32[]{:S(2)}, u32[]{:S(2)}) collective-permute-start(f32[8,128]{1,0:T(8,128)S(1)} %get-tuple-element.109.c0), channel_id=1, source_target_pairs={{64,0},{96,32},{0,64},{32,96},{65,1},{97,33},{1,65},{33,97},{66,2}... | collective-permute-start | bytes 12296 | tf_op jit(solution)/shard_map/ppermute | solution.py:634
  232.0 2.8 %collective-permute-start = (f32[8,128]{1,0:T(8,128)S(1)}, f32[8,128]{1,0:T(8,128)S(1)}, u32[]{:S(2)}, u32[]{:S(2)}) collective-permute-start(f32[8,128]{1,0:T(8,128)S(1)} %get-tuple-element.109.c0), channel_id=1, source_target_pairs={{32,0},{64,32},{96,64},{0,96},{33,1},{65,33},{97,65},{1,97},{34,2}... | collective-permute-start | bytes 12296 | tf_op jit(solution)/shard_map/ppermute | solution.py:634

commit v6 on v5

--- a/solution.py
+++ b/solution.py
@@ -369,17 +369,16 @@
 def forward_last(got_ref, y0, y1, y2, y3, x4_ref, w4_ref, w5_ref, msg_ref):
     y4 = times_columns(x4_ref[...], w4_ref[...])
     y5 = times_columns(columns_of(got_ref, 4), w5_ref[...])
-    for l in range(4):
-        for k, one in enumerate((y0, y1, y2, y3)):
-            msg_ref[pl.ds(96 * l + 16 * k, 16), :] = one[...]
-        msg_ref[pl.ds(96 * l + 64, 16), :] = y4
-        msg_ref[pl.ds(96 * l + 80, 16), :] = y5
+    for k, one in enumerate((y0, y1, y2, y3)):
+        msg_ref[pl.ds(16 * k, 16), :] = one[...]
+    msg_ref[pl.ds(64, 16), :] = y4
+    msg_ref[pl.ds(80, 16), :] = y5
 
 
 def run_forward_last(got, ys, x4, w4, w5):
     return call(
         forward_last,
-        sds((4 * 96, 128)),
+        sds((96, 128)),
         [VM] * 8,
         VM,
         flops=2 << 24,
@@ -394,23 +393,21 @@
             msg_ref[pl.ds(128 * l + 16 * t, 16), :] = turned
 
 
-def backward_start(got_ref, w_ref, y_ref, msg_ref):
-    y = got_ref[pl.ds(0, 96), :]
-    for l in range(1, 4):
-        y += got_ref[pl.ds(96 * l, 96), :]
+def backward_start(own_ref, g1, g2, g3, w_ref, y_ref, msg_ref):
+    y = (own_ref[...] + g1[...]) + (g2[...] + g3[...])
     y_ref[...] = y
     column_message(msg_ref, times_rows(y[80:96], w_ref[...]))
 
 
-def run_backward_start(got, w):
+def run_backward_start(own, others, w):
     return call(
         backward_start,
         (sds((96, 128)), sds((512, 128))),
-        [VM, VM],
+        [VM] * 5,
         (VM, VM),
         flops=1 << 24,
         nbytes=1 << 20,
-    )(got, w)
+    )(own, *others, w)
 
 
 def rows_of(got_ref):
@@ -594,6 +591,10 @@
     return lax.all_to_all(message, axis, 0, 0, tiled=True)
 
 
+def from_other_leaves(array):
+    return [lax.ppermute(array, "leaf", [((l + d) % 4, l) for l in range(4)]) for d in range(1, 4)]
+
+
 def per_device(leaf_rhs, leaf_inv, update_blocks, row_map, live_rows, sep_rhs, inv_diag, panels):
     place = lax.axis_index("leaf").astype(jnp.int32).reshape(1)
     rhs = sep_rhs.reshape(V, LEVELS * 128)
@@ -616,7 +617,7 @@
     )
     x4, message = run_forward_step(5, 4, got, pend, [], [first])
     message = run_forward_last(exchange(message), [y0, y1, y2, y3], x4, d4, d5)
-    y, message = run_backward_start(exchange(message, "leaf"), d5)
+    y, message = run_backward_start(message, from_other_leaves(message), d5)
     s5, message = run_backward_next(exchange(message), y, d4, first)
     got = exchange(message)
     pend, (first, far, near) = run_backward_diag(y, s5, panels, inv_diag, ((4, 3), (4, 2), (3, 2)))
@@ -629,9 +630,7 @@
     xs = [s1, s2, s3, s4, s5]
     chunk, message = run_own_finish(place, exchange(message, "sep"), xs, index)
     got = exchange(message)
-    chunks = [chunk]
-    for d in range(1, 4):
-        chunks.append(lax.ppermute(chunk, "leaf", [((l + d) % 4, l) for l in range(4)]))
+    chunks = [chunk, *from_other_leaves(chunk)]
     rows = run_write_rows(place, chunks, xs)
     leaf_x = run_leaf_backward(live_rows, got, table, rank, leaf_y, leaf_inv, update_blocks)
     sep_solution = rows.reshape(V, LEVELS, 4, 1, 32)

time: 244 us -> 243 us (level)
  blocking collectives: 123 us -> 117 us
  starting transfers between devices: 38.4 us -> 41.7 us
    all_to_all x9 -> x8, blocking collectives: 123 us -> 117 us  [exchange(): return lax.all_to_all(message, axis, 0, 0, tiled=True)]
    ppermute x3 -> x6, starting transfers between devices: 5.16 us -> 8.49 us  [from_other_leaves(): lax.ppermute(array, 'leaf', [((l + d) % 4, l) for l in range(4)])]
  transfers between devices with their start and end apart: 9 -> 12, of which waited for: 8 -> 11; matrix products, arithmetic and copies ran while one was open for 1% -> 1% of each run, Pallas kernels for 6% -> 6%
where the time goes in v6:
time: 243 us; the launch traced here: 242 us
  blocking collectives  117 us (48%)
  waiting for transfers between devices  43.9 us (18%)
  starting transfers between devices  41.7 us (17%)
  Pallas kernels  35.6 us (15%)
    all_to_all x8, blocking collectives, exchange(): return lax.all_to_all(message, axis, 0, 0, tiled=True)  117 us
    all_to_all x6, waiting for transfers between devices, exchange(): return lax.all_to_all(message, axis, 0, 0, tiled=True)  40 us
    all_to_all x6, starting transfers between devices, exchange(): return lax.all_to_all(message, axis, 0, 0, tiled=True)  33.2 us
    ppermute x6, starting transfers between devices, from_other_leaves(): lax.ppermute(array, 'leaf', [((l + d) % 4, l) for l in range(4)])  8.49 us
    pallas_call x2, Pallas kernels, run_forward_rest(): call(functools.partial(forward_rest, levels, wanted), (sds((LEVELS, V, 12...  7.56 us
    pallas_call x1, Pallas kernels, run_leaf_forward(): call(leaf_forward, (sds((V, UPD)), sds((512, 128)), sds((256, UPD), BF16)...  5.76 us
    pallas_call x1, Pallas kernels, run_leaf_backward(): call(leaf_backward, sds((1, V, 1024)), [SMEM, VM, VM, VM, VM, HBM, HBM],...  4.98 us
  transfers between devices with their start and end apart: 12, of which 11 were waited for; matrix products, arithmetic and copies ran while one was open for 1% of the time, Pallas kernels for 6%

profile of v6, /device:TPU:1, one launch (start us, length us, event | category | flops | bytes accessed | tf_op | source)
XLA Modules:
  0.0 242.3 jit_solution(2814676318227477021)
XLA Ops:
  1.3 5.8 %shard_map.95 = (f32[16,1024]{1,0:T(8,128)}, f32[512,128]{1,0:T(8,128)}, bf16[256,1024]{1,0:T(8,128)(2,1)}, s32[8,1024]{1,0:T(8,128)}) custom-call(s32[1]{0:T(128)S(6)} %copy.11.live_ref, f32[1,16,1024]{2,1,0:T(8,128)} %rhs_hbm.1, s32[1,1024]{1,0:T(1,128)} %map_hbm.1, f32[1,1024,1024]{2,1,0:T(8,128)} %inv_ref.3, f32[1,1024,1024]{2,1,0:T(8,128)} %upd_ref.3), custom_call_target="tpu_custom_call" | custom-call | flops 201326592 | bytes 8388608 | tf_op jit(solution)/shard_map/pallas_call | solution.py:150
  7.1 11.5 %all-to-all-start = ((f32[128,4,128]{2,1,0:T(4,128)}), f32[128,4,128]{2,1,0:T(4,128)S(1)}, u32[]{:S(2)}, u32[]{:S(2)}) async-start(f32[128,4,128]{2,1,0:T(4,128)} %bitcast.54), calls=%async_computation | async-start | bytes 524288 | tf_op jit(solution)/shard_map/all_to_all | solution.py:591
  21.3 1.5 shard_map.96
  22.8 6.7 %all-to-all-done = f32[128,4,128]{2,1,0:T(4,128)S(1)} async-done(((f32[128,4,128]{2,1,0:T(4,128)}), f32[128,4,128]{2,1,0:T(4,128)S(1)}, u32[]{:S(2)}, u32[]{:S(2)}) %all-to-all-start) | async-done | bytes 262176 | tf_op jit(solution)/shard_map/all_to_all | solution.py:591
  30.2 11.7 %all_to_all.154 = f32[32,4,128]{2,1,0:T(4,128)S(1)} all-to-all(f32[32,4,128]{2,1,0:T(4,128)S(1)} %bitcast.53), channel_id=1, replica_groups=mesh['leaf'=4,'sep'=32] {'sep'}, dimensions={0} | all-to-all | bytes 131072 | tf_op jit(solution)/shard_map/all_to_all | solution.py:591
  42.3 14.4 %all_to_all.155 = f32[128,4,128]{2,1,0:T(4,128)S(1)} all-to-all(f32[128,4,128]{2,1,0:T(4,128)S(1)} %bitcast.46), channel_id=1, replica_groups=mesh['leaf'=4,'sep'=32] {'leaf','sep'}, dimensions={0} | all-to-all | bytes 524288 | tf_op jit(solution)/shard_map/all_to_all | solution.py:591
  57.9 4.5 %all-to-all-start.3 = ((f32[128,4,128]{2,1,0:T(4,128)}), f32[128,4,128]{2,1,0:T(4,128)S(1)}, u32[]{:S(2)}, u32[]{:S(2)}) async-start(f32[128,4,128]{2,1,0:T(4,128)} %bitcast.7), calls=%async_computation.3 | async-start | bytes 524288 | tf_op jit(solution)/shard_map/all_to_all | solution.py:591
  62.4 4.6 %shard_map.100 = (f32[6,16,128]{2,1,0:T(8,128)S(1)}, f32[16,128]{1,0:T(8,128)S(1)}, f32[16,128]{1,0:T(8,128)S(1)}, bf16[256,1024]{1,0:T(8,128)(2,1)S(1)}, bf16[2...) custom-call(f32[16,1024]{1,0:T(8,128)S(1)} %get-tuple-element.63.refs_2_.refs_0_, ...), custom_call_target="tpu_custom_call" | custom-call | flops 184549376 | bytes 5767168 | tf_op jit(solution)/shard_map/pallas_call | solution.py:357
  67.0 6.4 %all-to-all-done.3 = f32[128,4,128]{2,1,0:T(4,128)S(1)} async-done(((f32[128,4,128]{2,1,0:T(4,128)}), f32[128,4,128]{2,1,0:T(4,128)S(1)}, u32[]{:S(2)}, u32[]{:S(2)}) %all-to-all-start.3) | async-done | bytes 262176 | tf_op jit(solution)/shard_map/all_to_all | solution.py:591
  73.8 15.3 %all_to_all.156 = f32[128,4,128]{2,1,0:T(4,128)S(1)} all-to-all(f32[128,4,128]{2,1,0:T(4,128)S(1)} %bitcast.47), channel_id=1, replica_groups=mesh['leaf'=4,'sep'=32] {'leaf','sep'}, dimensions={0} | all-to-all | bytes 524288 | tf_op jit(solution)/shard_map/all_to_all | solution.py:591
  90.3 4.5 %all-to-all-start.5 = ((f32[128,4,128]{2,1,0:T(4,128)}), f32[128,4,128]{2,1,0:T(4,128)S(1)}, u32[]{:S(2)}, u32[]{:S(2)}) async-start(f32[128,4,128]{2,1,0:T(4,128)} %bitcast.11), calls=%async_computation.5 | async-start | bytes 524288 | tf_op jit(solution)/shard_map/all_to_all | solution.py:591
  94.8 3.0 %shard_map.103 = (f32[6,16,128]{2,1,0:T(8,128)S(1)}, f32[16,128]{1,0:T(8,128)S(1)}, f32[16,128]{1,0:T(8,128)S(1)}, bf16[256,1024]{1,0:T(8,128)(2,1)S(1)}, bf16[2...) custom-call(f32[16,1024]{1,0:T(8,128)S(1)} %get-tuple-element.70.refs_2_.refs_0_, ...), custom_call_target="tpu_custom_call" | custom-call | flops 117440512 | bytes 3670016 | tf_op jit(solution)/shard_map/pallas_call | solution.py:357
  97.7 8.0 %all-to-all-done.5 = f32[128,4,128]{2,1,0:T(4,128)S(1)} async-done(((f32[128,4,128]{2,1,0:T(4,128)}), f32[128,4,128]{2,1,0:T(4,128)S(1)}, u32[]{:S(2)}, u32[]{:S(2)}) %all-to-all-start.5) | async-done | bytes 262176 | tf_op jit(solution)/shard_map/all_to_all | solution.py:591
  106.1 15.3 %all_to_all.157 = f32[128,4,128]{2,1,0:T(4,128)S(1)} all-to-all(f32[128,4,128]{2,1,0:T(4,128)S(1)} %bitcast.48), channel_id=1, replica_groups=mesh['leaf'=4,'sep'=32] {'leaf','sep'}, dimensions={0} | all-to-all | bytes 524288 | tf_op jit(solution)/shard_map/all_to_all | solution.py:591
  122.1 1.7 collective-permute-start.1
  123.7 1.4 collective-permute-start
  127.7 17.8 %all_to_all.158 = f32[128,4,128]{2,1,0:T(4,128)S(1)} all-to-all(f32[128,4,128]{2,1,0:T(4,128)S(1)} %bitcast.45), channel_id=1, replica_groups=mesh['leaf'=4,'sep'=32] {'leaf','sep'}, dimensions={0} | all-to-all | bytes 524288 | tf_op jit(solution)/shard_map/all_to_all | solution.py:591
  146.5 4.5 %all-to-all-start.8 = ((f32[128,4,128]{2,1,0:T(4,128)}), f32[128,4,128]{2,1,0:T(4,128)S(1)}, u32[]{:S(2)}, u32[]{:S(2)}) async-start(f32[128,4,128]{2,1,0:T(4,128)} %bitcast.17), calls=%async_computation.8 | async-start | bytes 524288 | tf_op jit(solution)/shard_map/all_to_all | solution.py:591
  151.0 3.0 %shard_map.108 = (f32[4,16,1024]{2,1,0:T(8,128)S(1)}, bf16[256,1024]{1,0:T(8,128)(2,1)S(1)}, bf16[256,1024]{1,0:T(8,128)(2,1)S(1)}, bf16[256,1024]{1,0:T(8,128)(2,1)S(1)}) custom-call(f32[96,128]{1,0:T(8,128)S(1)} %get-tuple-element.86.y_ref, f32[16,128]{1,0:T(8,128)S(1)} %get-tuple-element.88.x_ref.x5, f32[15,4,1,32,1024]{4,3,2,1,0:T(8,128)} %refs_3_.5, ...), custom_call_target="tpu_custom_call" | custom-call | flops 184549376 | bytes 6291456 | tf_op jit(solution)/shard_map/pallas_call | solution.py:478
  154.1 7.9 %all-to-all-done.8 = f32[128,4,128]{2,1,0:T(4,128)S(1)} async-done(((f32[128,4,128]{2,1,0:T(4,128)}), f32[128,4,128]{2,1,0:T(4,128)S(1)}, u32[]{:S(2)}, u32[]{:S(2)}) %all-to-all-start.8) | async-done | bytes 262176 | tf_op jit(solution)/shard_map/all_to_all | solution.py:591
  162.4 15.3 %all_to_all.159 = f32[128,4,128]{2,1,0:T(4,128)S(1)} all-to-all(f32[128,4,128]{2,1,0:T(4,128)S(1)} %bitcast.49), channel_id=1, replica_groups=mesh['leaf'=4,'sep'=32] {'leaf','sep'}, dimensions={0} | all-to-all | bytes 524288 | tf_op jit(solution)/shard_map/all_to_all | solution.py:591
  178.7 4.5 %all-to-all-start.10 = ((f32[128,4,128]{2,1,0:T(4,128)}), f32[128,4,128]{2,1,0:T(4,128)S(1)}, u32[]{:S(2)}, u32[]{:S(2)}) async-start(f32[128,4,128]{2,1,0:T(4,128)} %bitcast.21), calls=%async_computation.10 | async-start | bytes 524288 | tf_op jit(solution)/shard_map/all_to_all | solution.py:591
  183.3 2.3 shard_map.111
  185.5 8.7 %all-to-all-done.10 = f32[128,4,128]{2,1,0:T(4,128)S(1)} async-done(((f32[128,4,128]{2,1,0:T(4,128)}), f32[128,4,128]{2,1,0:T(4,128)S(1)}, u32[]{:S(2)}, u32[]{:S(2)}) %all-to-all-start.10) | async-done | bytes 262176 | tf_op jit(solution)/shard_map/all_to_all | solution.py:591
  194.6 15.3 %all_to_all.160 = f32[128,4,128]{2,1,0:T(4,128)S(1)} all-to-all(f32[128,4,128]{2,1,0:T(4,128)S(1)} %bitcast.50), channel_id=1, replica_groups=mesh['leaf'=4,'sep'=32] {'leaf','sep'}, dimensions={0} | all-to-all | bytes 524288 | tf_op jit(solution)/shard_map/all_to_all | solution.py:591
  210.2 11.7 %all_to_all.161 = f32[32,4,128]{2,1,0:T(4,128)S(1)} all-to-all(f32[32,4,128]{2,1,0:T(4,128)S(1)} %bitcast.51), channel_id=1, replica_groups=mesh['leaf'=4,'sep'=32] {'sep'}, dimensions={0} | all-to-all | bytes 131072 | tf_op jit(solution)/shard_map/all_to_all | solution.py:591
  221.9 1.5 shard_map.114
  223.4 3.8 %all-to-all-start.13 = ((f32[128,2,128]{2,1,0:T(2,128)}), f32[128,2,128]{2,1,0:T(2,128)S(1)}, u32[]{:S(2)}, u32[]{:S(2)}) async-start(f32[128,2,128]{2,1,0:T(2,128)} %bitcast.27), calls=%async_computation.13 | async-start | bytes 262144 | tf_op jit(solution)/shard_map/all_to_all | solution.py:591
  227.2 1.5 collective-permute-start.5
  228.7 2.5 %collective-permute-start.4 = (f32[8,128]{1,0:T(8,128)S(1)}, f32[8,128]{1,0:T(8,128)S(1)}, u32[]{:S(2)}, u32[]{:S(2)}) collective-permute-start(f32[8,128]{1,0:T(8,128)S(1)} %get-tuple-element.109.c0), channel_id=1, source_target_pairs={{64,0},{96,32},{0,64},{32,96},{65,1},{97,33},{1,65},{33,97},{66,2}... | collective-permute-start | bytes 12296 | tf_op jit(solution)/shard_map/ppermute | solution.py:595
  234.8 2.3 all-to-all-done.13
  237.1 5.0 %shard_map.115 = f32[1,16,1024]{2,1,0:T(8,128)} custom-call(s32[1]{0:T(128)S(6)} %copy.11.live_ref, f32[256,128]{1,0:T(8,128)S(1)} %bitcast.43, bf16[256,1024]{1,0:T(8,128)(2,1)S(1)} %copy-done, s32[8,1024]{1,0:T(8,128)S(1)} %copy-done.3, f32[16,1024]{1,0:T(8,128)S(1)} %copy-done.2, f32[1,1024,1024]{2,1,0:T(8,128)} %inv_ref.3, f32[1,1024,1024]{2,1,0:T(8,128)} %upd_ref.3), custom_call_target="tpu_custom_call" | custom-call | flops 201326592 | bytes 8388608 | tf_op jit(solution)/shard_map/pallas_call | solution.py:196
  (35 shorter events, 17.1 us)
Async XLA Ops:
  1.3 17.8 %copy-start.4 = (f32[16,6,4,1,32]{4,3,2,1,0:T(1,128)S(1)}, f32[16,6,4,1,32]{4,3,2,1,0:T(1,128)}, u32[]{:S(2)}) copy-start(f32[16,6,4,1,32]{4,3,2,1,0:T(1,128)} %param.13) | copy-start | bytes 147460
  7.1 22.4 %all-to-all-start = ((f32[128,4,128]{2,1,0:T(4,128)}), f32[128,4,128]{2,1,0:T(4,128)S(1)}, u32[]{:S(2)}, u32[]{:S(2)}) async-start(f32[128,4,128]{2,1,0:T(4,128)} %bitcast.54), calls=%async_computation | async-start | bytes 524288 | tf_op jit(solution)/shard_map/all_to_all | solution.py:591
  20.5 0.8 copy-start.1
  57.9 15.5 %all-to-all-start.3 = ((f32[128,4,128]{2,1,0:T(4,128)}), f32[128,4,128]{2,1,0:T(4,128)S(1)}, u32[]{:S(2)}, u32[]{:S(2)}) async-start(f32[128,4,128]{2,1,0:T(4,128)} %bitcast.7), calls=%async_computation.3 | async-start | bytes 524288 | tf_op jit(solution)/shard_map/all_to_all | solution.py:591
  90.3 15.5 %all-to-all-start.5 = ((f32[128,4,128]{2,1,0:T(4,128)}), f32[128,4,128]{2,1,0:T(4,128)S(1)}, u32[]{:S(2)}, u32[]{:S(2)}) async-start(f32[128,4,128]{2,1,0:T(4,128)} %bitcast.11), calls=%async_computation.5 | async-start | bytes 524288 | tf_op jit(solution)/shard_map/all_to_all | solution.py:591
  121.8 4.2 %collective-permute-start.2 = (f32[96,128]{1,0:T(8,128)S(1)}, f32[96,128]{1,0:T(8,128)S(1)}, u32[]{:S(2)}, u32[]{:S(2)}) collective-permute-start(f32[96,128]{1,0:T(8,128)S(1)} %shard_map.105.own_ref), channel_id=1, source_target_pairs={{96,0},{0,32},{32,64},{64,96},{97,1},{1,33},{33,65},{65,97},{98,2}... | collective-permute-start | bytes 147464 | tf_op jit(solution)/shard_map/ppermute | solution.py:595
  122.1 4.7 %collective-permute-start.1 = (f32[96,128]{1,0:T(8,128)S(1)}, f32[96,128]{1,0:T(8,128)S(1)}, u32[]{:S(2)}, u32[]{:S(2)}) collective-permute-start(f32[96,128]{1,0:T(8,128)S(1)} %shard_map.105.own_ref), channel_id=1, source_target_pairs={{64,0},{96,32},{0,64},{32,96},{65,1},{97,33},{1,65},{33,97},{66,2}... | collective-permute-start | bytes 147464 | tf_op jit(solution)/shard_map/ppermute | solution.py:595
  123.7 3.6 %collective-permute-start = (f32[96,128]{1,0:T(8,128)S(1)}, f32[96,128]{1,0:T(8,128)S(1)}, u32[]{:S(2)}, u32[]{:S(2)}) collective-permute-start(f32[96,128]{1,0:T(8,128)S(1)} %shard_map.105.own_ref), channel_id=1, source_target_pairs={{32,0},{64,32},{96,64},{0,96},{33,1},{65,33},{97,65},{1,97},{34,2}... | collective-permute-start | bytes 147464 | tf_op jit(solution)/shard_map/ppermute | solution.py:595
  146.5 15.5 %all-to-all-start.8 = ((f32[128,4,128]{2,1,0:T(4,128)}), f32[128,4,128]{2,1,0:T(4,128)S(1)}, u32[]{:S(2)}, u32[]{:S(2)}) async-start(f32[128,4,128]{2,1,0:T(4,128)} %bitcast.17), calls=%async_computation.8 | async-start | bytes 524288 | tf_op jit(solution)/shard_map/all_to_all | solution.py:591
  178.7 15.5 %all-to-all-start.10 = ((f32[128,4,128]{2,1,0:T(4,128)}), f32[128,4,128]{2,1,0:T(4,128)S(1)}, u32[]{:S(2)}, u32[]{:S(2)}) async-start(f32[128,4,128]{2,1,0:T(4,128)} %bitcast.21), calls=%async_computation.10 | async-start | bytes 524288 | tf_op jit(solution)/shard_map/all_to_all | solution.py:591
  183.2 53.9 %copy-start = (bf16[256,1024]{1,0:T(8,128)(2,1)S(1)}, bf16[256,1024]{1,0:T(8,128)(2,1)}, u32[]{:S(2)}) copy-start(bf16[256,1024]{1,0:T(8,128)(2,1)} %get-tuple-element.107.t_ref) | copy-start | bytes 1572868
  183.2 53.9 %copy-start.2 = (f32[16,1024]{1,0:T(8,128)S(1)}, f32[16,1024]{1,0:T(8,128)}, u32[]{:S(2)}) copy-start(f32[16,1024]{1,0:T(8,128)} %get-tuple-element.57.after_ref.y_ref) | copy-start | bytes 196612
  183.3 53.9 %copy-start.3 = (s32[8,1024]{1,0:T(8,128)S(1)}, s32[8,1024]{1,0:T(8,128)}, u32[]{:S(2)}) copy-start(s32[8,1024]{1,0:T(8,128)} %get-tuple-element.108.rank_ref) | copy-start | bytes 98308
  223.4 13.7 %all-to-all-start.13 = ((f32[128,2,128]{2,1,0:T(2,128)}), f32[128,2,128]{2,1,0:T(2,128)S(1)}, u32[]{:S(2)}, u32[]{:S(2)}) async-start(f32[128,2,128]{2,1,0:T(2,128)} %bitcast.27), calls=%async_computation.13 | async-start | bytes 262144 | tf_op jit(solution)/shard_map/all_to_all | solution.py:591
  227.2 5.2 %collective-permute-start.5 = (f32[8,128]{1,0:T(8,128)S(1)}, f32[8,128]{1,0:T(8,128)S(1)}, u32[]{:S(2)}, u32[]{:S(2)}) collective-permute-start(f32[8,128]{1,0:T(8,128)S(1)} %get-tuple-element.109.c0), channel_id=1, source_target_pairs={{96,0},{0,32},{32,64},{64,96},{97,1},{1,33},{33,65},{65,97},{98,2}... | collective-permute-start | bytes 12296 | tf_op jit(solution)/shard_map/ppermute | solution.py:595
  228.7 4.3 %collective-permute-start.4 = (f32[8,128]{1,0:T(8,128)S(1)}, f32[8,128]{1,0:T(8,128)S(1)}, u32[]{:S(2)}, u32[]{:S(2)}) collective-permute-start(f32[8,128]{1,0:T(8,128)S(1)} %get-tuple-element.109.c0), channel_id=1, source_target_pairs={{64,0},{96,32},{0,64},{32,96},{65,1},{97,33},{1,65},{33,97},{66,2}... | collective-permute-start | bytes 12296 | tf_op jit(solution)/shard_map/ppermute | solution.py:595
  231.2 2.8 %collective-permute-start.3 = (f32[8,128]{1,0:T(8,128)S(1)}, f32[8,128]{1,0:T(8,128)S(1)}, u32[]{:S(2)}, u32[]{:S(2)}) collective-permute-start(f32[8,128]{1,0:T(8,128)S(1)} %get-tuple-element.109.c0), channel_id=1, source_target_pairs={{32,0},{64,32},{96,64},{0,96},{33,1},{65,33},{97,65},{1,97},{34,2}... | collective-permute-start | bytes 12296 | tf_op jit(solution)/shard_map/ppermute | solution.py:595
